TPU v7x, 128 devices: a whole 4x4x4 slice. The times are simulated.
128 devices in a mesh: dp: 16 (over y_lo, z, core), seq: 8 (over x, y_hi).
Axes of the slice: x: 4, y: 4 (y_hi: 2, y_lo: 2; y = y_hi * 2 + y_lo), z: 4, core: 2. Of those that a mesh axis runs over, the one named last changes fastest.
Arguments:
- inputs: bfloat16 [16, 8, 8, 16, 1536], P('dp', 'seq'), may hold values from -6 to 6
- spatial_q: bfloat16 [16, 8, 8, 16, 1536], P('dp', 'seq'), may hold values from -68 to 68
- spatial_k: bfloat16 [16, 8, 8, 16, 1536], P('dp', 'seq'), may hold values from -4 to 4
- spatial_v: bfloat16 [16, 8, 8, 16, 1536], P('dp', 'seq'), may hold values from -6 to 6
- out_weight: bfloat16 [1536, 1536], P('dp'), may hold values from -0.15625 to 0.15625
- norm_gain: float32 [1536], replicated, may hold values from 0.1 to 1.9
- qkv_weight: bfloat16 [1536, 4608], P('dp', 'seq')
- grad_out: bfloat16 [16, 8, 8, 16, 1536], P('dp', 'seq'), may hold values from -6 to 6
- grad_resid: bfloat16 [16, 8, 8, 16, 1536], P('dp', 'seq'), may hold values from -6 to 6
Outputs:
- hidden: bfloat16 [16, 8, 8, 16, 1536], P('dp', 'seq')
- temporal_out: bfloat16 [16, 8, 8, 16, 1536], P('dp', 'seq')
- grad_input: bfloat16 [16, 8, 8, 16, 1536], P('dp', 'seq')
- grad_spatial_q: bfloat16 [16, 8, 8, 16, 1536], P('dp', 'seq')
- grad_spatial_k: bfloat16 [16, 8, 8, 16, 1536], P('dp', 'seq')
- grad_spatial_v: bfloat16 [16, 8, 8, 16, 1536], P('dp', 'seq')
- qkv_grad: float32 [1536, 4608], P('dp', 'seq')
- out_grad: float32 [1536, 1536], P('dp')
- gain_grad: float32 [1536], replicated
All inputs are finite; a program needn't handle non-finite values.
Results may differ from a plain program's by a relative error of at most 0.03.
Values may be sent and summed in bfloat16 or wider, within the bound.
No kernel may reach another device: no remote copies, remote signals or barrier semaphores. Data moves between devices by JAX's collectives and lax.ppermute only.
A program may use at most 128 MiB of HBM per device.

v0:
```python
import jax
import jax.numpy as jnp
from jax import lax
from jax.sharding import PartitionSpec as P

HEADS = 24
HDIM = 64


EPSILON = 1e-06


def contract_rows(left_side, right_side):
    return lax.dot_general(
        left_side, right_side, (((0,), (0,)), ((), ())), preferred_element_type=jnp.float32
    )


def contract_last(left_side, right_side):
    return lax.dot_general(
        left_side, right_side, (((1,), (1,)), ((), ())), preferred_element_type=jnp.float32
    )


def spatial_forward(queries, key_rows, values):
    frame_len = queries.shape[0]
    shaped = (frame_len, HEADS, HDIM)
    scores = jnp.einsum(
        "shd,thd->hst",
        queries.reshape(shaped),
        key_rows.reshape(shaped),
        preferred_element_type=jnp.float32,
    ) * HDIM ** (-0.5)
    row_max = jnp.max(scores, axis=-1, keepdims=True)
    raised = jnp.exp(scores - row_max)
    soft_weights = raised / jnp.sum(raised, axis=-1, keepdims=True)
    mixed_heads = jnp.einsum(
        "hst,thd->shd",
        soft_weights.astype(jnp.bfloat16),
        values.reshape(shaped),
        preferred_element_type=jnp.float32,
    )
    return (mixed_heads.astype(jnp.bfloat16).reshape(frame_len, HEADS * HDIM), soft_weights)


def spatial_backward(queries, key_rows, values, grad_heads):
    frame_len = queries.shape[0]
    shaped = (frame_len, HEADS, HDIM)
    _, soft_weights = spatial_forward(queries, key_rows, values)
    queries, key_rows, values, grad_heads = (
        queries.reshape(shaped),
        key_rows.reshape(shaped),
        values.reshape(shaped),
        grad_heads.reshape(shaped),
    )
    soft_grad = jnp.einsum("shd,thd->hst", grad_heads, values, preferred_element_type=jnp.float32)
    dvalues = jnp.einsum(
        "hst,shd->thd",
        soft_weights.astype(jnp.bfloat16),
        grad_heads,
        preferred_element_type=jnp.float32,
    ).astype(jnp.bfloat16)
    inner_sum = jnp.sum(soft_weights * soft_grad, axis=-1, keepdims=True)
    dscores = (soft_weights * (soft_grad - inner_sum) * HDIM ** (-0.5)).astype(jnp.bfloat16)
    dqueries = jnp.einsum(
        "hst,thd->shd", dscores, key_rows, preferred_element_type=jnp.float32
    ).astype(jnp.bfloat16)
    key_grad = jnp.einsum(
        "hst,shd->thd", dscores, queries, preferred_element_type=jnp.float32
    ).astype(jnp.bfloat16)
    flat_shape = (frame_len, HEADS * HDIM)
    return (dqueries.reshape(flat_shape), key_grad.reshape(flat_shape), dvalues.reshape(flat_shape))


def split_heads(block_in):
    frames_all, rows_here, cols_here, proj_width = block_in.shape
    head_count = proj_width // (3 * HDIM)
    split_parts = block_in.reshape(frames_all, rows_here, cols_here, head_count, 3, HDIM)
    return (split_parts[:, :, :, :, 0], split_parts[:, :, :, :, 1], split_parts[:, :, :, :, 2])


def temporal_forward(block_in):
    queries, key_rows, values = split_heads(block_in)
    scores = jnp.einsum(
        "fachd,gachd->fachg", queries, key_rows, preferred_element_type=jnp.float32
    ) * HDIM ** (-0.5)
    row_max = jnp.max(scores, axis=-1, keepdims=True)
    raised = jnp.exp(scores - row_max)
    soft_rows = raised / jnp.sum(raised, axis=-1, keepdims=True)
    mixed_heads = jnp.einsum(
        "fachg,gachd->fachd",
        soft_rows.astype(jnp.bfloat16),
        values,
        preferred_element_type=jnp.float32,
    )
    out_shape = block_in.shape[:3] + (queries.shape[3] * HDIM,)
    return (mixed_heads.astype(jnp.bfloat16).reshape(out_shape), soft_rows)


def temporal_backward(block_in, soft_rows, grad_heads):
    queries, key_rows, values = split_heads(block_in)
    grad_heads = grad_heads.reshape(queries.shape)
    soft_grad = jnp.einsum(
        "fachd,gachd->fachg", grad_heads, values, preferred_element_type=jnp.float32
    )
    dvalues = jnp.einsum(
        "fachg,fachd->gachd",
        soft_rows.astype(jnp.bfloat16),
        grad_heads,
        preferred_element_type=jnp.float32,
    ).astype(jnp.bfloat16)
    inner_sum = jnp.sum(soft_rows * soft_grad, axis=-1, keepdims=True)
    dscores = (soft_rows * (soft_grad - inner_sum) * HDIM ** (-0.5)).astype(jnp.bfloat16)
    dqueries = jnp.einsum(
        "fachg,gachd->fachd", dscores, key_rows, preferred_element_type=jnp.float32
    ).astype(jnp.bfloat16)
    key_grad = jnp.einsum(
        "fachg,fachd->gachd", dscores, queries, preferred_element_type=jnp.float32
    ).astype(jnp.bfloat16)
    stacked = jnp.stack([dqueries, key_grad, dvalues], axis=4)
    return stacked.reshape(block_in.shape)


def body(
    inputs, spatial_q, spatial_k, spatial_v, out_weight, norm_gain, qkv_weight, grad_out, grad_resid
):
    frames_here, row_count, col_count, model_width = inputs.shape[1:]
    head_width = HEADS * HDIM
    frame_len = row_count * col_count
    token_count = frames_here * frame_len
    all_tokens = token_count * lax.axis_size("dp") * lax.axis_size("seq")
    grad_scale = all_tokens ** (-0.5)
    grid_shape = (frames_here, row_count, col_count)
    whole_out, head_proj = (
        lax.all_gather(out_weight, "dp", axis=0, tiled=True),
        lax.all_gather(qkv_weight, "dp", axis=0, tiled=True),
    )
    proj_width = head_proj.shape[1]

    def by_frame(array):
        return array.reshape(frames_here, frame_len, head_width)

    def spatial_step(triple):
        mixed_heads, _ = spatial_forward(triple[0], triple[1], triple[2])
        return mixed_heads

    frame_q, frame_k, frame_v = (by_frame(spatial_q), by_frame(spatial_k), by_frame(spatial_v))
    mixed = lax.map(spatial_step, (frame_q, frame_k, frame_v)).reshape(token_count, head_width)
    flat_in = inputs.reshape(token_count, model_width).astype(jnp.float32)
    hidden = (flat_in + contract_last(mixed, whole_out)).astype(jnp.bfloat16)
    hidden_wide = hidden.astype(jnp.float32)
    inverse = lax.rsqrt(jnp.mean(hidden_wide * hidden_wide, axis=-1, keepdims=True) + EPSILON)
    unit_rows = hidden_wide * inverse
    normed = (unit_rows * norm_gain).astype(jnp.bfloat16)
    normed_all = lax.all_gather(normed, "seq", axis=0, tiled=True)
    clip_tokens = normed_all.shape[0]
    frames_all = clip_tokens // frame_len
    projected_all = jnp.dot(normed_all, head_proj, preferred_element_type=jnp.float32).astype(
        jnp.bfloat16
    )
    projected_all = projected_all.reshape(frames_all, row_count, col_count, proj_width)
    heads_out, soft_rows = temporal_forward(projected_all)
    temporal_out = lax.all_to_all(heads_out, "seq", split_axis=0, concat_axis=3, tiled=True)
    grad_heads = lax.all_to_all(
        grad_out.reshape(grid_shape + (head_width,)), "seq", split_axis=3, concat_axis=0, tiled=True
    )
    dproj_all = temporal_backward(projected_all, soft_rows, grad_heads).reshape(
        clip_tokens, proj_width
    )
    dnormed = lax.psum_scatter(
        contract_last(dproj_all, head_proj).astype(jnp.bfloat16),
        "seq",
        scatter_dimension=0,
        tiled=True,
    )
    dnormed_wide = dnormed.astype(jnp.float32)
    local_gain = jnp.sum(dnormed_wide * unit_rows, axis=0) * grad_scale
    scaled = dnormed_wide * norm_gain
    through_norm = inverse * (
        scaled - unit_rows * jnp.mean(scaled * unit_rows, axis=-1, keepdims=True)
    )
    grad_input = (
        grad_resid.reshape(token_count, model_width).astype(jnp.float32) + through_norm
    ).astype(jnp.bfloat16)
    grad_share = lax.psum_scatter(
        jnp.concatenate(
            [
                contract_rows(normed_all, dproj_all) * grad_scale,
                contract_rows(grad_input, mixed) * grad_scale,
            ],
            axis=1,
        ).astype(jnp.bfloat16),
        "dp",
        scatter_dimension=0,
        tiled=True,
    ).astype(jnp.float32)
    qkv_grad = grad_share[:, :proj_width]
    out_grad = lax.psum(grad_share[:, proj_width:].astype(jnp.bfloat16), "seq").astype(jnp.float32)
    gain_grad = lax.psum(local_gain, ("dp", "seq"))
    dmixed = jnp.dot(grad_input, whole_out, preferred_element_type=jnp.float32).astype(jnp.bfloat16)

    def spatial_back(frame_group):
        return spatial_backward(frame_group[0], frame_group[1], frame_group[2], frame_group[3])

    grad_sq, grad_sk, grad_sv = lax.map(spatial_back, (frame_q, frame_k, frame_v, by_frame(dmixed)))
    head_shape = (1,) + grid_shape + (head_width,)
    model_shape = (1,) + grid_shape + (model_width,)
    return (
        hidden.reshape(model_shape),
        temporal_out.reshape(head_shape),
        grad_input.reshape(model_shape),
        grad_sq.reshape(head_shape),
        grad_sk.reshape(head_shape),
        grad_sv.reshape(head_shape),
        qkv_grad,
        out_grad,
        gain_grad,
    )


def solution(mesh):
    placed = (
        P("dp", "seq", None, None, None),
        P("dp", "seq", None, None, None),
        P("dp", "seq", None, None, None),
        P("dp", "seq", None, None, None),
        P("dp", None),
        P(),
        P("dp", "seq"),
        P("dp", "seq", None, None, None),
        P("dp", "seq", None, None, None),
    )
    return jax.shard_map(
        body,
        mesh=mesh,
        in_specs=placed,
        out_specs=(
            P("dp", "seq", None, None, None),
            P("dp", "seq", None, None, None),
            P("dp", "seq", None, None, None),
            P("dp", "seq", None, None, None),
            P("dp", "seq", None, None, None),
            P("dp", "seq", None, None, None),
            P("dp", "seq"),
            P("dp", None),
            P(),
        ),
        check_vma=False,
    )
```

profile of v0, /device:TPU:0, one launch (start us, length us, event | category | flops | bytes accessed | tf_op | source)
XLA Modules:
  0.0 475.7 jit_solution(14756888716965673746)
XLA Ops:
  16.5 34.4 %all-gather.4.cloned.1.call-done = bf16[1536,1536]{1,0:T(8,128)(2,1)} async-done(((bf16[96,1536]{1,0:T(8,128)(2,1)}), bf16[1536,1536]{1,0:T(8,128)(2,1)}) %all-gather.4.cloned.1.call-update) | async-done | bytes 4718608 | tf_op jit(solution)/shard_map/all_gather | solution.py:135
  50.9 4.1 fusion.51
  56.1 3.4 copy.106
  61.5 3.9 reshape.146
  65.4 17.3 %all_to_all.30 = bf16[8,2,12288]{2,1,0:T(2,128)(2,1)} all-to-all(bf16[8,2,12288]{2,1,0:T(2,128)(2,1)} %reshape.146), channel_id=1, replica_groups=mesh['dp'=16,'seq'=8] {'seq'}, dimensions={0} | all-to-all | bytes 786432 | tf_op jit(solution)/shard_map/all_to_all | solution.py:164
  82.7 3.7 reshape.147
  86.4 3.0 copy.107
  89.3 3.2 reshape.136
  92.5 64.3 %all-gather.6.cloned.1.call-done = bf16[1024,1536]{1,0:T(8,128)(2,1)} async-done(((bf16[128,1536]{1,0:T(8,128)(2,1)}), bf16[1024,1536]{1,0:T(8,128)(2,1)}) %all-gather.6.cloned.1.call-update) | async-done | bytes 3145744 | tf_op jit(solution)/shard_map/all_gather | solution.py:155
  156.9 4.5 convolution_convert_fusion.2
  162.8 5.5 %reshape_reshape.7 = bf16[8,8,16,3,3,64]{5,4,3,2,1,0:T(4,128)(2,1)S(1)} reshape(bf16[1024,576]{1,0:T(8,128)(2,1)} %copy.99) | data formatting | bytes 2359296 | tf_op jit(solution)/shard_map/reshape;reshape | solution.py:78
  168.4 6.3 %fusion.74 = (bf16[8,8,16,3,1,64]{5,4,3,2,1,0:T(2,128)(2,1)}, bf16[8,8,16,3,1,64]{5,4,3,2,1,0:T(2,128)(2,1)}, bf16[8,8,16,3,1,64]{5,4,3,2,1,0:T(2,128)(2,1)}) fusion(bf16[8,8,16,3,3,64]{5,4,3,2,1,0:T(4,128)(2,1)S(1)} %reshape_reshape.7), kind=kLoop, calls=%fused_computation.91 | loop fusion | bytes 2359296 | tf_op jit(solution)/shard_map/slice | solution.py:79
  174.7 5.7 %fusion.76 = (f32[8,8,16,3]{0,3,2,1:T(4,128)S(1)}, f32[8,8,16,3,8]{0,4,3,2,1:T(8,128)}) fusion(bf16[8,8,16,3,1,64]{5,4,3,2,1,0:T(2,128)(2,1)} %get-tuple-element.86, bf16[8,8,16,3,1,64]{5,4,3,2,1,0:T(2,128)(2,1)} %get-tuple-element.87), kind=kOutput, calls=%fused_computation.93 | convolution fusion | flops 3219463 | bytes 897024 | tf_op jit(solution)/shard_map/sub | solution.py:88
  180.4 2.8 fusion.57
  183.2 6.1 %fusion.26 = bf16[8,8,16,3,1,64]{5,0,3,2,1,4:T(8,128)(2,1)} fusion(bf16[8,8,16,3,1,64]{5,4,3,2,1,0:T(2,128)(2,1)} %get-tuple-element.87, f32[8,16,3,8,8]{4,3,2,1,0:T(8,128)} %fusion.57, f32[8,8,16,3,8]{0,4,3,2,1:T(8,128)} %get-tuple-element.94, f32[8,8,16,3]{0,3,2,1:T(4,128)S(1)} %get-tuple-element.93), kind=kOutput, calls=%fused_computation.37 | convolution fusion | flops 3517447 | bytes 995328 | tf_op jit(solution)/shard_map/fachg,gachd->fachd/dot_general | solution.py:114
  189.3 5.4 %fusion.27 = bf16[8,8,16,3,1,64]{5,0,3,2,1,4:T(8,128)(2,1)} fusion(bf16[8,8,16,3,1,64]{5,4,3,2,1,0:T(2,128)(2,1)S(1)} %copy-done.8, f32[8,16,3,8,8]{4,3,2,1,0:T(8,128)} %fusion.57, f32[8,8,16,3,8]{0,4,3,2,1:T(8,128)} %get-tuple-element.94, f32[8,8,16,3]{0,3,2,1:T(4,128)S(1)} %get-tuple-element.93), kind=kOutput, calls=%fused_computation.38 | convolution fusion | flops 3517447 | bytes 995328 | tf_op jit(solution)/shard_map/fachg,fachd->gachd/dot_general | solution.py:117
  194.7 2.4 fusion.28
  199.7 3.2 reshape_reshape.8
  202.9 6.3 %convolution_convert_fusion = bf16[1024,1536]{1,0:T(8,128)(2,1)} fusion(bf16[1024,576]{1,0:T(8,128)(2,1)} %reshape_reshape.8, bf16[1536,576]{1,0:T(8,128)(2,1)} %all-gather.8.cloned.1.call-done), kind=kOutput, calls=%fused_computation.7 | convolution fusion | flops 1813512192 | bytes 6094848 | tf_op jit(solution)/shard_map/dot_general | solution.py:20
  210.5 5.2 %multiply_convert_fusion = bf16[1536,576]{0,1:T(8,128)(2,1)} fusion(bf16[1024,1536]{1,0:T(8,128)(2,1)} %all-gather.6.cloned.1.call-done, bf16[1024,576]{1,0:T(8,128)(2,1)S(1)} %copy-done.11), kind=kOutput, calls=%fused_computation.8 | convolution fusion | flops 1813708800 | bytes 6094848 | tf_op jit(solution)/shard_map/dot_general | solution.py:14
  215.7 72.0 %reduce-scatter.5.cloned.1.call-done = bf16[128,1536]{1,0:T(8,128)(2,1)} async-done(((bf16[1024,1536]{1,0:T(8,128)(2,1)}), bf16[128,1536]{1,0:T(8,128)(2,1)}) %reduce-scatter.5.cloned.1.call-update) | async-done | bytes 393232 | tf_op jit(solution)/shard_map/reduce_scatter | solution.py:170
  292.0 3.1 pad_maximum_fusion
  295.2 9.3 %copy.130 = bf16[1536,2112]{1,0:T(8,128)(2,1)} copy(bf16[1536,2112]{0,1:T(8,128)(2,1)} %pad_maximum_fusion) | data formatting | bytes 12976128
  306.3 2.1 fusion.25
  309.7 13.8 %all_to_all.31 = bf16[8,8,16,192]{3,2,1,0:T(8,128)(2,1)S(1)} all-to-all(bf16[8,8,16,192]{3,2,1,0:T(8,128)(2,1)S(1)} %reshape.133), channel_id=1, replica_groups=mesh['dp'=16,'seq'=8] {'seq'}, dimensions={0} | all-to-all | bytes 786432 | tf_op jit(solution)/shard_map/all_to_all | solution.py:163
  324.9 3.3 convolution_convert_fusion.1
  329.2 2.6 fusion.38
  331.8 2.1 fusion.41
  333.9 45.9 %reduce-scatter.7.cloned.1.call-done = bf16[96,2112]{1,0:T(8,128)(2,1)} async-done(((bf16[1536,2112]{1,0:T(8,128)(2,1)}), bf16[96,2112]{1,0:T(8,128)(2,1)}) %reduce-scatter.7.cloned.1.call-update) | async-done | bytes 405520
  381.9 2.6 fusion.35
  389.5 66.0 %psum.15 = f32[1536]{0:T(1024)} all-reduce(f32[1536]{0:T(1024)S(1)} %broadcast_multiply_fusion), channel_id=1, replica_groups=mesh['dp'=16,'seq'=8] {'dp','seq'}, use_global_device_ids=true, to_apply=%region_12.13 | all-reduce | flops 1536 | bytes 12288 | tf_op jit(solution)/shard_map/psum | solution.py:199
  456.5 10.1 %all-reduce.2.cloned.1.call-done = bf16[96,1536]{0,1:T(8,128)(2,1)} async-done(((bf16[96,1536]{0,1:T(8,128)(2,1)}), bf16[96,1536]{0,1:T(8,128)(2,1)}) %all-reduce.2.cloned.1.call-update) | async-done | bytes 294928 | tf_op jit(solution)/shard_map/psum | solution.py:198
  (113 shorter events, 37.3 us)
Async XLA Ops:
  7.2 3.6 copy-start.16
  7.2 43.7 %all-gather.4.cloned.1.call-start = ((), (), s32[]{:S(2)}) async-start(), calls=%async_computation.4 | async-start | bytes 5013504 | tf_op jit(solution)/shard_map/all_gather | solution.py:135
  7.9 84.6 %all-gather.8.cloned.1.call-start = ((), (), s32[]{:S(2)}) async-start(), calls=%async_computation.6 | async-start | bytes 2088960 | tf_op jit(solution)/shard_map/all_gather | solution.py:136
  8.7 148.2 %all-gather.6.cloned.1.call-start = ((), (), s32[]{:S(2)}) async-start(), calls=%async_computation.5 | async-start | bytes 3538944 | tf_op jit(solution)/shard_map/all_gather | solution.py:155
  10.8 1.9 copy-start.19
  11.8 2.8 copy-start.21
  12.8 3.7 copy-start.9
  14.6 1.8 copy-start.26
  14.6 36.3 %copy-start.14 = (bf16[1,1,8,16,1536]{4,3,2,1,0:T(8,128)(2,1)S(1)}, bf16[1,1,8,16,1536]{4,3,2,1,0:T(8,128)(2,1)}, u32[]{:S(2)}) copy-start(bf16[1,1,8,16,1536]{4,3,2,1,0:T(8,128)(2,1)} %param.9) | copy-start | bytes 1179652
  16.5 38.6 %copy-start.5 = (bf16[24,128,64]{1,2,0:T(8,128)(2,1)}, bf16[24,128,64]{1,2,0:T(8,128)(2,1)S(1)}, u32[]{:S(2)}) copy-start(bf16[24,128,64]{1,2,0:T(8,128)(2,1)S(1)} %convolution_convert_fusion.7) | copy-start | bytes 1179652
  50.9 4.2 copy-start.23
  50.9 5.2 %copy-start.15 = (bf16[1,1,8,16,1536]{4,3,2,1,0:T(8,128)(2,1)S(1)}, bf16[1,1,8,16,1536]{4,3,2,1,0:T(8,128)(2,1)}, u32[]{:S(2)}) copy-start(bf16[1,1,8,16,1536]{4,3,2,1,0:T(8,128)(2,1)} %param.16) | copy-start | bytes 1179652
  55.0 234.0 %copy-start = (bf16[128,1536]{1,0:T(8,128)(2,1)}, bf16[128,1536]{1,0:T(8,128)(2,1)S(1)}, u32[]{:S(2)}) copy-start(bf16[128,1536]{1,0:T(8,128)(2,1)S(1)} %get-tuple-element.92) | copy-start | bytes 1179652
  56.0 231.7 %reduce-scatter.5.cloned.1.call-start = ((), (), s32[]{:S(2)}) async-start(), calls=%async_computation.7 | async-start | bytes 3538944 | tf_op jit(solution)/shard_map/reduce_scatter | solution.py:170
  174.7 5.7 %copy-start.1 = (bf16[8,8,16,3,1,64]{5,4,3,2,1,0:T(2,128)(2,1)S(1)}, bf16[8,8,16,3,1,64]{5,4,3,2,1,0:T(2,128)(2,1)}, u32[]{:S(2)}) copy-start(bf16[8,8,16,3,1,64]{5,4,3,2,1,0:T(2,128)(2,1)} %get-tuple-element.88) | copy-start | bytes 1179652
  174.7 5.7 %copy-start.4 = (bf16[8,8,16,3,64]{4,3,2,1,0:T(4,128)(2,1)S(1)}, bf16[8,8,16,3,64]{4,3,2,1,0:T(4,128)(2,1)}, u32[]{:S(2)}) copy-start(bf16[8,8,16,3,64]{4,3,2,1,0:T(4,128)(2,1)} %reshape.136) | copy-start | bytes 1179652
  180.4 14.3 %copy-start.30 = (f32[8,8,16,3]{0,3,2,1:T(4,128)}, f32[8,8,16,3]{0,3,2,1:T(4,128)S(1)}, u32[]{:S(2)}) copy-start(f32[8,8,16,3]{0,3,2,1:T(4,128)S(1)} %get-tuple-element.93) | copy-start | bytes 36868
  183.2 6.1 %copy-start.8 = (bf16[8,8,16,3,1,64]{5,4,3,2,1,0:T(2,128)(2,1)S(1)}, bf16[8,8,16,3,1,64]{5,4,3,2,1,0:T(2,128)(2,1)}, u32[]{:S(2)}) copy-start(bf16[8,8,16,3,1,64]{5,4,3,2,1,0:T(2,128)(2,1)} %get-tuple-element.86) | copy-start | bytes 1179652
  194.7 2.4 copy-start.12
  194.7 2.4 copy-start.13
  209.2 78.5 %copy-start.25 = (f32[128]{0:T(128)S(1)}, f32[128]{0:T(128)}, u32[]{:S(2)}) copy-start(f32[128]{0:T(128)} %copy-done.24) | copy-start | bytes 1540
  209.2 79.8 %copy-start.18 = (bf16[1,1,8,16,1536]{4,3,2,1,0:T(8,128)(2,1)S(1)}, bf16[1,1,8,16,1536]{4,3,2,1,0:T(8,128)(2,1)}, u32[]{:S(2)}) copy-start(bf16[1,1,8,16,1536]{4,3,2,1,0:T(8,128)(2,1)} %param.17) | copy-start | bytes 1179652
  209.2 170.6 %reduce-scatter.7.cloned.1.call-start = ((), (), s32[]{:S(2)}) async-start(), calls=%async_computation.9 | async-start | bytes 7102464
  215.7 74.7 %copy-start.6 = (bf16[24,128,64]{1,2,0:T(8,128)(2,1)S(1)}, bf16[24,128,64]{1,2,0:T(8,128)(2,1)}, u32[]{:S(2)}) copy-start(bf16[24,128,64]{1,2,0:T(8,128)(2,1)} %copy-done.5) | copy-start | bytes 1179652
  290.4 34.5 %copy-start.3 = (bf16[128,1536]{1,0:T(8,128)(2,1)}, bf16[128,1536]{1,0:T(8,128)(2,1)S(1)}, u32[]{:S(2)}) copy-start(bf16[128,1536]{1,0:T(8,128)(2,1)S(1)} %fusion.48) | copy-start | bytes 1179652
  290.4 1.6 copy-start.7
  304.4 1.9 copy-start.29
  304.5 162.2 %all-reduce.2.cloned.1.call-start = ((), (), s32[]{:S(2)}) async-start(), calls=%async_computation.8 | async-start | bytes 786432 | tf_op jit(solution)/shard_map/psum | solution.py:198
  324.9 3.5 copy-start.10
  333.9 48.0 %copy-start.20 = (bf16[128,24,64]{0,2,1:T(8,128)(2,1)S(1)}, bf16[128,24,64]{0,2,1:T(8,128)(2,1)}, u32[]{:S(2)}) copy-start(bf16[128,24,64]{0,2,1:T(8,128)(2,1)} %copy-done.19) | copy-start | bytes 1179652
  333.9 48.0 %copy-start.28 = (f32[24,128]{1,0:T(8,128)S(1)}, f32[24,128]{1,0:T(8,128)}, u32[]{:S(2)}) copy-start(f32[24,128]{1,0:T(8,128)} %copy-done.26) | copy-start | bytes 36868
  387.8 67.7 %slice-start = ((bf16[96,2112]{1,0:T(8,128)(2,1)}), bf16[96,576]{1,0:T(8,128)(2,1)S(1)}, s32[]{:S(2)}) async-start(bf16[96,2112]{1,0:T(8,128)(2,1)} %reduce-scatter.7.cloned.1.call-done), calls=%async_computation.10 | async-start | bytes 245760 | tf_op jit(solution)/shard_map/slice | solution.py:197
  (6 other events, 7.2 us)
Sparse Core Ops, SparseCore 0:
  9.7 41.1 all-gather.3
  52.6 36.9 all-gather.7
  92.5 64.3 all-gather.5
  209.3 78.2 reduce-scatter.4
  304.6 75.1 reduce-scatter.6
  382.9 83.6 all-reduce.1
where the time goes:
time: 482 us; the launch traced here: 476 us
  waiting for transfers between devices  228 us (47%)
  blocking collectives  97.1 us (20%)
  local copies, waits for them, and re-layouts  67.5 us (14%)
  matrix products  60.4 us (13%)
  between operations  14.9 us (3%)
  other arithmetic  7.35 us (2%)
    reduce_scatter x1, waiting for transfers between devices, body(): lax.psum_scatter(contract_last(dproj_all, head_proj).astype(jnp.bfloat16)...  72 us
    psum x1, blocking collectives, body(): gain_grad = lax.psum(local_gain, ('dp', 'seq'))  66 us
    all_gather x1, waiting for transfers between devices, body(): normed_all = lax.all_gather(normed, 'seq', axis=0, tiled=True)  64.3 us
    unnamed x7, waiting for transfers between devices  47.4 us
    all_gather x1, waiting for transfers between devices, body(): lax.all_gather(out_weight, 'dp', axis=0, tiled=True)  34.4 us
    unnamed x71, local copies, waits for them, and re-layouts  29.9 us
    all_to_all x1, blocking collectives, body(): lax.all_to_all(grad_out.reshape(grid_shape + (head_width,)), 'seq', split...  17.3 us
    all_to_all x1, blocking collectives, body(): lax.all_to_all(heads_out, 'seq', split_axis=0, concat_axis=3, tiled=True)  13.8 us
  transfers between devices with their start and end apart: 6, of which 5 were waited for; matrix products, arithmetic and copies ran while one was open for 12% of the time, Pallas kernels for 0%

commit v1 on v0

v1 whole, which is shorter than its diff:
```python
import functools

import jax
import jax.numpy as jnp
from jax import lax
from jax.experimental import pallas as pl
from jax.experimental.pallas import tpu as pltpu
from jax.sharding import PartitionSpec as P

HEADS = 24
HDIM = 64
EPSILON = 1e-06
XS = 4
SEQ = 8
DP = 16
TOK = 128
WIDTH = HEADS * HDIM
GROUP = WIDTH // SEQ
LANE = 128
BF = jnp.bfloat16
F32 = jnp.float32
SCALE = HDIM**-0.5
VMEM_LIMIT = 48 * 1024 * 1024


def params(semantics=1):
    return pltpu.CompilerParams(
        vmem_limit_bytes=VMEM_LIMIT, dimension_semantics=("arbitrary",) * semantics
    )


def dot_nt(a, b):
    return lax.dot_general(a, b, (((1,), (1,)), ((), ())), preferred_element_type=F32)


def dot_tn(a, b):
    return lax.dot_general(a, b, (((0,), (0,)), ((), ())), preferred_element_type=F32)


def dot_nn(a, b):
    return lax.dot_general(a, b, (((1,), (0,)), ((), ())), preferred_element_type=F32)


def spread(block, heads):
    lane = lax.broadcasted_iota(jnp.int32, block.shape, 1) // HDIM
    return jnp.concatenate(
        [jnp.where(lane == h, block, jnp.zeros_like(block)) for h in range(heads)], axis=0
    )


def pick(stacked, heads):
    rows = stacked.shape[0] // heads
    lane = lax.broadcasted_iota(jnp.int32, (rows, stacked.shape[1]), 1) // HDIM
    out = stacked[:rows]
    for h in range(1, heads):
        out = jnp.where(lane == h, stacked[h * rows : (h + 1) * rows], out)
    return out


def soft(scores, heads, valid=None):
    cols = scores.shape[1] // heads
    probs = []
    for h in range(heads):
        part = scores[:, h * cols : (h + 1) * cols] * SCALE
        if valid is not None:
            part = jnp.where(valid, part, -jnp.inf)
        raised = jnp.exp(part - jnp.max(part, axis=-1, keepdims=True))
        probs.append(raised / jnp.sum(raised, axis=-1, keepdims=True))
    return probs


def score_grad(probs, dprobs):
    cols = probs[0].shape[1]
    parts = []
    for h, prob in enumerate(probs):
        dpart = dprobs[:, h * cols : (h + 1) * cols]
        inner = jnp.sum(prob * dpart, axis=-1, keepdims=True)
        parts.append((prob * (dpart - inner) * SCALE).astype(BF))
    return jnp.concatenate(parts, axis=1)


def rounded(probs):
    return jnp.concatenate([p.astype(BF) for p in probs], axis=1)


PAIRS = 4


def spatial_fwd_kernel(q_ref, k_ref, v_ref, out_ref):
    for pair in range(PAIRS):
        cols = slice(pair * LANE, (pair + 1) * LANE)
        probs = soft(dot_nt(q_ref[:, cols], spread(k_ref[:, cols], 2)), 2)
        out_ref[:, cols] = dot_nn(rounded(probs), spread(v_ref[:, cols], 2)).astype(BF)


def spatial_fwd(q, k, v):
    spec = pl.BlockSpec((TOK, PAIRS * LANE), lambda i: (0, i))
    return pl.pallas_call(
        spatial_fwd_kernel,
        grid=(WIDTH // (PAIRS * LANE),),
        in_specs=[spec] * 3,
        out_specs=spec,
        out_shape=jax.ShapeDtypeStruct((TOK, WIDTH), BF),
        compiler_params=params(),
        name="spatial_fwd",
    )(q, k, v)


def spatial_bwd_kernel(gi_ref, w_ref, q_ref, k_ref, v_ref, dq_ref, dk_ref, dv_ref):
    dmixed = dot_nn(gi_ref[...], w_ref[...]).astype(BF)
    for pair in range(PAIRS):
        cols = slice(pair * LANE, (pair + 1) * LANE)
        q, dout = q_ref[:, cols], dmixed[:, cols]
        keys, values = spread(k_ref[:, cols], 2), spread(v_ref[:, cols], 2)
        probs = soft(dot_nt(q, keys), 2)
        dscores = score_grad(probs, dot_nt(dout, values))
        dv_ref[:, cols] = pick(dot_tn(rounded(probs), dout), 2).astype(BF)
        dq_ref[:, cols] = dot_nn(dscores, keys).astype(BF)
        dk_ref[:, cols] = pick(dot_tn(dscores, q), 2).astype(BF)


def spatial_bwd(grad_input, whole_out, q, k, v):
    spec = pl.BlockSpec((TOK, PAIRS * LANE), lambda i: (0, i))
    return pl.pallas_call(
        spatial_bwd_kernel,
        grid=(WIDTH // (PAIRS * LANE),),
        in_specs=[
            pl.BlockSpec((TOK, WIDTH), lambda i: (0, 0)),
            pl.BlockSpec((WIDTH, PAIRS * LANE), lambda i: (0, i)),
        ]
        + [spec] * 3,
        out_specs=[spec] * 3,
        out_shape=[jax.ShapeDtypeStruct((TOK, WIDTH), BF)] * 3,
        compiler_params=params(),
        name="spatial_bwd",
    )(grad_input, whole_out, q, k, v)


OUT_BLOCK = 512


def out_norm_kernel(mixed_ref, w_ref, in_ref, gain_ref, hidden_ref, normed_ref):
    step = pl.program_id(0)
    block = in_ref[...].astype(F32) + dot_nt(mixed_ref[...], w_ref[...])
    start = pl.multiple_of(step * OUT_BLOCK, OUT_BLOCK)
    hidden_ref[:, pl.ds(start, OUT_BLOCK)] = block.astype(BF)

    @pl.when(step == pl.num_programs(0) - 1)
    def _():
        wide = hidden_ref[...].astype(F32)
        inverse = lax.rsqrt(jnp.mean(wide * wide, axis=-1, keepdims=True) + EPSILON)
        normed_ref[...] = (wide * inverse * gain_ref[...]).astype(BF)


def out_norm(mixed, whole_out, inputs, gain):
    whole = pl.BlockSpec((TOK, WIDTH), lambda i: (0, 0))
    return pl.pallas_call(
        out_norm_kernel,
        grid=(WIDTH // OUT_BLOCK,),
        in_specs=[
            whole,
            pl.BlockSpec((OUT_BLOCK, WIDTH), lambda i: (i, 0)),
            pl.BlockSpec((TOK, OUT_BLOCK), lambda i: (0, i)),
            pl.BlockSpec((1, WIDTH), lambda i: (0, 0)),
        ],
        out_specs=[whole, whole],
        out_shape=[jax.ShapeDtypeStruct((TOK, WIDTH), BF)] * 2,
        compiler_params=params(),
        name="out_norm",
    )(mixed, whole_out, inputs, gain)


PADDED = 256
THREE = 3 * PADDED


def widen_kernel(w_ref, out_ref):
    rows = w_ref.shape[0]
    block = w_ref[...]
    for j in range(3):
        for h in range(3):
            out_ref[:, j * PADDED + h * HDIM : j * PADDED + (h + 1) * HDIM] = block[
                :, (h * 3 + j) * HDIM : (h * 3 + j + 1) * HDIM
            ]
        out_ref[:, j * PADDED + GROUP : (j + 1) * PADDED] = jnp.zeros((rows, PADDED - GROUP), BF)


def widen(head_proj):
    rows = 768
    return pl.pallas_call(
        widen_kernel,
        grid=(WIDTH // rows,),
        in_specs=[pl.BlockSpec((rows, 3 * GROUP), lambda i: (i, 0))],
        out_specs=pl.BlockSpec((rows, THREE), lambda i: (i, 0)),
        out_shape=jax.ShapeDtypeStruct((WIDTH, THREE), BF),
        compiler_params=params(),
        name="widen",
    )(head_proj)


POS = 16


def temporal_kernel(order_ref, *refs):
    proj, (grad_ref, out_ref, dproj_ref) = refs[:SEQ], refs[SEQ:]

    def rows(j):
        return jnp.concatenate(
            [p[:, j * PADDED : j * PADDED + GROUP] for p in proj], axis=0
        )

    q = rows(0)
    keys, values = spread(rows(1), 3), spread(rows(2), 3)
    dout = jnp.concatenate([grad_ref[order_ref[r]] for r in range(SEQ)], axis=0)
    shape = (SEQ * POS, SEQ * POS)
    valid = (
        lax.broadcasted_iota(jnp.int32, shape, 0) % POS
        == lax.broadcasted_iota(jnp.int32, shape, 1) % POS
    )
    probs = soft(dot_nt(q, keys), 3, valid)
    prob_round = rounded(probs)
    heads_out = dot_nn(prob_round, values).astype(BF)
    dscores = score_grad(probs, dot_nt(dout, values))
    grads = (
        dot_nn(dscores, keys).astype(BF),
        pick(dot_tn(dscores, q), 3).astype(BF),
        pick(dot_tn(prob_round, dout), 3).astype(BF),
    )
    for r in range(SEQ):
        here = slice(r * POS, (r + 1) * POS)
        out_ref[order_ref[r]] = heads_out[here]
        for j in range(3):
            dproj_ref[r, :, j * PADDED : j * PADDED + GROUP] = grads[j][here]
            dproj_ref[r, :, j * PADDED + GROUP : (j + 1) * PADDED] = jnp.zeros(
                (POS, PADDED - GROUP), BF
            )


def temporal(order, proj, grad_heads):
    frame = pl.BlockSpec((POS, THREE), lambda i, o: (i, 0))
    heads = pl.BlockSpec((SEQ, POS, GROUP), lambda i, o: (0, i, 0))
    return pl.pallas_call(
        temporal_kernel,
        grid_spec=pltpu.PrefetchScalarGridSpec(
            num_scalar_prefetch=1,
            grid=(TOK // POS,),
            in_specs=[frame] * SEQ + [heads],
            out_specs=[heads, pl.BlockSpec((SEQ, POS, THREE), lambda i, o: (0, i, 0))],
        ),
        out_shape=[
            jax.ShapeDtypeStruct((SEQ, TOK, GROUP), BF),
            jax.ShapeDtypeStruct((SEQ, TOK, THREE), BF),
        ],
        compiler_params=params(),
        name="temporal",
    )(order, *proj, grad_heads)


GRAD_ROWS = 512


def qkv_grad_kernel(factor, *refs):
    frames, dproj_ref, out_ref = refs[:-2], refs[-2], refs[-1]
    left = jnp.concatenate([f[...] for f in frames], axis=0)
    right = dproj_ref[...].reshape(SEQ * TOK, THREE)
    full = (dot_tn(left, right) * factor).astype(BF)
    for j in range(3):
        for h in range(3):
            out_ref[:, (h * 3 + j) * HDIM : (h * 3 + j + 1) * HDIM] = full[
                :, j * PADDED + h * HDIM : j * PADDED + (h + 1) * HDIM
            ]


def qkv_product(frames, dproj, factor):
    return pl.pallas_call(
        functools.partial(qkv_grad_kernel, factor),
        grid=(WIDTH // GRAD_ROWS,),
        in_specs=[pl.BlockSpec((f.shape[0], GRAD_ROWS), lambda i: (0, i)) for f in frames]
        + [pl.BlockSpec((SEQ, TOK, THREE), lambda i: (0, 0, 0))],
        out_specs=pl.BlockSpec((GRAD_ROWS, 3 * GROUP), lambda i: (i, 0)),
        out_shape=jax.ShapeDtypeStruct((WIDTH, 3 * GROUP), BF),
        compiler_params=params(),
        name="qkv_product",
    )(*frames, dproj)


SHARE = 12
SLOT = 16
FOUR = 4


def grad_input_kernel(factor, sum_a, sum_b, sum_c, sum_d, hidden_ref, resid_ref, gain_ref,
                      out_ref, groups_ref, gain_out_ref):
    def wide(ref):
        return ref[...].astype(F32)

    dnormed = (wide(sum_a) + wide(sum_b) + wide(sum_c) + wide(sum_d)).astype(BF).astype(F32)
    hidden = wide(hidden_ref)
    inverse = lax.rsqrt(jnp.mean(hidden * hidden, axis=-1, keepdims=True) + EPSILON)
    unit = hidden * inverse
    gain_out_ref[...] = jnp.sum(dnormed * unit, axis=0, keepdims=True) * factor
    scaled = dnormed * gain_ref[...]
    through = inverse * (scaled - unit * jnp.mean(scaled * unit, axis=-1, keepdims=True))
    grad = (wide(resid_ref) + through).astype(BF)
    out_ref[...] = grad
    rows, cols = FOUR * SHARE * SEQ, FOUR * SLOT * SEQ
    source = lax.broadcasted_iota(jnp.int32, (rows, cols), 0)
    target = lax.broadcasted_iota(jnp.int32, (rows, cols), 1)
    group = target // (FOUR * SLOT)
    block = (target // SLOT) % FOUR
    turn = target % SLOT
    wanted = block * (SHARE * SEQ) + group * SHARE + turn
    move = jnp.where((source == wanted) & (turn < SHARE), 1.0, 0.0).astype(BF)
    for four in range(DP // FOUR):
        moved = dot_nn(grad[:, four * rows : (four + 1) * rows], move).astype(BF)
        for j in range(SEQ):
            groups_ref[j, :, four * FOUR * SLOT : (four + 1) * FOUR * SLOT] = moved[
                :, j * FOUR * SLOT : (j + 1) * FOUR * SLOT
            ]


def grad_input_call(sums, hidden, resid, gain, factor):
    return pl.pallas_call(
        functools.partial(grad_input_kernel, factor),
        out_shape=[
            jax.ShapeDtypeStruct((TOK, WIDTH), BF),
            jax.ShapeDtypeStruct((SEQ, TOK, DP * SLOT), BF),
            jax.ShapeDtypeStruct((1, WIDTH), F32),
        ],
        compiler_params=pltpu.CompilerParams(vmem_limit_bytes=VMEM_LIMIT),
        name="grad_input",
    )(*sums, hidden, resid, gain)


def out_product_kernel(factor, order_ref, groups_ref, *refs):
    frames, out_ref = refs[:-1], refs[-1]
    left = jnp.concatenate([groups_ref[order_ref[r]] for r in range(SEQ)], axis=0)
    right = jnp.concatenate([f[...] for f in frames], axis=0)
    out_ref[...] = (dot_tn(left, right) * factor).astype(BF)


def out_product(order, groups, frames, factor):
    cols = 512
    return pl.pallas_call(
        functools.partial(out_product_kernel, factor),
        grid_spec=pltpu.PrefetchScalarGridSpec(
            num_scalar_prefetch=1,
            grid=(WIDTH // cols,),
            in_specs=[pl.BlockSpec((SEQ, TOK, DP * SLOT), lambda i, o: (0, 0, 0))]
            + [pl.BlockSpec((f.shape[0], cols), lambda i, o: (0, i)) for f in frames],
            out_specs=pl.BlockSpec((DP * SLOT, cols), lambda i, o: (0, i)),
        ),
        out_shape=jax.ShapeDtypeStruct((DP * SLOT, WIDTH), BF),
        compiler_params=params(),
        name="out_product",
    )(order, groups, *frames)


def along_x(array, shift):
    pairs = [(i, ((i // 2 + shift) % XS) * 2 + i % 2) for i in range(SEQ)]
    return lax.ppermute(array, "seq", pairs)


def across_y(array):
    return lax.ppermute(array, "seq", [(i, i ^ 1) for i in range(SEQ)])


HALF = TOK // 2


def gather_frames(own):
    behind, ahead, partner = along_x(own, 1), along_x(own, -1), across_y(own)
    far_top, far_low = along_x(behind[:HALF], 1), along_x(ahead[HALF:], -1)
    partner_behind, partner_ahead = along_x(partner, 1), along_x(partner, -1)
    return (
        own, behind, ahead, far_top, far_low,
        partner, partner_behind, partner_ahead, across_y(far_top), across_y(far_low),
    )


def whole_frames(parts):
    own, behind, ahead, top, low, partner, pbehind, pahead, ptop, plow = parts
    return (
        own, behind, ahead, jnp.concatenate([top, low], axis=0),
        partner, pbehind, pahead, jnp.concatenate([ptop, plow], axis=0),
    )


def scatter_frames(shares):
    own, behind, ahead, far, partner, pbehind, pahead, pfar = shares
    far = far + across_y(pfar)
    partner = partner + along_x(pbehind, -1) + along_x(pahead, 1)
    top, low = along_x(far[:HALF], -1), along_x(far[HALF:], 1)
    behind = jnp.concatenate([behind[:HALF] + top, behind[HALF:]], axis=0)
    ahead = jnp.concatenate([ahead[:HALF], ahead[HALF:] + low], axis=0)
    return own, across_y(partner), along_x(behind, -1), along_x(ahead, 1)


def body(
    inputs, spatial_q, spatial_k, spatial_v, out_weight, norm_gain, qkv_weight, grad_out, grad_resid
):
    block_shape = inputs.shape
    factor = (TOK * DP * SEQ) ** (-0.5)
    flat_in, q, k, v, dout, resid = (
        a.reshape(TOK, WIDTH)
        for a in (inputs, spatial_q, spatial_k, spatial_v, grad_out, grad_resid)
    )
    gain = norm_gain.reshape(1, WIDTH)
    me = lax.axis_index("seq")
    place_x, place_y = me // 2, me % 2
    order = jnp.stack(
        [((place_x + s) % XS) * 2 + y for y in (place_y, 1 - place_y) for s in (0, 3, 1, 2)]
    ).astype(jnp.int32)

    whole_out = lax.all_gather(out_weight, "dp", axis=0, tiled=True)
    head_proj = lax.all_gather(qkv_weight, "dp", axis=0, tiled=True)

    grad_heads = lax.all_to_all(
        dout.reshape(TOK, SEQ, GROUP).transpose(1, 0, 2), "seq", 0, 0, tiled=True
    )
    mixed = spatial_fwd(q, k, v)
    mixed_parts = gather_frames(mixed)
    hidden, normed = out_norm(mixed, whole_out, flat_in, gain)
    normed_parts = gather_frames(normed)
    wide_proj = widen(head_proj)
    proj = [dot_nn(f, wide_proj).astype(BF) for f in whole_frames(normed_parts)]
    heads_out, dproj = temporal(order, proj, grad_heads)
    shares = [dot_nt(dproj[r], wide_proj).astype(BF) for r in range(SEQ)]
    sums = scatter_frames(shares)
    qkv_share = qkv_product(normed_parts, dproj, factor)
    qkv_grad = lax.psum_scatter(qkv_share, "dp", scatter_dimension=0, tiled=True).astype(F32)
    temporal_out = lax.all_to_all(heads_out, "seq", 0, 0, tiled=True)
    temporal_out = temporal_out.transpose(1, 0, 2).reshape(TOK, WIDTH)

    grad_input, groups, local_gain = grad_input_call(sums, hidden, resid, gain, factor)
    gain_grad = lax.psum(local_gain.reshape(WIDTH), ("dp", "seq"))
    groups = lax.all_to_all(groups, "seq", 0, 0, tiled=True)
    out_share = out_product(order, groups, mixed_parts, factor)
    out_rows = lax.psum_scatter(out_share, "dp", scatter_dimension=0, tiled=True)
    out_all = lax.all_to_all(
        jnp.broadcast_to(out_rows[None], (SEQ, SLOT, WIDTH)), "seq", 0, 0, tiled=True
    )
    out_grad = out_all[:, :SHARE].reshape(SEQ * SHARE, WIDTH).astype(F32)
    grad_q, grad_k, grad_v = spatial_bwd(grad_input, whole_out, q, k, v)
    return tuple(
        a.reshape(block_shape) for a in (hidden, temporal_out, grad_input, grad_q, grad_k, grad_v)
    ) + (qkv_grad, out_grad, gain_grad)


def solution(mesh):
    tokens = P("dp", "seq", None, None, None)
    return jax.shard_map(
        body,
        mesh=mesh,
        in_specs=(
            tokens, tokens, tokens, tokens, P("dp", None), P(), P("dp", "seq"), tokens, tokens,
        ),
        out_specs=(
            tokens, tokens, tokens, tokens, tokens, tokens, P("dp", "seq"), P("dp", None), P(),
        ),
        check_vma=False,
    )
```

time: 482 us -> 363 us (0.75)
  waiting for transfers between devices: 228 us -> 127 us
  starting transfers between devices: 0.24 us -> 59.7 us
  matrix products: 60.4 us -> 11 us
  local copies, waits for them, and re-layouts: 67.5 us -> 32.8 us
  Pallas kernels: 0 us -> 33.9 us
  blocking collectives: 97.1 us -> 80.4 us
  other arithmetic: 7.35 us -> 1.83 us
    unnamed x7 -> x4, waiting for transfers between devices: 47.4 us -> 1.41 us
    ppermute x0 -> x26, starting transfers between devices: none -> 42.1 us  [the longest x18 24.7 us: along_x(): return lax.ppermute(array, 'seq', pairs)]
    dot_general x16, matrix products: 52.9 us -> 11 us  [the longest x8 7.17 us: dot_nt(): lax.dot_general(a, b, (((1,), (1,)), ((), ())), preferred_element_type=F32)]
    all_gather x3 -> x2, waiting for transfers between devices: 98.7 us -> 58.9 us  [the longest x1 31.7 us: body(): whole_out = lax.all_gather(out_weight, 'dp', axis=0, tiled=True)]
    reduce_scatter x1 -> x2, waiting for transfers between devices: 72 us -> 33.5 us  [the longest x1 33.5 us: body(): lax.psum_scatter(out_share, 'dp', scatter_dimension=0, tiled=True)]
    pallas_call x0 -> x8, Pallas kernels: none -> 33.9 us  [the longest x1 8.55 us: spatial_bwd(): pl.pallas_call(spatial_bwd_kernel, grid=(WIDTH // (PAIRS * LANE),), in_sp...]
    ppermute x0 -> x26, waiting for transfers between devices: none -> 33.2 us  [the longest x18 20.3 us: along_x(): return lax.ppermute(array, 'seq', pairs)]
    all_to_all x0 -> x3, starting transfers between devices: none -> 17.4 us  [the longest x1 7.01 us: body(): lax.all_to_all(dout.reshape(TOK, SEQ, GROUP).transpose(1, 0, 2), 'seq', 0...]
  transfers between devices with their start and end apart: 6 -> 33, of which waited for: 5 -> 15; matrix products, arithmetic and copies ran while one was open for 12% -> 5% of each run, Pallas kernels for 0% -> 6%
where the time goes in v1:
time: 363 us; the launch traced here: 361 us
  waiting for transfers between devices  127 us (35%)
  blocking collectives  80.4 us (22%)
  starting transfers between devices  59.7 us (16%)
  Pallas kernels  33.9 us (9%)
  local copies, waits for them, and re-layouts  32.8 us (9%)
  between operations  14.4 us (4%)
  matrix products  11 us (3%)
    psum x1, blocking collectives, body(): gain_grad = lax.psum(local_gain.reshape(WIDTH), ('dp', 'seq'))  64.8 us
    reduce_scatter x1, waiting for transfers between devices, body(): lax.psum_scatter(out_share, 'dp', scatter_dimension=0, tiled=True)  33.5 us
    all_gather x1, waiting for transfers between devices, body(): whole_out = lax.all_gather(out_weight, 'dp', axis=0, tiled=True)  31.7 us
    all_gather x1, waiting for transfers between devices, body(): head_proj = lax.all_gather(qkv_weight, 'dp', axis=0, tiled=True)  27.2 us
    ppermute x18, starting transfers between devices, along_x(): return lax.ppermute(array, 'seq', pairs)  24.7 us
    unnamed x82, local copies, waits for them, and re-layouts  21.5 us
    ppermute x18, waiting for transfers between devices, along_x(): return lax.ppermute(array, 'seq', pairs)  20.3 us
    ppermute x8, starting transfers between devices, across_y(): return lax.ppermute(array, 'seq', [(i, i ^ 1) for i in range(SEQ)])  17.4 us
  transfers between devices with their start and end apart: 33, of which 15 were waited for; matrix products, arithmetic and copies ran while one was open for 5% of the time, Pallas kernels for 6%

profile of v1, /device:TPU:0, one launch (start us, length us, event | category | flops | bytes accessed | tf_op | source)
XLA Modules:
  0.0 361.1 jit_solution(5640003939578425261)
XLA Ops:
  11.3 7.0 %all-to-all-start = ((bf16[8,128,192]{1,2,0:T(8,128)(2,1)}), bf16[8,128,192]{1,2,0:T(8,128)(2,1)}, u32[]{:S(2)}, u32[]{:S(2)}) async-start(bf16[8,128,192]{1,2,0:T(8,128)(2,1)} %copy.20), calls=%async_computation | async-start | bytes 786432 | tf_op jit(solution)/shard_map/all_to_all | solution.py:418
  18.4 2.8 spatial_fwd.1.mixed_ref.refs_0_
  21.2 31.7 %all-gather.3.cloned.1.call-done.w_ref = bf16[1536,1536]{1,0:T(8,128)(2,1)} async-done(((bf16[96,1536]{1,0:T(8,128)(2,1)}), bf16[1536,1536]{1,0:T(8,128)(2,1)}) %all-gather.3.cloned.1.call-update) | async-done | bytes 4718608 | tf_op jit(solution)/shard_map/all_gather | solution.py:415
  53.0 2.3 copy-done
  55.3 2.9 out_norm.1
  61.6 27.2 %all-gather.5.cloned.1.call-done.w_ref = bf16[1536,576]{1,0:T(8,128)(2,1)} async-done(((bf16[96,576]{1,0:T(8,128)(2,1)}), bf16[1536,576]{1,0:T(8,128)(2,1)}) %all-gather.5.cloned.1.call-update) | async-done | bytes 1769488 | tf_op jit(solution)/shard_map/all_gather | solution.py:416
  91.0 2.9 collective-permute-start.4
  94.3 2.8 collective-permute-start.3
  98.2 5.6 %collective-permute-done.4.refs_5_ = bf16[128,1536]{1,0:T(8,128)(2,1)S(1)} collective-permute-done((bf16[128,1536]{1,0:T(8,128)(2,1)S(1)}, bf16[128,1536]{1,0:T(8,128)(2,1)S(1)}, u32[]{:S(2)}, u32[]{:S(2)}) %collective-permute-start.4) | collective-permute-done | bytes 393248 | tf_op jit(solution)/shard_map/ppermute | solution.py:365
  107.6 2.8 collective-permute-start.8
  111.7 3.7 %collective-permute-done.5.refs_6_ = bf16[128,1536]{1,0:T(8,128)(2,1)S(1)} collective-permute-done((bf16[128,1536]{1,0:T(8,128)(2,1)S(1)}, bf16[128,1536]{1,0:T(8,128)(2,1)S(1)}, u32[]{:S(2)}, u32[]{:S(2)}) %collective-permute-start.5) | collective-permute-done | bytes 393248 | tf_op jit(solution)/shard_map/ppermute | solution.py:361
  116.5 2.5 collective-permute-done.7.refs_8_
  119.5 8.4 %temporal.1 = (bf16[8,128,192]{2,1,0:T(8,128)(2,1)S(1)}, bf16[8,128,768]{2,1,0:T(8,128)(2,1)S(1)}) custom-call(s32[8]{0:T(128)S(1)} %stack.35.order_ref, bf16[128,768]{1,0:T(8,128)(2,1)S(1)} %convolution_convert_fusion.15.refs_0_, bf16[128,768]{1,0:T(8,128)(2,1)S(1)} %convolution_convert_fusion.14.refs_1_, ...), custom_call_target="tpu_custom_call" | custom-call | tf_op jit(solution)/shard_map/temporal/pallas_call | solution.py:242
  130.7 3.0 collective-permute-start.12
  135.0 2.9 collective-permute-start.9
  138.8 3.4 collective-permute-done.12
  145.8 2.2 collective-permute-start.11
  149.1 2.8 collective-permute-start.14
  151.9 4.6 %collective-permute-done.15 = bf16[64,1536]{1,0:T(8,128)(2,1)S(1)} collective-permute-done((bf16[64,1536]{1,0:T(8,128)(2,1)S(1)}, bf16[64,1536]{1,0:T(8,128)(2,1)S(1)}, u32[]{:S(2)}, u32[]{:S(2)}) %collective-permute-start.15) | collective-permute-done | bytes 196640 | tf_op jit(solution)/shard_map/ppermute | solution.py:361
  162.1 5.8 %collective-permute-done.16.sum_d = bf16[128,1536]{1,0:T(8,128)(2,1)S(1)} collective-permute-done((bf16[128,1536]{1,0:T(8,128)(2,1)S(1)}, bf16[128,1536]{1,0:T(8,128)(2,1)S(1)}, u32[]{:S(2)}, u32[]{:S(2)}) %collective-permute-start.16) | collective-permute-done | bytes 393248 | tf_op jit(solution)/shard_map/ppermute | solution.py:361
  170.4 3.5 all-to-all-start.2
  173.9 2.6 collective-permute-done.17.refs_1_
  178.3 2.6 collective-permute-start.23
  183.9 2.4 collective-permute-done.19.refs_3_
  188.5 2.9 collective-permute-start.25
  202.1 4.4 %out_product.1 = bf16[256,1536]{1,0:T(8,128)(2,1)} custom-call(s32[8]{0:T(128)S(1)} %stack.35.order_ref, bf16[8,128,256]{2,1,0:T(8,128)(2,1)S(1)} %all-to-all-done.2.groups_ref, bf16[128,1536]{1,0:T(8,128)(2,1)S(1)} %spatial_fwd.1.mixed_ref.refs_0_, bf16[128,1536]{1,0:T(8,128)(2,1)} %collective-permute-done.17.refs_1_, ...), custom_call_target="tpu_custom_call" | custom-call | tf_op jit(solution)/shard_map/out_product/pallas_call | solution.py:344
  213.4 4.4 %qkv_product.1 = bf16[1536,576]{1,0:T(8,128)(2,1)} custom-call(bf16[128,1536]{1,0:T(8,128)(2,1)S(1)} %copy-done.9, bf16[128,1536]{1,0:T(8,128)(2,1)S(1)} %collective-permute-done.refs_1_, bf16[128,1536]{1,0:T(8,128)(2,1)S(1)} %collective-permute-done.1.refs_2_, bf16[64,1536]{1,0:T(8,128)(2,1)S(1)} %copy-done.17, ...), custom_call_target="tpu_custom_call" | custom-call | tf_op jit(solution)/shard_map/qkv_product/pallas_call | solution.py:275
  219.3 15.7 %all_to_all.20 = bf16[8,128,192]{1,2,0:T(8,128)(2,1)S(1)} all-to-all(bf16[8,128,192]{1,2,0:T(8,128)(2,1)S(1)} %copy.22), channel_id=1, replica_groups=mesh['dp'=16,'seq'=8] {'seq'}, dimensions={0} | all-to-all | bytes 786432 | tf_op jit(solution)/shard_map/all_to_all | solution.py:432
  234.9 33.5 %reduce-scatter.5.cloned.1.call-done = bf16[16,1536]{1,0:T(8,128)(2,1)} async-done(((bf16[256,1536]{1,0:T(8,128)(2,1)}), bf16[16,1536]{1,0:T(8,128)(2,1)}) %reduce-scatter.5.cloned.1.call-update) | async-done | bytes 49168 | tf_op jit(solution)/shard_map/reduce_scatter | solution.py:439
  270.0 6.9 %all-to-all-start.3 = ((bf16[8,16,1536]{2,1,0:T(8,128)(2,1)}), bf16[8,16,1536]{2,1,0:T(8,128)(2,1)S(1)}, u32[]{:S(2)}, u32[]{:S(2)}) async-start(bf16[8,16,1536]{2,1,0:T(8,128)(2,1)} %broadcast_in_dim.2), calls=%async_computation.5 | async-start | bytes 786432 | tf_op jit(solution)/shard_map/all_to_all | solution.py:440
  278.6 8.6 %spatial_bwd.1 = (bf16[128,1536]{1,0:T(8,128)(2,1)}, bf16[128,1536]{1,0:T(8,128)(2,1)}, bf16[128,1536]{1,0:T(8,128)(2,1)}) custom-call(bf16[128,1536]{1,0:T(8,128)(2,1)S(1)} %copy-done.25, bf16[1536,1536]{1,0:T(8,128)(2,1)} %all-gather.3.cloned.1.call-done.w_ref, bf16[128,1536]{1,0:T(8,128)(2,1)S(1)} %bitcast.69, bf16[128,1536]{1,0:T(8,128)(2,1)S(1)} %bitcast.71, ...), custom_call_target="tpu_custom_call" | custom-call | tf_op jit(solution)/shard_map/spatial_bwd/pallas_call | solution.py:124
  287.1 64.8 %psum.7 = f32[1536]{0:T(1024)} all-reduce(f32[1536]{0:T(1024)S(1)} %reduce), channel_id=1, replica_groups=mesh['dp'=16,'seq'=8] {'dp','seq'}, use_global_device_ids=true, to_apply=%region_2.3 | all-reduce | flops 1536 | bytes 12288 | tf_op jit(solution)/shard_map/psum | solution.py:436
  (168 shorter events, 67.0 us)
Async XLA Ops:
  7.2 45.7 %all-gather.3.cloned.1.call-start = ((), (), s32[]{:S(2)}) async-start(), calls=%async_computation.6 | async-start | bytes 5013504 | tf_op jit(solution)/shard_map/all_gather | solution.py:415
  8.0 80.7 %all-gather.5.cloned.1.call-start = ((), (), s32[]{:S(2)}) async-start(), calls=%async_computation.7 | async-start | bytes 2088960 | tf_op jit(solution)/shard_map/all_gather | solution.py:416
  11.3 49.1 %all-to-all-start = ((bf16[8,128,192]{1,2,0:T(8,128)(2,1)}), bf16[8,128,192]{1,2,0:T(8,128)(2,1)}, u32[]{:S(2)}, u32[]{:S(2)}) async-start(bf16[8,128,192]{1,2,0:T(8,128)(2,1)} %copy.20), calls=%async_computation | async-start | bytes 786432 | tf_op jit(solution)/shard_map/all_to_all | solution.py:418
  58.2 36.1 %collective-permute-start.1 = (bf16[128,1536]{1,0:T(8,128)(2,1)S(1)}, bf16[128,1536]{1,0:T(8,128)(2,1)S(1)}, u32[]{:S(2)}, u32[]{:S(2)}) collective-permute-start(bf16[128,1536]{1,0:T(8,128)(2,1)S(1)} %get-tuple-element.20.refs_0_), channel_id=1, source_target_pairs={{0,6},{1,7},{2,0},{3,1},{4,2},{5,3},{6,4},{7,5},{8,14},{9,15},{10,... | collective-permute-start | bytes 1179656 | tf_op jit(solution)/shard_map/ppermute | solution.py:361
  60.1 37.0 %collective-permute-start = (bf16[128,1536]{1,0:T(8,128)(2,1)S(1)}, bf16[128,1536]{1,0:T(8,128)(2,1)S(1)}, u32[]{:S(2)}, u32[]{:S(2)}) collective-permute-start(bf16[128,1536]{1,0:T(8,128)(2,1)S(1)} %get-tuple-element.20.refs_0_), channel_id=1, source_target_pairs={{0,2},{1,3},{2,4},{3,5},{4,6},{5,7},{6,0},{7,1},{8,10},{9,11},{10,... | collective-permute-start | bytes 1179656 | tf_op jit(solution)/shard_map/ppermute | solution.py:361
  91.0 12.8 %collective-permute-start.4 = (bf16[128,1536]{1,0:T(8,128)(2,1)S(1)}, bf16[128,1536]{1,0:T(8,128)(2,1)S(1)}, u32[]{:S(2)}, u32[]{:S(2)}) collective-permute-start(bf16[128,1536]{1,0:T(8,128)(2,1)S(1)} %get-tuple-element.20.refs_0_), channel_id=1, source_target_pairs={{0,1},{1,0},{2,3},{3,2},{4,5},{5,4},{6,7},{7,6},{8,9},{9,8},{10,11... | collective-permute-start | bytes 1179656 | tf_op jit(solution)/shard_map/ppermute | solution.py:365
  94.3 13.3 %collective-permute-start.3 = (bf16[64,1536]{1,0:T(8,128)(2,1)S(1)}, bf16[64,1536]{1,0:T(8,128)(2,1)S(1)}, u32[]{:S(2)}, u32[]{:S(2)}) collective-permute-start(bf16[64,1536]{1,0:T(8,128)(2,1)S(1)} %slice.77), channel_id=1, source_target_pairs={{0,6},{1,7},{2,0},{3,1},{4,2},{5,3},{6,4},{7,5},{8,14},{9,15},{10,... | collective-permute-start | bytes 589832 | tf_op jit(solution)/shard_map/ppermute | solution.py:361
  97.1 13.2 %collective-permute-start.2 = (bf16[64,1536]{1,0:T(8,128)(2,1)S(1)}, bf16[64,1536]{1,0:T(8,128)(2,1)S(1)}, u32[]{:S(2)}, u32[]{:S(2)}) collective-permute-start(bf16[64,1536]{1,0:T(8,128)(2,1)S(1)} %slice.76), channel_id=1, source_target_pairs={{0,2},{1,3},{2,4},{3,5},{4,6},{5,7},{6,0},{7,1},{8,10},{9,11},{10,... | collective-permute-start | bytes 589832 | tf_op jit(solution)/shard_map/ppermute | solution.py:361
  103.8 11.6 %collective-permute-start.5 = (bf16[128,1536]{1,0:T(8,128)(2,1)S(1)}, bf16[128,1536]{1,0:T(8,128)(2,1)S(1)}, u32[]{:S(2)}, u32[]{:S(2)}) collective-permute-start(bf16[128,1536]{1,0:T(8,128)(2,1)S(1)} %collective-permute-done.4.refs_5_), channel_id=1, source_target_pairs={{0,2},{1,3},{2,4},{3,5},{4,6},{5,7},{6,0},{7,1},{8,10},{9,11},{10,... | collective-permute-start | bytes 1179656 | tf_op jit(solution)/shard_map/ppermute | solution.py:361
  105.7 10.2 %collective-permute-start.6 = (bf16[128,1536]{1,0:T(8,128)(2,1)S(1)}, bf16[128,1536]{1,0:T(8,128)(2,1)S(1)}, u32[]{:S(2)}, u32[]{:S(2)}) collective-permute-start(bf16[128,1536]{1,0:T(8,128)(2,1)S(1)} %collective-permute-done.4.refs_5_), channel_id=1, source_target_pairs={{0,6},{1,7},{2,0},{3,1},{4,2},{5,3},{6,4},{7,5},{8,14},{9,15},{10,... | collective-permute-start | bytes 1179656 | tf_op jit(solution)/shard_map/ppermute | solution.py:361
  107.6 8.9 %collective-permute-start.8 = (bf16[64,1536]{1,0:T(8,128)(2,1)S(1)}, bf16[64,1536]{1,0:T(8,128)(2,1)S(1)}, u32[]{:S(2)}, u32[]{:S(2)}) collective-permute-start(bf16[64,1536]{1,0:T(8,128)(2,1)S(1)} %collective-permute-done.3.refs_4_), channel_id=1, source_target_pairs={{0,1},{1,0},{2,3},{3,2},{4,5},{5,4},{6,7},{7,6},{8,9},{9,8},{10,11... | collective-permute-start | bytes 589832 | tf_op jit(solution)/shard_map/ppermute | solution.py:365
  110.9 8.1 %collective-permute-start.7 = (bf16[64,1536]{1,0:T(8,128)(2,1)S(1)}, bf16[64,1536]{1,0:T(8,128)(2,1)S(1)}, u32[]{:S(2)}, u32[]{:S(2)}) collective-permute-start(bf16[64,1536]{1,0:T(8,128)(2,1)S(1)} %collective-permute-done.2.refs_3_), channel_id=1, source_target_pairs={{0,1},{1,0},{2,3},{3,2},{4,5},{5,4},{6,7},{7,6},{8,9},{9,8},{10,11... | collective-permute-start | bytes 589832 | tf_op jit(solution)/shard_map/ppermute | solution.py:365
  130.7 11.6 %collective-permute-start.12 = (bf16[128,1536]{1,0:T(8,128)(2,1)S(1)}, bf16[128,1536]{1,0:T(8,128)(2,1)S(1)}, u32[]{:S(2)}, u32[]{:S(2)}) collective-permute-start(bf16[128,1536]{1,0:T(8,128)(2,1)S(1)} %convolution_convert_fusion.1), channel_id=1, source_target_pairs={{0,1},{1,0},{2,3},{3,2},{4,5},{5,4},{6,7},{7,6},{8,9},{9,8},{10,11... | collective-permute-start | bytes 1179656 | tf_op jit(solution)/shard_map/ppermute | solution.py:365
  134.6 10.1 %collective-permute-start.10 = (bf16[128,1536]{1,0:T(8,128)(2,1)S(1)}, bf16[128,1536]{1,0:T(8,128)(2,1)S(1)}, u32[]{:S(2)}, u32[]{:S(2)}) collective-permute-start(bf16[128,1536]{1,0:T(8,128)(2,1)S(1)} %convolution_convert_fusion.4), channel_id=1, source_target_pairs={{0,2},{1,3},{2,4},{3,5},{4,6},{5,7},{6,0},{7,1},{8,10},{9,11},{10,... | collective-permute-start | bytes 1179656 | tf_op jit(solution)/shard_map/ppermute | solution.py:361
  135.0 9.9 %collective-permute-start.9 = (bf16[128,1536]{1,0:T(8,128)(2,1)S(1)}, bf16[128,1536]{1,0:T(8,128)(2,1)S(1)}, u32[]{:S(2)}, u32[]{:S(2)}) collective-permute-start(bf16[128,1536]{1,0:T(8,128)(2,1)S(1)} %convolution_convert_fusion.5), channel_id=1, source_target_pairs={{0,6},{1,7},{2,0},{3,1},{4,2},{5,3},{6,4},{7,5},{8,14},{9,15},{10,... | collective-permute-start | bytes 1179656 | tf_op jit(solution)/shard_map/ppermute | solution.py:361
  145.8 14.2 %collective-permute-start.11 = (bf16[128,1536]{1,0:T(8,128)(2,1)S(1)}, bf16[128,1536]{1,0:T(8,128)(2,1)S(1)}, u32[]{:S(2)}, u32[]{:S(2)}) collective-permute-start(bf16[128,1536]{1,0:T(8,128)(2,1)S(1)} %fusion.1), channel_id=1, source_target_pairs={{0,1},{1,0},{2,3},{3,2},{4,5},{5,4},{6,7},{7,6},{8,9},{9,8},{10,11... | collective-permute-start | bytes 1179656 | tf_op jit(solution)/shard_map/ppermute | solution.py:365
  148.0 8.5 %collective-permute-start.15 = (bf16[64,1536]{1,0:T(8,128)(2,1)S(1)}, bf16[64,1536]{1,0:T(8,128)(2,1)S(1)}, u32[]{:S(2)}, u32[]{:S(2)}) collective-permute-start(bf16[64,1536]{1,0:T(8,128)(2,1)S(1)} %get-tuple-element.31), channel_id=1, source_target_pairs={{0,2},{1,3},{2,4},{3,5},{4,6},{5,7},{6,0},{7,1},{8,10},{9,11},{10,... | collective-permute-start | bytes 589832 | tf_op jit(solution)/shard_map/ppermute | solution.py:361
  149.1 13.0 %collective-permute-start.14 = (bf16[128,1536]{1,0:T(8,128)(2,1)S(1)}, bf16[128,1536]{1,0:T(8,128)(2,1)S(1)}, u32[]{:S(2)}, u32[]{:S(2)}) collective-permute-start(bf16[128,1536]{1,0:T(8,128)(2,1)S(1)} %pad_maximum_fusion), channel_id=1, source_target_pairs={{0,6},{1,7},{2,0},{3,1},{4,2},{5,3},{6,4},{7,5},{8,14},{9,15},{10,... | collective-permute-start | bytes 1179656 | tf_op jit(solution)/shard_map/ppermute | solution.py:361
  156.6 11.4 %collective-permute-start.16 = (bf16[128,1536]{1,0:T(8,128)(2,1)S(1)}, bf16[128,1536]{1,0:T(8,128)(2,1)S(1)}, u32[]{:S(2)}, u32[]{:S(2)}) collective-permute-start(bf16[128,1536]{1,0:T(8,128)(2,1)S(1)} %pad_maximum_fusion.1), channel_id=1, source_target_pairs={{0,2},{1,3},{2,4},{3,5},{4,6},{5,7},{6,0},{7,1},{8,10},{9,11},{10,... | collective-permute-start | bytes 1179656 | tf_op jit(solution)/shard_map/ppermute | solution.py:361
  156.7 19.9 %collective-permute-start.17 = (bf16[128,1536]{1,0:T(8,128)(2,1)S(1)}, bf16[128,1536]{1,0:T(8,128)(2,1)}, u32[]{:S(2)}, u32[]{:S(2)}) collective-permute-start(bf16[128,1536]{1,0:T(8,128)(2,1)S(1)} %spatial_fwd.1.mixed_ref.refs_0_), channel_id=1, source_target_pairs={{0,2},{1,3},{2,4},{3,5},{4,6},{5,7},{6,0},{7,1},{8,10},{9,11},{10,... | collective-permute-start | bytes 1179656 | tf_op jit(solution)/shard_map/ppermute | solution.py:361
  158.5 19.1 %collective-permute-start.21 = (bf16[128,1536]{1,0:T(8,128)(2,1)S(1)}, bf16[128,1536]{1,0:T(8,128)(2,1)}, u32[]{:S(2)}, u32[]{:S(2)}) collective-permute-start(bf16[128,1536]{1,0:T(8,128)(2,1)S(1)} %spatial_fwd.1.mixed_ref.refs_0_), channel_id=1, source_target_pairs={{0,1},{1,0},{2,3},{3,2},{4,5},{5,4},{6,7},{7,6},{8,9},{9,8},{10,11... | collective-permute-start | bytes 1179656 | tf_op jit(solution)/shard_map/ppermute | solution.py:365
  160.0 20.9 %collective-permute-start.18 = (bf16[128,1536]{1,0:T(8,128)(2,1)S(1)}, bf16[128,1536]{1,0:T(8,128)(2,1)}, u32[]{:S(2)}, u32[]{:S(2)}) collective-permute-start(bf16[128,1536]{1,0:T(8,128)(2,1)S(1)} %spatial_fwd.1.mixed_ref.refs_0_), channel_id=1, source_target_pairs={{0,6},{1,7},{2,0},{3,1},{4,2},{5,3},{6,4},{7,5},{8,14},{9,15},{10,... | collective-permute-start | bytes 1179656 | tf_op jit(solution)/shard_map/ppermute | solution.py:361
  170.4 26.0 %all-to-all-start.2 = ((bf16[8,128,256]{2,1,0:T(8,128)(2,1)}), bf16[8,128,256]{2,1,0:T(8,128)(2,1)S(1)}, u32[]{:S(2)}, u32[]{:S(2)}) async-start(bf16[8,128,256]{2,1,0:T(8,128)(2,1)} %copy-done.23), calls=%async_computation.3 | async-start | bytes 1048576 | tf_op jit(solution)/shard_map/all_to_all | solution.py:437
  173.9 94.6 %reduce-scatter.5.cloned.1.call-start = ((), (), s32[]{:S(2)}) async-start(), calls=%async_computation.9 | async-start | bytes 835584 | tf_op jit(solution)/shard_map/reduce_scatter | solution.py:439
  177.5 8.7 %collective-permute-start.19 = (bf16[64,1536]{1,0:T(8,128)(2,1)S(1)}, bf16[64,1536]{1,0:T(8,128)(2,1)S(1)}, u32[]{:S(2)}, u32[]{:S(2)}) collective-permute-start(bf16[64,1536]{1,0:T(8,128)(2,1)S(1)} %slice.84), channel_id=1, source_target_pairs={{0,2},{1,3},{2,4},{3,5},{4,6},{5,7},{6,0},{7,1},{8,10},{9,11},{10,... | collective-permute-start | bytes 589832 | tf_op jit(solution)/shard_map/ppermute | solution.py:361
  177.6 14.5 %collective-permute-start.22 = (bf16[128,1536]{1,0:T(8,128)(2,1)}, bf16[128,1536]{1,0:T(8,128)(2,1)S(1)}, u32[]{:S(2)}, u32[]{:S(2)}) collective-permute-start(bf16[128,1536]{1,0:T(8,128)(2,1)} %collective-permute-done.21.refs_5_), channel_id=1, source_target_pairs={{0,2},{1,3},{2,4},{3,5},{4,6},{5,7},{6,0},{7,1},{8,10},{9,11},{10,... | collective-permute-start | bytes 1179656 | tf_op jit(solution)/shard_map/ppermute | solution.py:361
  178.3 14.5 %collective-permute-start.23 = (bf16[128,1536]{1,0:T(8,128)(2,1)}, bf16[128,1536]{1,0:T(8,128)(2,1)S(1)}, u32[]{:S(2)}, u32[]{:S(2)}) collective-permute-start(bf16[128,1536]{1,0:T(8,128)(2,1)} %collective-permute-done.21.refs_5_), channel_id=1, source_target_pairs={{0,6},{1,7},{2,0},{3,1},{4,2},{5,3},{6,4},{7,5},{8,14},{9,15},{10,... | collective-permute-start | bytes 1179656 | tf_op jit(solution)/shard_map/ppermute | solution.py:361
  181.9 6.7 %collective-permute-start.20 = (bf16[64,1536]{1,0:T(8,128)(2,1)S(1)}, bf16[64,1536]{1,0:T(8,128)(2,1)S(1)}, u32[]{:S(2)}, u32[]{:S(2)}) collective-permute-start(bf16[64,1536]{1,0:T(8,128)(2,1)S(1)} %slice.85), channel_id=1, source_target_pairs={{0,6},{1,7},{2,0},{3,1},{4,2},{5,3},{6,4},{7,5},{8,14},{9,15},{10,... | collective-permute-start | bytes 589832 | tf_op jit(solution)/shard_map/ppermute | solution.py:361
  186.2 7.4 %collective-permute-start.24 = (bf16[64,1536]{1,0:T(8,128)(2,1)S(1)}, bf16[64,1536]{1,0:T(8,128)(2,1)S(1)}, u32[]{:S(2)}, u32[]{:S(2)}) collective-permute-start(bf16[64,1536]{1,0:T(8,128)(2,1)S(1)} %collective-permute-done.19.refs_3_), channel_id=1, source_target_pairs={{0,1},{1,0},{2,3},{3,2},{4,5},{5,4},{6,7},{7,6},{8,9},{9,8},{10,11... | collective-permute-start | bytes 589832 | tf_op jit(solution)/shard_map/ppermute | solution.py:365
  188.5 7.2 %collective-permute-start.25 = (bf16[64,1536]{1,0:T(8,128)(2,1)S(1)}, bf16[64,1536]{1,0:T(8,128)(2,1)S(1)}, u32[]{:S(2)}, u32[]{:S(2)}) collective-permute-start(bf16[64,1536]{1,0:T(8,128)(2,1)S(1)} %collective-permute-done.20.refs_4_), channel_id=1, source_target_pairs={{0,1},{1,0},{2,3},{3,2},{4,5},{5,4},{6,7},{7,6},{8,9},{9,8},{10,11... | collective-permute-start | bytes 589832 | tf_op jit(solution)/shard_map/ppermute | solution.py:365
  206.6 146.4 %reduce-scatter.3.cloned.1.call-start = ((), (), s32[]{:S(2)}) async-start(), calls=%async_computation.8 | async-start | bytes 2088960 | tf_op jit(solution)/shard_map/reduce_scatter | solution.py:431
  270.0 81.9 %all-to-all-start.3 = ((bf16[8,16,1536]{2,1,0:T(8,128)(2,1)}), bf16[8,16,1536]{2,1,0:T(8,128)(2,1)S(1)}, u32[]{:S(2)}, u32[]{:S(2)}) async-start(bf16[8,16,1536]{2,1,0:T(8,128)(2,1)} %broadcast_in_dim.2), calls=%async_computation.5 | async-start | bytes 786432 | tf_op jit(solution)/shard_map/all_to_all | solution.py:440
  (42 other events, 481.8 us)
Sparse Core Ops, SparseCore 0:
  9.8 43.1 all-gather.2
  54.6 34.0 all-gather.4
  206.7 61.7 reduce-scatter.4
  270.9 63.0 reduce-scatter.2

commit v2 on v1

--- a/solution.py
+++ b/solution.py
@@ -20,13 +20,16 @@
 BF = jnp.bfloat16
 F32 = jnp.float32
 SCALE = HDIM**-0.5
-VMEM_LIMIT = 48 * 1024 * 1024
-
-
-def params(semantics=1):
-    return pltpu.CompilerParams(
-        vmem_limit_bytes=VMEM_LIMIT, dimension_semantics=("arbitrary",) * semantics
-    )
+VMEM_LIMIT = 24 * 1024 * 1024
+HBM_RATE = 3_000_000
+
+
+def params():
+    return pltpu.CompilerParams(vmem_limit_bytes=VMEM_LIMIT)
+
+
+def cost(micros):
+    return pl.CostEstimate(flops=0, bytes_accessed=int(micros * HBM_RATE), transcendentals=0)
 
 
 def dot_nt(a, b):
@@ -103,6 +106,7 @@
         out_shape=jax.ShapeDtypeStruct((TOK, WIDTH), BF),
         compiler_params=params(),
         name="spatial_fwd",
+        cost_estimate=cost(4),
     )(q, k, v)
 
 
@@ -133,6 +137,7 @@
         out_shape=[jax.ShapeDtypeStruct((TOK, WIDTH), BF)] * 3,
         compiler_params=params(),
         name="spatial_bwd",
+        cost_estimate=cost(9),
     )(grad_input, whole_out, q, k, v)
 
 
@@ -167,6 +172,7 @@
         out_shape=[jax.ShapeDtypeStruct((TOK, WIDTH), BF)] * 2,
         compiler_params=params(),
         name="out_norm",
+        cost_estimate=cost(4),
     )(mixed, whole_out, inputs, gain)
 
 
@@ -195,6 +201,7 @@
         out_shape=jax.ShapeDtypeStruct((WIDTH, THREE), BF),
         compiler_params=params(),
         name="widen",
+        cost_estimate=cost(1.5),
     )(head_proj)
 
 
@@ -253,6 +260,7 @@
         ],
         compiler_params=params(),
         name="temporal",
+        cost_estimate=cost(9),
     )(order, *proj, grad_heads)
 
 
@@ -281,16 +289,35 @@
         out_shape=jax.ShapeDtypeStruct((WIDTH, 3 * GROUP), BF),
         compiler_params=params(),
         name="qkv_product",
+        cost_estimate=cost(5),
     )(*frames, dproj)
 
 
 SHARE = 12
 SLOT = 16
 FOUR = 4
+EXTRA = 16
+GROUPED = DP * SLOT
+
+
+def mover():
+    shape = (FOUR * SHARE * SEQ, FOUR * SLOT * SEQ)
+    source = lax.broadcasted_iota(jnp.int32, shape, 0)
+    target = lax.broadcasted_iota(jnp.int32, shape, 1)
+    group = target // (FOUR * SLOT)
+    block = (target // SLOT) % FOUR
+    turn = target % SLOT
+    wanted = block * (SHARE * SEQ) + group * SHARE + turn
+    return jnp.where((source == wanted) & (turn < SHARE), 1.0, 0.0).astype(BF)
+
+
+def two_parts(row):
+    high = row.astype(BF)
+    return high, (row - high.astype(F32)).astype(BF)
 
 
 def grad_input_kernel(factor, sum_a, sum_b, sum_c, sum_d, hidden_ref, resid_ref, gain_ref,
-                      out_ref, groups_ref, gain_out_ref):
+                      out_ref, groups_ref):
     def wide(ref):
         return ref[...].astype(F32)
 
@@ -298,25 +325,20 @@
     hidden = wide(hidden_ref)
     inverse = lax.rsqrt(jnp.mean(hidden * hidden, axis=-1, keepdims=True) + EPSILON)
     unit = hidden * inverse
-    gain_out_ref[...] = jnp.sum(dnormed * unit, axis=0, keepdims=True) * factor
+    gain_high, gain_low = two_parts(jnp.sum(dnormed * unit, axis=0, keepdims=True) * factor)
     scaled = dnormed * gain_ref[...]
     through = inverse * (scaled - unit * jnp.mean(scaled * unit, axis=-1, keepdims=True))
     grad = (wide(resid_ref) + through).astype(BF)
     out_ref[...] = grad
-    rows, cols = FOUR * SHARE * SEQ, FOUR * SLOT * SEQ
-    source = lax.broadcasted_iota(jnp.int32, (rows, cols), 0)
-    target = lax.broadcasted_iota(jnp.int32, (rows, cols), 1)
-    group = target // (FOUR * SLOT)
-    block = (target // SLOT) % FOUR
-    turn = target % SLOT
-    wanted = block * (SHARE * SEQ) + group * SHARE + turn
-    move = jnp.where((source == wanted) & (turn < SHARE), 1.0, 0.0).astype(BF)
+    row = lax.broadcasted_iota(jnp.int32, (EXTRA, WIDTH), 0)
+    extra = jnp.where(row == 0, gain_high.astype(F32), jnp.where(row == 1, gain_low.astype(F32), 0.0))
+    both = jnp.concatenate([grad, extra.astype(BF)], axis=0)
+    move = mover()
+    rows, cols = FOUR * SHARE * SEQ, FOUR * SLOT
     for four in range(DP // FOUR):
-        moved = dot_nn(grad[:, four * rows : (four + 1) * rows], move).astype(BF)
+        moved = dot_nn(both[:, four * rows : (four + 1) * rows], move).astype(BF)
         for j in range(SEQ):
-            groups_ref[j, :, four * FOUR * SLOT : (four + 1) * FOUR * SLOT] = moved[
-                :, j * FOUR * SLOT : (j + 1) * FOUR * SLOT
-            ]
+            groups_ref[j, :, four * cols : (four + 1) * cols] = moved[:, j * cols : (j + 1) * cols]
 
 
 def grad_input_call(sums, hidden, resid, gain, factor):
@@ -324,19 +346,29 @@
         functools.partial(grad_input_kernel, factor),
         out_shape=[
             jax.ShapeDtypeStruct((TOK, WIDTH), BF),
-            jax.ShapeDtypeStruct((SEQ, TOK, DP * SLOT), BF),
-            jax.ShapeDtypeStruct((1, WIDTH), F32),
+            jax.ShapeDtypeStruct((SEQ, TOK + EXTRA, GROUPED), BF),
         ],
-        compiler_params=pltpu.CompilerParams(vmem_limit_bytes=VMEM_LIMIT),
+        compiler_params=params(),
         name="grad_input",
+        cost_estimate=cost(2),
     )(*sums, hidden, resid, gain)
 
 
 def out_product_kernel(factor, order_ref, groups_ref, *refs):
     frames, out_ref = refs[:-1], refs[-1]
-    left = jnp.concatenate([groups_ref[order_ref[r]] for r in range(SEQ)], axis=0)
+    cols = out_ref.shape[1]
+    left = jnp.concatenate([groups_ref[order_ref[r], :TOK] for r in range(SEQ)], axis=0)
     right = jnp.concatenate([f[...] for f in frames], axis=0)
-    out_ref[...] = (dot_tn(left, right) * factor).astype(BF)
+    product = dot_tn(left, right) * factor
+    extras = sum(groups_ref[r, TOK:].astype(F32) for r in range(SEQ))
+    high, low = two_parts(extras[0:1] + extras[1:2])
+    filler = jnp.zeros((1, cols - GROUPED), F32)
+    turn = lax.broadcasted_iota(jnp.int32, product.shape, 0) % SLOT
+    first = pl.program_id(0) == 0
+    for place, part in ((SHARE, high), (SHARE + 1, low)):
+        full = jnp.concatenate([part.astype(F32), filler], axis=1)
+        product = jnp.where((turn == place) & first, full, product)
+    out_ref[...] = product.astype(BF)
 
 
 def out_product(order, groups, frames, factor):
@@ -346,14 +378,66 @@
         grid_spec=pltpu.PrefetchScalarGridSpec(
             num_scalar_prefetch=1,
             grid=(WIDTH // cols,),
-            in_specs=[pl.BlockSpec((SEQ, TOK, DP * SLOT), lambda i, o: (0, 0, 0))]
+            in_specs=[pl.BlockSpec((SEQ, TOK + EXTRA, GROUPED), lambda i, o: (0, 0, 0))]
             + [pl.BlockSpec((f.shape[0], cols), lambda i, o: (0, i)) for f in frames],
-            out_specs=pl.BlockSpec((DP * SLOT, cols), lambda i, o: (0, i)),
+            out_specs=pl.BlockSpec((GROUPED, cols), lambda i, o: (0, i)),
         ),
-        out_shape=jax.ShapeDtypeStruct((DP * SLOT, WIDTH), BF),
+        out_shape=jax.ShapeDtypeStruct((GROUPED, WIDTH), BF),
         compiler_params=params(),
         name="out_product",
+        cost_estimate=cost(5),
     )(order, groups, *frames)
+
+
+def fold_kernel(in_ref, out_ref):
+    total = in_ref[0].astype(F32)
+    for d in range(1, DP // 2):
+        total = total + in_ref[d].astype(F32)
+    high, low = two_parts(total[SHARE : SHARE + 1] + total[SHARE + 1 : SHARE + 2])
+    turn = lax.broadcasted_iota(jnp.int32, total.shape, 0)
+    total = jnp.where(turn == SHARE, high.astype(F32), total)
+    total = jnp.where(turn == SHARE + 1, low.astype(F32), total).astype(BF)
+    for j in range(SEQ):
+        out_ref[j] = total
+
+
+def fold(pieces):
+    return pl.pallas_call(
+        fold_kernel,
+        out_shape=jax.ShapeDtypeStruct((SEQ, SLOT, WIDTH), BF),
+        compiler_params=params(),
+        name="fold",
+        cost_estimate=cost(1.5),
+    )(pieces)
+
+
+def finish_kernel(in_ref, out_ref, gain_ref):
+    out_ref[...] = jnp.concatenate(
+        [in_ref[j].astype(F32)[:SHARE] for j in range(SEQ)], axis=0
+    )
+    move = mover()
+    rows, cols = FOUR * SHARE * SEQ, FOUR * SLOT
+    for four in range(DP // FOUR):
+        left = jnp.concatenate(
+            [in_ref[j, :, four * cols : (four + 1) * cols] for j in range(SEQ)], axis=1
+        )
+        back = dot_nt(left, move)
+        gain_ref[:, four * rows : (four + 1) * rows] = (
+            back[SHARE : SHARE + 1] + back[SHARE + 1 : SHARE + 2]
+        )
+
+
+def finish(gathered):
+    return pl.pallas_call(
+        finish_kernel,
+        out_shape=[
+            jax.ShapeDtypeStruct((SEQ * SHARE, WIDTH), F32),
+            jax.ShapeDtypeStruct((1, WIDTH), F32),
+        ],
+        compiler_params=params(),
+        name="finish",
+        cost_estimate=cost(2),
+    )(gathered)
 
 
 def along_x(array, shift):
@@ -396,6 +480,16 @@
     return own, across_y(partner), along_x(behind, -1), along_x(ahead, 1)
 
 
+def dp_pieces(share):
+    blocks = share.reshape(DP // 2, 2, SLOT, WIDTH)
+    core = lax.axis_index("dp") % 2
+    mine = lax.dynamic_index_in_dim(blocks, core, 1, keepdims=False)
+    other = lax.dynamic_index_in_dim(blocks, 1 - core, 1, keepdims=False)
+    got = lax.ppermute(other, "dp", [(i, i ^ 1) for i in range(DP)])
+    groups = [[2 * i + c for i in range(DP // 2)] for c in range(2)]
+    return lax.all_to_all(mine + got, "dp", 0, 0, axis_index_groups=groups, tiled=True)
+
+
 def body(
     inputs, spatial_q, spatial_k, spatial_v, out_weight, norm_gain, qkv_weight, grad_out, grad_resid
 ):
@@ -415,36 +509,40 @@
     whole_out = lax.all_gather(out_weight, "dp", axis=0, tiled=True)
     head_proj = lax.all_gather(qkv_weight, "dp", axis=0, tiled=True)
 
+    mixed = spatial_fwd(q, k, v)
     grad_heads = lax.all_to_all(
         dout.reshape(TOK, SEQ, GROUP).transpose(1, 0, 2), "seq", 0, 0, tiled=True
     )
-    mixed = spatial_fwd(q, k, v)
     mixed_parts = gather_frames(mixed)
+    whole_out, grad_heads, *mixed_parts = lax.optimization_barrier(
+        (whole_out, grad_heads, *mixed_parts)
+    )
     hidden, normed = out_norm(mixed, whole_out, flat_in, gain)
     normed_parts = gather_frames(normed)
+    head_proj, *early = lax.optimization_barrier((head_proj, *normed_parts[:8]))
     wide_proj = widen(head_proj)
-    proj = [dot_nn(f, wide_proj).astype(BF) for f in whole_frames(normed_parts)]
+    proj = [
+        dot_nn(f, wide_proj).astype(BF) for f in whole_frames((*early, *normed_parts[8:]))
+    ]
     heads_out, dproj = temporal(order, proj, grad_heads)
     shares = [dot_nt(dproj[r], wide_proj).astype(BF) for r in range(SEQ)]
+    *shares, dproj, heads_out = lax.optimization_barrier((*shares, dproj, heads_out))
+    qkv_share = qkv_product(normed_parts, dproj, factor)
     sums = scatter_frames(shares)
-    qkv_share = qkv_product(normed_parts, dproj, factor)
+    *sums, qkv_share = lax.optimization_barrier((*sums, qkv_share))
     qkv_grad = lax.psum_scatter(qkv_share, "dp", scatter_dimension=0, tiled=True).astype(F32)
+
+    grad_input, groups = grad_input_call(sums, hidden, resid, gain, factor)
+    groups = lax.all_to_all(groups, "seq", 0, 0, tiled=True)
+    out_share = out_product(order, groups, mixed_parts, factor)
+    pieces = dp_pieces(out_share)
     temporal_out = lax.all_to_all(heads_out, "seq", 0, 0, tiled=True)
     temporal_out = temporal_out.transpose(1, 0, 2).reshape(TOK, WIDTH)
-
-    grad_input, groups, local_gain = grad_input_call(sums, hidden, resid, gain, factor)
-    gain_grad = lax.psum(local_gain.reshape(WIDTH), ("dp", "seq"))
-    groups = lax.all_to_all(groups, "seq", 0, 0, tiled=True)
-    out_share = out_product(order, groups, mixed_parts, factor)
-    out_rows = lax.psum_scatter(out_share, "dp", scatter_dimension=0, tiled=True)
-    out_all = lax.all_to_all(
-        jnp.broadcast_to(out_rows[None], (SEQ, SLOT, WIDTH)), "seq", 0, 0, tiled=True
-    )
-    out_grad = out_all[:, :SHARE].reshape(SEQ * SHARE, WIDTH).astype(F32)
     grad_q, grad_k, grad_v = spatial_bwd(grad_input, whole_out, q, k, v)
+    out_grad, gain_grad = finish(lax.all_to_all(fold(pieces), "seq", 0, 0, tiled=True))
     return tuple(
         a.reshape(block_shape) for a in (hidden, temporal_out, grad_input, grad_q, grad_k, grad_v)
-    ) + (qkv_grad, out_grad, gain_grad)
+    ) + (qkv_grad, out_grad, gain_grad.reshape(WIDTH))
 
 
 def solution(mesh):

time: 363 us -> 243 us (0.67)
  blocking collectives: 80.4 us -> 0 us
  waiting for transfers between devices: 127 us -> 85.9 us
  local copies, waits for them, and re-layouts: 32.8 us -> 25.7 us
  other arithmetic: 1.83 us -> 5.56 us
    psum x1 -> x0, blocking collectives: 64.8 us -> none  [body(): gain_grad = lax.psum(local_gain.reshape(WIDTH), ('dp', 'seq'))]
    reduce_scatter x1 -> x0, waiting for transfers between devices: 33.5 us -> none  [body(): lax.psum_scatter(out_share, 'dp', scatter_dimension=0, tiled=True)]
    all_gather x1, waiting for transfers between devices: 31.7 us -> 0.01 us  [body(): whole_out = lax.all_gather(out_weight, 'dp', axis=0, tiled=True)]
    all_gather x1, waiting for transfers between devices: 27.2 us -> 0.01 us  [body(): head_proj = lax.all_gather(qkv_weight, 'dp', axis=0, tiled=True)]
    ppermute x8, waiting for transfers between devices: 12.9 us -> 34.6 us  [across_y(): return lax.ppermute(array, 'seq', [(i, i ^ 1) for i in range(SEQ)])]
    all_to_all x1 -> x3, waiting for transfers between devices: 0.01 us -> 16.6 us  [the longest x1 8.67 us: body(): temporal_out = lax.all_to_all(heads_out, 'seq', 0, 0, tiled=True)]
    all_to_all x1 -> x0, blocking collectives: 15.7 us -> none  [body(): temporal_out = lax.all_to_all(heads_out, 'seq', 0, 0, tiled=True)]
    all_to_all x1, waiting for transfers between devices: 0.01 us -> 10.1 us  [body(): groups = lax.all_to_all(groups, 'seq', 0, 0, tiled=True)]
  transfers between devices with their start and end apart: 33 -> 35, of which waited for: 15 -> 16; matrix products, arithmetic and copies ran while one was open for 5% -> 7% of each run, Pallas kernels for 6% -> 11%
where the time goes in v2:
time: 243 us; the launch traced here: 241 us
  waiting for transfers between devices  85.9 us (35%)
  starting transfers between devices  61.4 us (25%)
  Pallas kernels  35.4 us (15%)
  local copies, waits for them, and re-layouts  25.7 us (11%)
  between operations  14.3 us (6%)
  matrix products  13 us (5%)
  other arithmetic  5.56 us (2%)
    ppermute x8, waiting for transfers between devices, across_y(): return lax.ppermute(array, 'seq', [(i, i ^ 1) for i in range(SEQ)])  34.6 us
    ppermute x18, starting transfers between devices, along_x(): return lax.ppermute(array, 'seq', pairs)  23 us
    unnamed x70, local copies, waits for them, and re-layouts  18.1 us
    ppermute x18, waiting for transfers between devices, along_x(): return lax.ppermute(array, 'seq', pairs)  17.9 us
    ppermute x8, starting transfers between devices, across_y(): return lax.ppermute(array, 'seq', [(i, i ^ 1) for i in range(SEQ)])  14.5 us
    all_to_all x1, waiting for transfers between devices, body(): groups = lax.all_to_all(groups, 'seq', 0, 0, tiled=True)  10.1 us
    all_to_all x1, waiting for transfers between devices, body(): temporal_out = lax.all_to_all(heads_out, 'seq', 0, 0, tiled=True)  8.67 us
    pallas_call x1, Pallas kernels, temporal(): pl.pallas_call(temporal_kernel, grid_spec=pltpu.PrefetchScalarGridSpec(nu...  8.44 us
  transfers between devices with their start and end apart: 35, of which 16 were waited for; matrix products, arithmetic and copies ran while one was open for 7% of the time, Pallas kernels for 11%

profile of v2, /device:TPU:0, one launch (start us, length us, event | category | flops | bytes accessed | tf_op | source)
XLA Modules:
  0.0 241.1 jit_solution(1299750092195665991)
XLA Ops:
  11.7 2.8 %spatial_fwd.1.mixed_ref.refs_0_ = bf16[128,1536]{1,0:T(8,128)(2,1)S(1)} custom-call(bf16[128,1536]{1,0:T(8,128)(2,1)S(1)} %bitcast.79, bf16[128,1536]{1,0:T(8,128)(2,1)S(1)} %bitcast.81, bf16[128,1536]{1,0:T(8,128)(2,1)S(1)} %bitcast.83), custom_call_target="tpu_custom_call" | custom-call | bytes 12000000 | tf_op jit(solution)/shard_map/spatial_fwd/pallas_call | solution.py:101
  16.1 3.2 %collective-permute-start.4 = (bf16[128,1536]{1,0:T(8,128)(2,1)S(1)}, bf16[128,1536]{1,0:T(8,128)(2,1)S(1)}, u32[]{:S(2)}, u32[]{:S(2)}) collective-permute-start(bf16[128,1536]{1,0:T(8,128)(2,1)S(1)} %spatial_fwd.1.mixed_ref.refs_0_), channel_id=1, source_target_pairs={{0,1},{1,0},{2,3},{3,2},{4,5},{5,4},{6,7},{7,6},{8,9},{9,8},{10,11... | collective-permute-start | bytes 1179656 | tf_op jit(solution)/shard_map/ppermute | solution.py:449
  21.1 5.4 %collective-permute-done.refs_1_ = bf16[128,1536]{1,0:T(8,128)(2,1)S(1)} collective-permute-done((bf16[128,1536]{1,0:T(8,128)(2,1)S(1)}, bf16[128,1536]{1,0:T(8,128)(2,1)S(1)}, u32[]{:S(2)}, u32[]{:S(2)}) %collective-permute-start) | collective-permute-done | bytes 393248 | tf_op jit(solution)/shard_map/ppermute | solution.py:445
  27.1 8.1 %collective-permute-done.4.refs_5_ = bf16[128,1536]{1,0:T(8,128)(2,1)S(1)} collective-permute-done((bf16[128,1536]{1,0:T(8,128)(2,1)S(1)}, bf16[128,1536]{1,0:T(8,128)(2,1)S(1)}, u32[]{:S(2)}, u32[]{:S(2)}) %collective-permute-start.4) | collective-permute-done | bytes 393248 | tf_op jit(solution)/shard_map/ppermute | solution.py:449
  41.7 6.9 %all-to-all-start = ((bf16[8,128,192]{1,2,0:T(8,128)(2,1)}), bf16[8,128,192]{1,2,0:T(8,128)(2,1)}, u32[]{:S(2)}, u32[]{:S(2)}) async-start(bf16[8,128,192]{1,2,0:T(8,128)(2,1)} %copy.24), calls=%async_computation | async-start | bytes 786432 | tf_op jit(solution)/shard_map/all_to_all | solution.py:513
  48.6 3.6 %collective-permute-start.7 = (bf16[64,1536]{1,0:T(8,128)(2,1)S(1)}, bf16[64,1536]{1,0:T(8,128)(2,1)S(1)}, u32[]{:S(2)}, u32[]{:S(2)}) collective-permute-start(bf16[64,1536]{1,0:T(8,128)(2,1)S(1)} %collective-permute-done.2.refs_3_), channel_id=1, source_target_pairs={{0,1},{1,0},{2,3},{3,2},{4,5},{5,4},{6,7},{7,6},{8,9},{9,8},{10,11... | collective-permute-start | bytes 589832 | tf_op jit(solution)/shard_map/ppermute | solution.py:449
  54.0 3.6 %all-to-all-done = bf16[8,128,192]{1,2,0:T(8,128)(2,1)} async-done(((bf16[8,128,192]{1,2,0:T(8,128)(2,1)}), bf16[8,128,192]{1,2,0:T(8,128)(2,1)}, u32[]{:S(2)}, u32[]{:S(2)}) %all-to-all-start) | async-done | bytes 393248 | tf_op jit(solution)/shard_map/all_to_all | solution.py:513
  58.4 4.6 %collective-permute-done.7.refs_8_ = bf16[64,1536]{1,0:T(8,128)(2,1)S(1)} collective-permute-done((bf16[64,1536]{1,0:T(8,128)(2,1)S(1)}, bf16[64,1536]{1,0:T(8,128)(2,1)S(1)}, u32[]{:S(2)}, u32[]{:S(2)}) %collective-permute-start.7) | collective-permute-done | bytes 196640 | tf_op jit(solution)/shard_map/ppermute | solution.py:449
  63.0 2.6 %collective-permute-done.8.refs_9_ = bf16[64,1536]{1,0:T(8,128)(2,1)S(1)} collective-permute-done((bf16[64,1536]{1,0:T(8,128)(2,1)S(1)}, bf16[64,1536]{1,0:T(8,128)(2,1)S(1)}, u32[]{:S(2)}, u32[]{:S(2)}) %collective-permute-start.8) | collective-permute-done | bytes 196640 | tf_op jit(solution)/shard_map/ppermute | solution.py:449
  65.6 2.4 copy-done
  68.0 2.9 %out_norm.1 = (bf16[128,1536]{1,0:T(8,128)(2,1)}, bf16[128,1536]{1,0:T(8,128)(2,1)S(1)}) custom-call(bf16[128,1536]{1,0:T(8,128)(2,1)S(1)} %spatial_fwd.1.mixed_ref.refs_0_, bf16[1536,1536]{1,0:T(8,128)(2,1)S(1)} %copy-done, bf16[128,1536]{1,0:T(8,128)(2,1)S(1)} %bitcast.85, f32[1,1536]{1,0:T(1,128)S(1)} %reshape.61.gain_ref), custom_call_target="tpu_custom_call" | custom-call | bytes 12000000 | tf_op jit(solution)/shard_map/out_norm/pallas_call | solution.py:162
  71.7 2.5 %collective-permute-start.10 = (bf16[128,1536]{1,0:T(8,128)(2,1)S(1)}, bf16[128,1536]{1,0:T(8,128)(2,1)S(1)}, u32[]{:S(2)}, u32[]{:S(2)}) collective-permute-start(bf16[128,1536]{1,0:T(8,128)(2,1)S(1)} %get-tuple-element.59.refs_0_), channel_id=1, source_target_pairs={{0,6},{1,7},{2,0},{3,1},{4,2},{5,3},{6,4},{7,5},{8,14},{9,15},{10,... | collective-permute-start | bytes 1179656 | tf_op jit(solution)/shard_map/ppermute | solution.py:445
  74.2 14.1 %collective-permute-done.13.refs_5_ = bf16[128,1536]{1,0:T(8,128)(2,1)S(1)} collective-permute-done((bf16[128,1536]{1,0:T(8,128)(2,1)S(1)}, bf16[128,1536]{1,0:T(8,128)(2,1)S(1)}, u32[]{:S(2)}, u32[]{:S(2)}) %collective-permute-start.13) | collective-permute-done | bytes 393248 | tf_op jit(solution)/shard_map/ppermute | solution.py:449
  96.2 6.4 %collective-permute-done.12.refs_4_ = bf16[64,1536]{1,0:T(8,128)(2,1)S(1)} collective-permute-done((bf16[64,1536]{1,0:T(8,128)(2,1)}, bf16[64,1536]{1,0:T(8,128)(2,1)S(1)}, u32[]{:S(2)}, u32[]{:S(2)}) %collective-permute-start.12) | collective-permute-done | bytes 196640 | tf_op jit(solution)/shard_map/ppermute | solution.py:445
  103.3 2.8 %collective-permute-start.16 = (bf16[64,1536]{1,0:T(8,128)(2,1)}, bf16[64,1536]{1,0:T(8,128)(2,1)}, u32[]{:S(2)}, u32[]{:S(2)}) collective-permute-start(bf16[64,1536]{1,0:T(8,128)(2,1)} %collective-permute-done.11.refs_3_), channel_id=1, source_target_pairs={{0,1},{1,0},{2,3},{3,2},{4,5},{5,4},{6,7},{7,6},{8,9},{9,8},{10,11... | collective-permute-start | bytes 589832 | tf_op jit(solution)/shard_map/ppermute | solution.py:449
  114.3 8.4 %temporal.1 = (bf16[8,128,192]{2,1,0:T(8,128)(2,1)S(1)}, bf16[8,128,768]{2,1,0:T(8,128)(2,1)S(1)}) custom-call(s32[8]{0:T(128)S(1)} %stack.35.order_ref, bf16[128,768]{1,0:T(8,128)(2,1)S(1)} %convolution_convert_fusion.15.refs_0_, bf16[128,768]{1,0:T(8,128)(2,1)S(1)} %convolution_convert_fusion.14.refs_1_, ...), custom_call_target="tpu_custom_call" | custom-call | bytes 27000000 | tf_op jit(solution)/shard_map/temporal/pallas_call | solution.py:249
  132.0 2.1 collective-permute-start.18
  134.1 5.2 %collective-permute-done.21 = bf16[128,1536]{1,0:T(8,128)(2,1)S(1)} collective-permute-done((bf16[128,1536]{1,0:T(8,128)(2,1)S(1)}, bf16[128,1536]{1,0:T(8,128)(2,1)S(1)}, u32[]{:S(2)}, u32[]{:S(2)}) %collective-permute-start.21) | collective-permute-done | bytes 393248 | tf_op jit(solution)/shard_map/ppermute | solution.py:449
  139.5 2.8 %collective-permute-start.22 = (bf16[64,1536]{1,0:T(8,128)(2,1)S(1)}, bf16[64,1536]{1,0:T(8,128)(2,1)S(1)}, u32[]{:S(2)}, u32[]{:S(2)}) collective-permute-start(bf16[64,1536]{1,0:T(8,128)(2,1)S(1)} %get-tuple-element.106), channel_id=1, source_target_pairs={{0,6},{1,7},{2,0},{3,1},{4,2},{5,3},{6,4},{7,5},{8,14},{9,15},{10,... | collective-permute-start | bytes 589832 | tf_op jit(solution)/shard_map/ppermute | solution.py:445
  145.5 3.7 %collective-permute-done.24 = bf16[64,1536]{1,0:T(8,128)(2,1)S(1)} collective-permute-done((bf16[64,1536]{1,0:T(8,128)(2,1)S(1)}, bf16[64,1536]{1,0:T(8,128)(2,1)S(1)}, u32[]{:S(2)}, u32[]{:S(2)}) %collective-permute-start.24) | collective-permute-done | bytes 196640 | tf_op jit(solution)/shard_map/ppermute | solution.py:445
  152.8 5.2 %qkv_product.1 = bf16[1536,576]{1,0:T(8,128)(2,1)} custom-call(bf16[128,1536]{1,0:T(8,128)(2,1)S(1)} %get-tuple-element.59.refs_0_, bf16[128,1536]{1,0:T(8,128)(2,1)S(1)} %collective-permute-done.9.refs_1_, bf16[128,1536]{1,0:T(8,128)(2,1)S(1)} %collective-permute-done.10.refs_2_, bf16[64,1536]{1,0:T(8,128)(2,1)} %collective-permute-done.11.refs_3_, ...), custom_call_target="tpu_custom_call" | custom-call | bytes 15000000 | tf_op jit(solution)/shard_map/qkv_product/pallas_call | solution.py:283
  162.1 3.3 %grad_input.1 = (bf16[128,1536]{1,0:T(8,128)(2,1)}, bf16[8,144,256]{2,1,0:T(8,128)(2,1)}) custom-call(bf16[128,1536]{1,0:T(8,128)(2,1)S(1)} %convolution_convert_fusion.7.sum_a, bf16[128,1536]{1,0:T(8,128)(2,1)} %collective-permute-done.20.sum_b, bf16[128,1536]{1,0:T(8,128)(2,1)} %collective-permute-done.23.sum_c, ...), custom_call_target="tpu_custom_call" | custom-call | bytes 6000000 | tf_op jit(solution)/shard_map/grad_input/pallas_call | solution.py:345
  165.4 3.6 %all-to-all-start.2 = ((bf16[8,144,256]{2,1,0:T(8,128)(2,1)}), bf16[8,144,256]{2,1,0:T(8,128)(2,1)S(1)}, u32[]{:S(2)}, u32[]{:S(2)}) async-start(bf16[8,144,256]{2,1,0:T(8,128)(2,1)} %get-tuple-element.90), calls=%async_computation.3 | async-start | bytes 1179648 | tf_op jit(solution)/shard_map/all_to_all | solution.py:536
  169.0 10.1 %all-to-all-done.2.groups_ref = bf16[8,144,256]{2,1,0:T(8,128)(2,1)S(1)} async-done(((bf16[8,144,256]{2,1,0:T(8,128)(2,1)}), bf16[8,144,256]{2,1,0:T(8,128)(2,1)S(1)}, u32[]{:S(2)}, u32[]{:S(2)}) %all-to-all-start.2) | async-done | bytes 589856 | tf_op jit(solution)/shard_map/all_to_all | solution.py:536
  182.9 2.3 out_product.1
  187.9 5.7 %all-to-all-start.3 = ((bf16[8,16,1536]{2,1,0:T(8,128)(2,1)}), bf16[8,16,1536]{2,1,0:T(8,128)(2,1)S(1)}, u32[]{:S(2)}, u32[]{:S(2)}) async-start(bf16[8,16,1536]{2,1,0:T(8,128)(2,1)} %bitcast_add_fusion), calls=%async_computation.4 | async-start | bytes 786432 | tf_op jit(solution)/shard_map/all_to_all | solution.py:490
  194.6 7.9 %all-to-all-done.3.in_ref = bf16[8,16,1536]{2,1,0:T(8,128)(2,1)S(1)} async-done(((bf16[8,16,1536]{2,1,0:T(8,128)(2,1)}), bf16[8,16,1536]{2,1,0:T(8,128)(2,1)S(1)}, u32[]{:S(2)}, u32[]{:S(2)}) %all-to-all-start.3) | async-done | bytes 393248 | tf_op jit(solution)/shard_map/all_to_all | solution.py:490
  202.5 4.1 %all-to-all-start.1 = ((bf16[8,128,192]{1,2,0:T(8,128)(2,1)}), bf16[8,128,192]{1,2,0:T(8,128)(2,1)S(1)}, u32[]{:S(2)}, u32[]{:S(2)}) async-start(bf16[8,128,192]{1,2,0:T(8,128)(2,1)} %copy.26), calls=%async_computation.1 | async-start | bytes 786432 | tf_op jit(solution)/shard_map/all_to_all | solution.py:539
  207.4 8.7 %all-to-all-done.1 = bf16[8,128,192]{1,2,0:T(8,128)(2,1)S(1)} async-done(((bf16[8,128,192]{1,2,0:T(8,128)(2,1)}), bf16[8,128,192]{1,2,0:T(8,128)(2,1)S(1)}, u32[]{:S(2)}, u32[]{:S(2)}) %all-to-all-start.1) | async-done | bytes 393248 | tf_op jit(solution)/shard_map/all_to_all | solution.py:539
  216.1 3.5 %all-to-all-start.4 = ((bf16[8,16,1536]{2,1,0:T(8,128)(2,1)}), bf16[8,16,1536]{2,1,0:T(8,128)(2,1)S(1)}, u32[]{:S(2)}, u32[]{:S(2)}) async-start(bf16[8,16,1536]{2,1,0:T(8,128)(2,1)} %fold.1), calls=%async_computation.5 | async-start | bytes 786432 | tf_op jit(solution)/shard_map/all_to_all | solution.py:542
  221.2 2.3 copy-done.1
  223.5 7.5 %spatial_bwd.1 = (bf16[128,1536]{1,0:T(8,128)(2,1)}, bf16[128,1536]{1,0:T(8,128)(2,1)}, bf16[128,1536]{1,0:T(8,128)(2,1)}) custom-call(bf16[128,1536]{1,0:T(8,128)(2,1)S(1)} %copy-done.22, bf16[1536,1536]{1,0:T(8,128)(2,1)S(1)} %copy-done.1, bf16[128,1536]{1,0:T(8,128)(2,1)S(1)} %bitcast.80, bf16[128,1536]{1,0:T(8,128)(2,1)S(1)} %bitcast.82, ...), custom_call_target="tpu_custom_call" | custom-call | bytes 27000000 | tf_op jit(solution)/shard_map/spatial_bwd/pallas_call | solution.py:128
  (159 shorter events, 68.5 us)
Async XLA Ops:
  7.2 58.4 %all-gather.3.cloned.1.call-start = ((), (), s32[]{:S(2)}) async-start(), calls=%async_computation.6 | async-start | bytes 5013504 | tf_op jit(solution)/shard_map/all_gather | solution.py:509
  7.9 98.2 %all-gather.5.cloned.1.call-start = ((), (), s32[]{:S(2)}) async-start(), calls=%async_computation.7 | async-start | bytes 2088960 | tf_op jit(solution)/shard_map/all_gather | solution.py:510
  14.5 12.0 %collective-permute-start = (bf16[128,1536]{1,0:T(8,128)(2,1)S(1)}, bf16[128,1536]{1,0:T(8,128)(2,1)S(1)}, u32[]{:S(2)}, u32[]{:S(2)}) collective-permute-start(bf16[128,1536]{1,0:T(8,128)(2,1)S(1)} %spatial_fwd.1.mixed_ref.refs_0_), channel_id=1, source_target_pairs={{0,2},{1,3},{2,4},{3,5},{4,6},{5,7},{6,0},{7,1},{8,10},{9,11},{10,... | collective-permute-start | bytes 1179656 | tf_op jit(solution)/shard_map/ppermute | solution.py:445
  16.1 19.1 %collective-permute-start.4 = (bf16[128,1536]{1,0:T(8,128)(2,1)S(1)}, bf16[128,1536]{1,0:T(8,128)(2,1)S(1)}, u32[]{:S(2)}, u32[]{:S(2)}) collective-permute-start(bf16[128,1536]{1,0:T(8,128)(2,1)S(1)} %spatial_fwd.1.mixed_ref.refs_0_), channel_id=1, source_target_pairs={{0,1},{1,0},{2,3},{3,2},{4,5},{5,4},{6,7},{7,6},{8,9},{9,8},{10,11... | collective-permute-start | bytes 1179656 | tf_op jit(solution)/shard_map/ppermute | solution.py:449
  19.3 19.9 %collective-permute-start.1 = (bf16[128,1536]{1,0:T(8,128)(2,1)S(1)}, bf16[128,1536]{1,0:T(8,128)(2,1)S(1)}, u32[]{:S(2)}, u32[]{:S(2)}) collective-permute-start(bf16[128,1536]{1,0:T(8,128)(2,1)S(1)} %spatial_fwd.1.mixed_ref.refs_0_), channel_id=1, source_target_pairs={{0,6},{1,7},{2,0},{3,1},{4,2},{5,3},{6,4},{7,5},{8,14},{9,15},{10,... | collective-permute-start | bytes 1179656 | tf_op jit(solution)/shard_map/ppermute | solution.py:445
  26.5 22.1 %collective-permute-start.2 = (bf16[64,1536]{1,0:T(8,128)(2,1)S(1)}, bf16[64,1536]{1,0:T(8,128)(2,1)S(1)}, u32[]{:S(2)}, u32[]{:S(2)}) collective-permute-start(bf16[64,1536]{1,0:T(8,128)(2,1)S(1)} %slice.72), channel_id=1, source_target_pairs={{0,2},{1,3},{2,4},{3,5},{4,6},{5,7},{6,0},{7,1},{8,10},{9,11},{10,... | collective-permute-start | bytes 589832 | tf_op jit(solution)/shard_map/ppermute | solution.py:445
  35.2 22.4 %collective-permute-start.5 = (bf16[128,1536]{1,0:T(8,128)(2,1)S(1)}, bf16[128,1536]{1,0:T(8,128)(2,1)S(1)}, u32[]{:S(2)}, u32[]{:S(2)}) collective-permute-start(bf16[128,1536]{1,0:T(8,128)(2,1)S(1)} %collective-permute-done.4.refs_5_), channel_id=1, source_target_pairs={{0,2},{1,3},{2,4},{3,5},{4,6},{5,7},{6,0},{7,1},{8,10},{9,11},{10,... | collective-permute-start | bytes 1179656 | tf_op jit(solution)/shard_map/ppermute | solution.py:445
  36.6 21.1 %collective-permute-start.6 = (bf16[128,1536]{1,0:T(8,128)(2,1)S(1)}, bf16[128,1536]{1,0:T(8,128)(2,1)S(1)}, u32[]{:S(2)}, u32[]{:S(2)}) collective-permute-start(bf16[128,1536]{1,0:T(8,128)(2,1)S(1)} %collective-permute-done.4.refs_5_), channel_id=1, source_target_pairs={{0,6},{1,7},{2,0},{3,1},{4,2},{5,3},{6,4},{7,5},{8,14},{9,15},{10,... | collective-permute-start | bytes 1179656 | tf_op jit(solution)/shard_map/ppermute | solution.py:445
  40.1 12.7 %collective-permute-start.3 = (bf16[64,1536]{1,0:T(8,128)(2,1)}, bf16[64,1536]{1,0:T(8,128)(2,1)S(1)}, u32[]{:S(2)}, u32[]{:S(2)}) collective-permute-start(bf16[64,1536]{1,0:T(8,128)(2,1)} %slice.73), channel_id=1, source_target_pairs={{0,6},{1,7},{2,0},{3,1},{4,2},{5,3},{6,4},{7,5},{8,14},{9,15},{10,... | collective-permute-start | bytes 589832 | tf_op jit(solution)/shard_map/ppermute | solution.py:445
  41.7 15.9 %all-to-all-start = ((bf16[8,128,192]{1,2,0:T(8,128)(2,1)}), bf16[8,128,192]{1,2,0:T(8,128)(2,1)}, u32[]{:S(2)}, u32[]{:S(2)}) async-start(bf16[8,128,192]{1,2,0:T(8,128)(2,1)} %copy.24), calls=%async_computation | async-start | bytes 786432 | tf_op jit(solution)/shard_map/all_to_all | solution.py:513
  48.6 184.4 %reduce-scatter.2.cloned.1.call-start = ((), (), s32[]{:S(2)}) async-start(), calls=%async_computation.8 | async-start | bytes 2088960 | tf_op jit(solution)/shard_map/reduce_scatter | solution.py:533
  48.6 14.4 %collective-permute-start.7 = (bf16[64,1536]{1,0:T(8,128)(2,1)S(1)}, bf16[64,1536]{1,0:T(8,128)(2,1)S(1)}, u32[]{:S(2)}, u32[]{:S(2)}) collective-permute-start(bf16[64,1536]{1,0:T(8,128)(2,1)S(1)} %collective-permute-done.2.refs_3_), channel_id=1, source_target_pairs={{0,1},{1,0},{2,3},{3,2},{4,5},{5,4},{6,7},{7,6},{8,9},{9,8},{10,11... | collective-permute-start | bytes 589832 | tf_op jit(solution)/shard_map/ppermute | solution.py:449
  52.8 12.8 %collective-permute-start.8 = (bf16[64,1536]{1,0:T(8,128)(2,1)S(1)}, bf16[64,1536]{1,0:T(8,128)(2,1)S(1)}, u32[]{:S(2)}, u32[]{:S(2)}) collective-permute-start(bf16[64,1536]{1,0:T(8,128)(2,1)S(1)} %collective-permute-done.3.refs_4_), channel_id=1, source_target_pairs={{0,1},{1,0},{2,3},{3,2},{4,5},{5,4},{6,7},{7,6},{8,9},{9,8},{10,11... | collective-permute-start | bytes 589832 | tf_op jit(solution)/shard_map/ppermute | solution.py:449
  71.0 17.3 %collective-permute-start.13 = (bf16[128,1536]{1,0:T(8,128)(2,1)S(1)}, bf16[128,1536]{1,0:T(8,128)(2,1)S(1)}, u32[]{:S(2)}, u32[]{:S(2)}) collective-permute-start(bf16[128,1536]{1,0:T(8,128)(2,1)S(1)} %get-tuple-element.59.refs_0_), channel_id=1, source_target_pairs={{0,1},{1,0},{2,3},{3,2},{4,5},{5,4},{6,7},{7,6},{8,9},{9,8},{10,11... | collective-permute-start | bytes 1179656 | tf_op jit(solution)/shard_map/ppermute | solution.py:449
  71.7 19.9 %collective-permute-start.10 = (bf16[128,1536]{1,0:T(8,128)(2,1)S(1)}, bf16[128,1536]{1,0:T(8,128)(2,1)S(1)}, u32[]{:S(2)}, u32[]{:S(2)}) collective-permute-start(bf16[128,1536]{1,0:T(8,128)(2,1)S(1)} %get-tuple-element.59.refs_0_), channel_id=1, source_target_pairs={{0,6},{1,7},{2,0},{3,1},{4,2},{5,3},{6,4},{7,5},{8,14},{9,15},{10,... | collective-permute-start | bytes 1179656 | tf_op jit(solution)/shard_map/ppermute | solution.py:445
  74.2 18.3 %collective-permute-start.9 = (bf16[128,1536]{1,0:T(8,128)(2,1)S(1)}, bf16[128,1536]{1,0:T(8,128)(2,1)S(1)}, u32[]{:S(2)}, u32[]{:S(2)}) collective-permute-start(bf16[128,1536]{1,0:T(8,128)(2,1)S(1)} %get-tuple-element.59.refs_0_), channel_id=1, source_target_pairs={{0,2},{1,3},{2,4},{3,5},{4,6},{5,7},{6,0},{7,1},{8,10},{9,11},{10,... | collective-permute-start | bytes 1179656 | tf_op jit(solution)/shard_map/ppermute | solution.py:445
  88.3 17.9 %collective-permute-start.14 = (bf16[128,1536]{1,0:T(8,128)(2,1)S(1)}, bf16[128,1536]{1,0:T(8,128)(2,1)S(1)}, u32[]{:S(2)}, u32[]{:S(2)}) collective-permute-start(bf16[128,1536]{1,0:T(8,128)(2,1)S(1)} %collective-permute-done.13.refs_5_), channel_id=1, source_target_pairs={{0,2},{1,3},{2,4},{3,5},{4,6},{5,7},{6,0},{7,1},{8,10},{9,11},{10,... | collective-permute-start | bytes 1179656 | tf_op jit(solution)/shard_map/ppermute | solution.py:445
  89.9 16.3 %collective-permute-start.15 = (bf16[128,1536]{1,0:T(8,128)(2,1)S(1)}, bf16[128,1536]{1,0:T(8,128)(2,1)S(1)}, u32[]{:S(2)}, u32[]{:S(2)}) collective-permute-start(bf16[128,1536]{1,0:T(8,128)(2,1)S(1)} %collective-permute-done.13.refs_5_), channel_id=1, source_target_pairs={{0,6},{1,7},{2,0},{3,1},{4,2},{5,3},{6,4},{7,5},{8,14},{9,15},{10,... | collective-permute-start | bytes 1179656 | tf_op jit(solution)/shard_map/ppermute | solution.py:445
  92.2 10.4 %collective-permute-start.12 = (bf16[64,1536]{1,0:T(8,128)(2,1)}, bf16[64,1536]{1,0:T(8,128)(2,1)S(1)}, u32[]{:S(2)}, u32[]{:S(2)}) collective-permute-start(bf16[64,1536]{1,0:T(8,128)(2,1)} %slice.75), channel_id=1, source_target_pairs={{0,6},{1,7},{2,0},{3,1},{4,2},{5,3},{6,4},{7,5},{8,14},{9,15},{10,... | collective-permute-start | bytes 589832 | tf_op jit(solution)/shard_map/ppermute | solution.py:445
  93.2 10.1 %collective-permute-start.11 = (bf16[64,1536]{1,0:T(8,128)(2,1)}, bf16[64,1536]{1,0:T(8,128)(2,1)}, u32[]{:S(2)}, u32[]{:S(2)}) collective-permute-start(bf16[64,1536]{1,0:T(8,128)(2,1)} %slice.74), channel_id=1, source_target_pairs={{0,2},{1,3},{2,4},{3,5},{4,6},{5,7},{6,0},{7,1},{8,10},{9,11},{10,... | collective-permute-start | bytes 589832 | tf_op jit(solution)/shard_map/ppermute | solution.py:445
  102.6 10.1 %collective-permute-start.17 = (bf16[64,1536]{1,0:T(8,128)(2,1)S(1)}, bf16[64,1536]{1,0:T(8,128)(2,1)}, u32[]{:S(2)}, u32[]{:S(2)}) collective-permute-start(bf16[64,1536]{1,0:T(8,128)(2,1)S(1)} %collective-permute-done.12.refs_4_), channel_id=1, source_target_pairs={{0,1},{1,0},{2,3},{3,2},{4,5},{5,4},{6,7},{7,6},{8,9},{9,8},{10,11... | collective-permute-start | bytes 589832 | tf_op jit(solution)/shard_map/ppermute | solution.py:449
  103.3 9.5 %collective-permute-start.16 = (bf16[64,1536]{1,0:T(8,128)(2,1)}, bf16[64,1536]{1,0:T(8,128)(2,1)}, u32[]{:S(2)}, u32[]{:S(2)}) collective-permute-start(bf16[64,1536]{1,0:T(8,128)(2,1)} %collective-permute-done.11.refs_3_), channel_id=1, source_target_pairs={{0,1},{1,0},{2,3},{3,2},{4,5},{5,4},{6,7},{7,6},{8,9},{9,8},{10,11... | collective-permute-start | bytes 589832 | tf_op jit(solution)/shard_map/ppermute | solution.py:449
  130.0 9.4 %collective-permute-start.21 = (bf16[128,1536]{1,0:T(8,128)(2,1)S(1)}, bf16[128,1536]{1,0:T(8,128)(2,1)S(1)}, u32[]{:S(2)}, u32[]{:S(2)}) collective-permute-start(bf16[128,1536]{1,0:T(8,128)(2,1)S(1)} %convolution_convert_fusion), channel_id=1, source_target_pairs={{0,1},{1,0},{2,3},{3,2},{4,5},{5,4},{6,7},{7,6},{8,9},{9,8},{10,11... | collective-permute-start | bytes 1179656 | tf_op jit(solution)/shard_map/ppermute | solution.py:449
  130.9 11.4 %collective-permute-start.19 = (bf16[128,1536]{1,0:T(8,128)(2,1)S(1)}, bf16[128,1536]{1,0:T(8,128)(2,1)S(1)}, u32[]{:S(2)}, u32[]{:S(2)}) collective-permute-start(bf16[128,1536]{1,0:T(8,128)(2,1)S(1)} %convolution_convert_fusion.1), channel_id=1, source_target_pairs={{0,2},{1,3},{2,4},{3,5},{4,6},{5,7},{6,0},{7,1},{8,10},{9,11},{10,... | collective-permute-start | bytes 1179656 | tf_op jit(solution)/shard_map/ppermute | solution.py:445
  132.0 10.3 %collective-permute-start.18 = (bf16[128,1536]{1,0:T(8,128)(2,1)S(1)}, bf16[128,1536]{1,0:T(8,128)(2,1)S(1)}, u32[]{:S(2)}, u32[]{:S(2)}) collective-permute-start(bf16[128,1536]{1,0:T(8,128)(2,1)S(1)} %convolution_convert_fusion.2), channel_id=1, source_target_pairs={{0,6},{1,7},{2,0},{3,1},{4,2},{5,3},{6,4},{7,5},{8,14},{9,15},{10,... | collective-permute-start | bytes 1179656 | tf_op jit(solution)/shard_map/ppermute | solution.py:445
  143.1 14.9 %collective-permute-start.20 = (bf16[128,1536]{1,0:T(8,128)(2,1)}, bf16[128,1536]{1,0:T(8,128)(2,1)}, u32[]{:S(2)}, u32[]{:S(2)}) collective-permute-start(bf16[128,1536]{1,0:T(8,128)(2,1)} %add_add_fusion), channel_id=1, source_target_pairs={{0,1},{1,0},{2,3},{3,2},{4,5},{5,4},{6,7},{7,6},{8,9},{9,8},{10,11... | collective-permute-start | bytes 1179656 | tf_op jit(solution)/shard_map/ppermute | solution.py:449
  150.0 8.1 %collective-permute-start.23 = (bf16[128,1536]{1,0:T(8,128)(2,1)}, bf16[128,1536]{1,0:T(8,128)(2,1)}, u32[]{:S(2)}, u32[]{:S(2)}) collective-permute-start(bf16[128,1536]{1,0:T(8,128)(2,1)} %pad_maximum_fusion), channel_id=1, source_target_pairs={{0,6},{1,7},{2,0},{3,1},{4,2},{5,3},{6,4},{7,5},{8,14},{9,15},{10,... | collective-permute-start | bytes 1179656 | tf_op jit(solution)/shard_map/ppermute | solution.py:445
  150.8 9.3 %collective-permute-start.25 = (bf16[128,1536]{1,0:T(8,128)(2,1)}, bf16[128,1536]{1,0:T(8,128)(2,1)}, u32[]{:S(2)}, u32[]{:S(2)}) collective-permute-start(bf16[128,1536]{1,0:T(8,128)(2,1)} %pad_maximum_fusion.1), channel_id=1, source_target_pairs={{0,2},{1,3},{2,4},{3,5},{4,6},{5,7},{6,0},{7,1},{8,10},{9,11},{10,... | collective-permute-start | bytes 1179656 | tf_op jit(solution)/shard_map/ppermute | solution.py:445
  165.4 13.7 %all-to-all-start.2 = ((bf16[8,144,256]{2,1,0:T(8,128)(2,1)}), bf16[8,144,256]{2,1,0:T(8,128)(2,1)S(1)}, u32[]{:S(2)}, u32[]{:S(2)}) async-start(bf16[8,144,256]{2,1,0:T(8,128)(2,1)} %get-tuple-element.90), calls=%async_computation.3 | async-start | bytes 1179648 | tf_op jit(solution)/shard_map/all_to_all | solution.py:536
  187.9 14.6 %all-to-all-start.3 = ((bf16[8,16,1536]{2,1,0:T(8,128)(2,1)}), bf16[8,16,1536]{2,1,0:T(8,128)(2,1)S(1)}, u32[]{:S(2)}, u32[]{:S(2)}) async-start(bf16[8,16,1536]{2,1,0:T(8,128)(2,1)} %bitcast_add_fusion), calls=%async_computation.4 | async-start | bytes 786432 | tf_op jit(solution)/shard_map/all_to_all | solution.py:490
  202.5 13.6 %all-to-all-start.1 = ((bf16[8,128,192]{1,2,0:T(8,128)(2,1)}), bf16[8,128,192]{1,2,0:T(8,128)(2,1)S(1)}, u32[]{:S(2)}, u32[]{:S(2)}) async-start(bf16[8,128,192]{1,2,0:T(8,128)(2,1)} %copy.26), calls=%async_computation.1 | async-start | bytes 786432 | tf_op jit(solution)/shard_map/all_to_all | solution.py:539
  216.1 14.9 %all-to-all-start.4 = ((bf16[8,16,1536]{2,1,0:T(8,128)(2,1)}), bf16[8,16,1536]{2,1,0:T(8,128)(2,1)S(1)}, u32[]{:S(2)}, u32[]{:S(2)}) async-start(bf16[8,16,1536]{2,1,0:T(8,128)(2,1)} %fold.1), calls=%async_computation.5 | async-start | bytes 786432 | tf_op jit(solution)/shard_map/all_to_all | solution.py:542
  (38 other events, 427.9 us)
Sparse Core Ops, SparseCore 0:
  9.7 52.0 all-gather.2
  63.6 32.8 all-gather.4
  160.3 67.2 reduce-scatter.1

commit v3 on v2

--- a/solution.py
+++ b/solution.py
@@ -20,12 +20,12 @@
 BF = jnp.bfloat16
 F32 = jnp.float32
 SCALE = HDIM**-0.5
-VMEM_LIMIT = 24 * 1024 * 1024
+VMEM_LIMIT = 20 * 1024 * 1024
 HBM_RATE = 3_000_000
 
 
-def params():
-    return pltpu.CompilerParams(vmem_limit_bytes=VMEM_LIMIT)
+def params(limit=VMEM_LIMIT):
+    return pltpu.CompilerParams(vmem_limit_bytes=limit)
 
 
 def cost(micros):
@@ -191,68 +191,74 @@
         out_ref[:, j * PADDED + GROUP : (j + 1) * PADDED] = jnp.zeros((rows, PADDED - GROUP), BF)
 
 
-def widen(head_proj):
+def widen(weights):
     rows = 768
     return pl.pallas_call(
         widen_kernel,
         grid=(WIDTH // rows,),
-        in_specs=[pl.BlockSpec((rows, 3 * GROUP), lambda i: (i, 0))],
+        in_specs=[pl.BlockSpec((rows, THREE), lambda i: (i, WIDTH // THREE))],
         out_specs=pl.BlockSpec((rows, THREE), lambda i: (i, 0)),
         out_shape=jax.ShapeDtypeStruct((WIDTH, THREE), BF),
         compiler_params=params(),
         name="widen",
         cost_estimate=cost(1.5),
-    )(head_proj)
+    )(weights)
 
 
 POS = 16
+CHAINS = 4
+
+
+def temporal_block(q, keys, values, dout, valid):
+    keys, values = spread(keys, 3), spread(values, 3)
+    probs = soft(dot_nt(q, keys), 3, valid)
+    prob_round = rounded(probs)
+    dscores = score_grad(probs, dot_nt(dout, values))
+    return dot_nn(prob_round, values).astype(BF), (
+        dot_nn(dscores, keys).astype(BF),
+        pick(dot_tn(dscores, q), 3).astype(BF),
+        pick(dot_tn(prob_round, dout), 3).astype(BF),
+    )
 
 
 def temporal_kernel(order_ref, *refs):
     proj, (grad_ref, out_ref, dproj_ref) = refs[:SEQ], refs[SEQ:]
-
-    def rows(j):
-        return jnp.concatenate(
-            [p[:, j * PADDED : j * PADDED + GROUP] for p in proj], axis=0
-        )
-
-    q = rows(0)
-    keys, values = spread(rows(1), 3), spread(rows(2), 3)
-    dout = jnp.concatenate([grad_ref[order_ref[r]] for r in range(SEQ)], axis=0)
     shape = (SEQ * POS, SEQ * POS)
     valid = (
         lax.broadcasted_iota(jnp.int32, shape, 0) % POS
         == lax.broadcasted_iota(jnp.int32, shape, 1) % POS
     )
-    probs = soft(dot_nt(q, keys), 3, valid)
-    prob_round = rounded(probs)
-    heads_out = dot_nn(prob_round, values).astype(BF)
-    dscores = score_grad(probs, dot_nt(dout, values))
-    grads = (
-        dot_nn(dscores, keys).astype(BF),
-        pick(dot_tn(dscores, q), 3).astype(BF),
-        pick(dot_tn(prob_round, dout), 3).astype(BF),
-    )
-    for r in range(SEQ):
-        here = slice(r * POS, (r + 1) * POS)
-        out_ref[order_ref[r]] = heads_out[here]
-        for j in range(3):
-            dproj_ref[r, :, j * PADDED : j * PADDED + GROUP] = grads[j][here]
-            dproj_ref[r, :, j * PADDED + GROUP : (j + 1) * PADDED] = jnp.zeros(
-                (POS, PADDED - GROUP), BF
+    for chain in range(CHAINS):
+        place = slice(chain * POS, (chain + 1) * POS)
+
+        def rows(j):
+            return jnp.concatenate(
+                [p[place, j * PADDED : j * PADDED + GROUP] for p in proj], axis=0
             )
 
+        dout = jnp.concatenate([grad_ref[order_ref[r], place] for r in range(SEQ)], axis=0)
+        heads_out, grads = temporal_block(rows(0), rows(1), rows(2), dout, valid)
+        for r in range(SEQ):
+            here = slice(r * POS, (r + 1) * POS)
+            out_ref[order_ref[r], place] = heads_out[here]
+            for j in range(3):
+                dproj_ref[r, place, j * PADDED : j * PADDED + GROUP] = grads[j][here]
+                dproj_ref[r, place, j * PADDED + GROUP : (j + 1) * PADDED] = jnp.zeros(
+                    (POS, PADDED - GROUP), BF
+                )
+
 
 def temporal(order, proj, grad_heads):
-    frame = pl.BlockSpec((POS, THREE), lambda i, o: (i, 0))
-    heads = pl.BlockSpec((SEQ, POS, GROUP), lambda i, o: (0, i, 0))
+    rows = CHAINS * POS
+    frame = pl.BlockSpec((rows, THREE), lambda i, o: (i, 0))
+    heads = pl.BlockSpec((SEQ, rows, GROUP), lambda i, o: (0, i, 0))
     return pl.pallas_call(
         temporal_kernel,
         grid_spec=pltpu.PrefetchScalarGridSpec(
             num_scalar_prefetch=1,
-            grid=(TOK // POS,),
+            grid=(TOK // rows,),
             in_specs=[frame] * SEQ + [heads],
-            out_specs=[heads, pl.BlockSpec((SEQ, POS, THREE), lambda i, o: (0, i, 0))],
+            out_specs=[heads, pl.BlockSpec((SEQ, rows, THREE), lambda i, o: (0, i, 0))],
         ),
         out_shape=[
             jax.ShapeDtypeStruct((SEQ, TOK, GROUP), BF),
@@ -260,8 +266,35 @@
         ],
         compiler_params=params(),
         name="temporal",
-        cost_estimate=cost(9),
+        cost_estimate=cost(8),
     )(order, *proj, grad_heads)
+
+
+SHARE_COLS = 512
+
+
+def shares_kernel(dproj_ref, w_ref, *outs):
+    left = dproj_ref[...].reshape(len(outs) * TOK, THREE)
+    full = dot_nt(left, w_ref[...]).astype(BF)
+    for r, out in enumerate(outs):
+        out[...] = full[r * TOK : (r + 1) * TOK]
+
+
+def shares_of(dproj, wide_proj, half):
+    count = SEQ // 2
+    return pl.pallas_call(
+        shares_kernel,
+        grid=(WIDTH // SHARE_COLS,),
+        in_specs=[
+            pl.BlockSpec((count, TOK, THREE), lambda i: (half, 0, 0)),
+            pl.BlockSpec((SHARE_COLS, THREE), lambda i: (i, 0)),
+        ],
+        out_specs=[pl.BlockSpec((TOK, SHARE_COLS), lambda i: (0, i))] * count,
+        out_shape=[jax.ShapeDtypeStruct((TOK, WIDTH), BF)] * count,
+        compiler_params=params(),
+        name="shares",
+        cost_estimate=cost(2),
+    )(dproj, wide_proj)
 
 
 GRAD_ROWS = 512
@@ -317,7 +350,7 @@
 
 
 def grad_input_kernel(factor, sum_a, sum_b, sum_c, sum_d, hidden_ref, resid_ref, gain_ref,
-                      out_ref, groups_ref):
+                      heads_ref, out_ref, groups_ref):
     def wide(ref):
         return ref[...].astype(F32)
 
@@ -339,54 +372,61 @@
         moved = dot_nn(both[:, four * rows : (four + 1) * rows], move).astype(BF)
         for j in range(SEQ):
             groups_ref[j, :, four * cols : (four + 1) * cols] = moved[:, j * cols : (j + 1) * cols]
-
-
-def grad_input_call(sums, hidden, resid, gain, factor):
+    groups_ref[:, :TOK, GROUPED:] = heads_ref[...]
+    groups_ref[:, TOK:, GROUPED:] = jnp.zeros((SEQ, EXTRA, GROUP), BF)
+
+
+def grad_input_call(sums, hidden, resid, gain, heads_out, factor):
     return pl.pallas_call(
         functools.partial(grad_input_kernel, factor),
         out_shape=[
             jax.ShapeDtypeStruct((TOK, WIDTH), BF),
-            jax.ShapeDtypeStruct((SEQ, TOK + EXTRA, GROUPED), BF),
+            jax.ShapeDtypeStruct((SEQ, TOK + EXTRA, GROUPED + GROUP), BF),
         ],
         compiler_params=params(),
         name="grad_input",
         cost_estimate=cost(2),
-    )(*sums, hidden, resid, gain)
-
-
-def out_product_kernel(factor, order_ref, groups_ref, *refs):
-    frames, out_ref = refs[:-1], refs[-1]
-    cols = out_ref.shape[1]
+    )(*sums, hidden, resid, gain, heads_out)
+
+
+def out_product_kernel(factor, order_ref, groups_ref, mixed_ref, mine_ref, other_ref):
     left = jnp.concatenate([groups_ref[order_ref[r], :TOK] for r in range(SEQ)], axis=0)
-    right = jnp.concatenate([f[...] for f in frames], axis=0)
-    product = dot_tn(left, right) * factor
+    product = dot_tn(left, mixed_ref[...]) * factor
     extras = sum(groups_ref[r, TOK:].astype(F32) for r in range(SEQ))
     high, low = two_parts(extras[0:1] + extras[1:2])
-    filler = jnp.zeros((1, cols - GROUPED), F32)
-    turn = lax.broadcasted_iota(jnp.int32, product.shape, 0) % SLOT
+    turn = lax.broadcasted_iota(jnp.int32, (GROUPED, GROUPED), 0) % SLOT
     first = pl.program_id(0) == 0
+    begin = product[:, :GROUPED]
     for place, part in ((SHARE, high), (SHARE + 1, low)):
-        full = jnp.concatenate([part.astype(F32), filler], axis=1)
-        product = jnp.where((turn == place) & first, full, product)
-    out_ref[...] = product.astype(BF)
-
-
-def out_product(order, groups, frames, factor):
+        begin = jnp.where((turn == place) & first, part.astype(F32), begin)
+    product = jnp.concatenate([begin, product[:, GROUPED:]], axis=1).astype(BF)
+    first_core = order_ref[SEQ] == 0
+    for d in range(DP // 2):
+        even = product[2 * d * SLOT : (2 * d + 1) * SLOT]
+        odd = product[(2 * d + 1) * SLOT : (2 * d + 2) * SLOT]
+        mine_ref[d] = jnp.where(first_core, even, odd)
+        other_ref[d] = jnp.where(first_core, odd, even)
+
+
+def out_product(order, groups, mixed_all, factor):
     cols = 512
+    spec = pl.BlockSpec((DP // 2, SLOT, cols), lambda i, o: (0, 0, i))
     return pl.pallas_call(
         functools.partial(out_product_kernel, factor),
         grid_spec=pltpu.PrefetchScalarGridSpec(
             num_scalar_prefetch=1,
             grid=(WIDTH // cols,),
-            in_specs=[pl.BlockSpec((SEQ, TOK + EXTRA, GROUPED), lambda i, o: (0, 0, 0))]
-            + [pl.BlockSpec((f.shape[0], cols), lambda i, o: (0, i)) for f in frames],
-            out_specs=pl.BlockSpec((GROUPED, cols), lambda i, o: (0, i)),
+            in_specs=[
+                pl.BlockSpec((SEQ, TOK + EXTRA, GROUPED), lambda i, o: (0, 0, 0)),
+                pl.BlockSpec((SEQ * TOK, cols), lambda i, o: (0, i)),
+            ],
+            out_specs=[spec, spec],
         ),
-        out_shape=jax.ShapeDtypeStruct((GROUPED, WIDTH), BF),
+        out_shape=[jax.ShapeDtypeStruct((DP // 2, SLOT, WIDTH), BF)] * 2,
         compiler_params=params(),
         name="out_product",
-        cost_estimate=cost(5),
-    )(order, groups, *frames)
+        cost_estimate=cost(3),
+    )(order, groups, mixed_all)
 
 
 def fold_kernel(in_ref, out_ref):
@@ -411,7 +451,8 @@
     )(pieces)
 
 
-def finish_kernel(in_ref, out_ref, gain_ref):
+def finish_kernel(in_ref, qkv_ref, out_ref, gain_ref, qkv_out_ref):
+    qkv_out_ref[...] = qkv_ref[...].astype(F32)
     out_ref[...] = jnp.concatenate(
         [in_ref[j].astype(F32)[:SHARE] for j in range(SEQ)], axis=0
     )
@@ -422,22 +463,21 @@
             [in_ref[j, :, four * cols : (four + 1) * cols] for j in range(SEQ)], axis=1
         )
         back = dot_nt(left, move)
-        gain_ref[:, four * rows : (four + 1) * rows] = (
-            back[SHARE : SHARE + 1] + back[SHARE + 1 : SHARE + 2]
-        )
-
-
-def finish(gathered):
+        gain_ref[pl.ds(four * rows, rows)] = back[SHARE] + back[SHARE + 1]
+
+
+def finish(gathered, qkv_rows):
     return pl.pallas_call(
         finish_kernel,
         out_shape=[
             jax.ShapeDtypeStruct((SEQ * SHARE, WIDTH), F32),
-            jax.ShapeDtypeStruct((1, WIDTH), F32),
+            jax.ShapeDtypeStruct((WIDTH,), F32),
+            jax.ShapeDtypeStruct(qkv_rows.shape, F32),
         ],
         compiler_params=params(),
         name="finish",
         cost_estimate=cost(2),
-    )(gathered)
+    )(gathered, qkv_rows)
 
 
 def along_x(array, shift):
@@ -462,6 +502,17 @@
     )
 
 
+def gather_along_x(own):
+    behind, ahead, partner = along_x(own, 1), along_x(own, -1), across_y(own)
+    far_top, far_low = along_x(behind[:HALF], 1), along_x(ahead[HALF:], -1)
+    partner_behind, partner_ahead = along_x(partner, 1), along_x(partner, -1)
+    partner_top, partner_low = along_x(partner_behind[:HALF], 1), along_x(partner_ahead[HALF:], -1)
+    return (
+        own, behind, ahead, far_top, far_low,
+        partner, partner_behind, partner_ahead, partner_top, partner_low,
+    )
+
+
 def whole_frames(parts):
     own, behind, ahead, top, low, partner, pbehind, pahead, ptop, plow = parts
     return (
@@ -471,8 +522,8 @@
 
 
 def scatter_frames(shares):
-    own, behind, ahead, far, partner, pbehind, pahead, pfar = shares
-    far = far + across_y(pfar)
+    own, behind, ahead, far, partner, pbehind, pahead, far_share = shares
+    far = far + far_share
     partner = partner + along_x(pbehind, -1) + along_x(pahead, 1)
     top, low = along_x(far[:HALF], -1), along_x(far[HALF:], 1)
     behind = jnp.concatenate([behind[:HALF] + top, behind[HALF:]], axis=0)
@@ -480,14 +531,9 @@
     return own, across_y(partner), along_x(behind, -1), along_x(ahead, 1)
 
 
-def dp_pieces(share):
-    blocks = share.reshape(DP // 2, 2, SLOT, WIDTH)
-    core = lax.axis_index("dp") % 2
-    mine = lax.dynamic_index_in_dim(blocks, core, 1, keepdims=False)
-    other = lax.dynamic_index_in_dim(blocks, 1 - core, 1, keepdims=False)
-    got = lax.ppermute(other, "dp", [(i, i ^ 1) for i in range(DP)])
+def chip_exchange(blocks):
     groups = [[2 * i + c for i in range(DP // 2)] for c in range(2)]
-    return lax.all_to_all(mine + got, "dp", 0, 0, axis_index_groups=groups, tiled=True)
+    return lax.all_to_all(blocks, "dp", 0, 0, axis_index_groups=groups, tiled=True)
 
 
 def body(
@@ -504,45 +550,49 @@
     place_x, place_y = me // 2, me % 2
     order = jnp.stack(
         [((place_x + s) % XS) * 2 + y for y in (place_y, 1 - place_y) for s in (0, 3, 1, 2)]
+        + [lax.axis_index("dp") % 2]
     ).astype(jnp.int32)
 
-    whole_out = lax.all_gather(out_weight, "dp", axis=0, tiled=True)
-    head_proj = lax.all_gather(qkv_weight, "dp", axis=0, tiled=True)
-
+    filler = jnp.zeros((out_weight.shape[0], THREE - 3 * GROUP), BF)
+    weights = lax.all_gather(
+        jnp.concatenate([out_weight, qkv_weight, filler], axis=1), "dp", axis=0, tiled=True
+    )
     mixed = spatial_fwd(q, k, v)
     grad_heads = lax.all_to_all(
         dout.reshape(TOK, SEQ, GROUP).transpose(1, 0, 2), "seq", 0, 0, tiled=True
     )
-    mixed_parts = gather_frames(mixed)
-    whole_out, grad_heads, *mixed_parts = lax.optimization_barrier(
-        (whole_out, grad_heads, *mixed_parts)
-    )
-    hidden, normed = out_norm(mixed, whole_out, flat_in, gain)
+    mixed_parts = gather_along_x(mixed)
+    mixed_all = jnp.concatenate(mixed_parts, axis=0)
+    weights, grad_heads, mixed_all = lax.optimization_barrier((weights, grad_heads, mixed_all))
+    hidden, normed = out_norm(mixed, weights, flat_in, gain)
     normed_parts = gather_frames(normed)
-    head_proj, *early = lax.optimization_barrier((head_proj, *normed_parts[:8]))
-    wide_proj = widen(head_proj)
-    proj = [
-        dot_nn(f, wide_proj).astype(BF) for f in whole_frames((*early, *normed_parts[8:]))
-    ]
+    proj_weights, *first = lax.optimization_barrier((weights, *normed_parts[:3], normed_parts[5]))
+    frames = (*first[:3], *normed_parts[3:5], first[3], *normed_parts[6:])
+    wide_proj = widen(proj_weights)
+    proj = [dot_nn(f, wide_proj).astype(BF) for f in whole_frames(frames)]
     heads_out, dproj = temporal(order, proj, grad_heads)
-    shares = [dot_nt(dproj[r], wide_proj).astype(BF) for r in range(SEQ)]
-    *shares, dproj, heads_out = lax.optimization_barrier((*shares, dproj, heads_out))
-    qkv_share = qkv_product(normed_parts, dproj, factor)
-    sums = scatter_frames(shares)
-    *sums, qkv_share = lax.optimization_barrier((*sums, qkv_share))
-    qkv_grad = lax.psum_scatter(qkv_share, "dp", scatter_dimension=0, tiled=True).astype(F32)
-
-    grad_input, groups = grad_input_call(sums, hidden, resid, gain, factor)
+    partner_shares = shares_of(dproj, wide_proj, 1)
+    *partner_shares, dproj = lax.optimization_barrier((*partner_shares, dproj))
+    far_share, dproj_later = lax.optimization_barrier((across_y(partner_shares[3]), dproj))
+    qkv_share = qkv_product(normed_parts, dproj_later, factor)
+    qkv_grad = lax.psum_scatter(qkv_share, "dp", scatter_dimension=0, tiled=True)
+    sums = scatter_frames((*shares_of(dproj, wide_proj, 0), *partner_shares[:3], far_share))
+
+    grad_input, groups = grad_input_call(sums, hidden, resid, gain, heads_out, factor)
     groups = lax.all_to_all(groups, "seq", 0, 0, tiled=True)
-    out_share = out_product(order, groups, mixed_parts, factor)
-    pieces = dp_pieces(out_share)
-    temporal_out = lax.all_to_all(heads_out, "seq", 0, 0, tiled=True)
-    temporal_out = temporal_out.transpose(1, 0, 2).reshape(TOK, WIDTH)
-    grad_q, grad_k, grad_v = spatial_bwd(grad_input, whole_out, q, k, v)
-    out_grad, gain_grad = finish(lax.all_to_all(fold(pieces), "seq", 0, 0, tiled=True))
-    return tuple(
-        a.reshape(block_shape) for a in (hidden, temporal_out, grad_input, grad_q, grad_k, grad_v)
-    ) + (qkv_grad, out_grad, gain_grad.reshape(WIDTH))
+    grads = spatial_bwd(grad_input, weights, q, k, v)
+    groups, *grads = lax.optimization_barrier((groups, *grads))
+    mine, other = out_product(order, groups, mixed_all, factor)
+    summed = mine + lax.ppermute(other, "dp", [(i, i ^ 1) for i in range(DP)])
+    received = chip_exchange(summed)
+    temporal_out = groups[:, :TOK, GROUPED:].transpose(1, 0, 2).reshape(TOK, WIDTH)
+    gathered = lax.all_to_all(fold(received), "seq", 0, 0, tiled=True)
+    out_grad, gain_grad, qkv_grad = finish(gathered, qkv_grad)
+    return tuple(a.reshape(block_shape) for a in (hidden, temporal_out, grad_input, *grads)) + (
+        qkv_grad,
+        out_grad,
+        gain_grad,
+    )
 
 
 def solution(mesh):

time: 243 us -> 224 us (0.922)
  waiting for transfers between devices: 85.9 us -> 65.1 us
  blocking collectives: 0 us -> 14.8 us
  matrix products: 13 us -> 3.83 us
  other arithmetic: 5.56 us -> 2.57 us
    all_to_all x0 -> x1, blocking collectives: none -> 14.8 us  [chip_exchange(): lax.all_to_all(blocks, 'dp', 0, 0, axis_index_groups=groups, tiled=True)]
    ppermute x8 -> x6, waiting for transfers between devices: 34.6 us -> 23.4 us  [across_y(): return lax.ppermute(array, 'seq', [(i, i ^ 1) for i in range(SEQ)])]
    ppermute x18 -> x20, starting transfers between devices: 23 us -> 32.8 us  [along_x(): return lax.ppermute(array, 'seq', pairs)]
    all_to_all x3 -> x1, waiting for transfers between devices: 16.6 us -> 7.94 us  [body(): gathered = lax.all_to_all(fold(received), 'seq', 0, 0, tiled=True)]
    all_to_all x3 -> x1, starting transfers between devices: 13.2 us -> 5.53 us  [body(): gathered = lax.all_to_all(fold(received), 'seq', 0, 0, tiled=True)]
    all_to_all x1, waiting for transfers between devices: 10.1 us -> 2.72 us  [body(): groups = lax.all_to_all(groups, 'seq', 0, 0, tiled=True)]
    dot_general x8 -> x0, matrix products: 7.16 us -> none  [dot_nt(): lax.dot_general(a, b, (((1,), (1,)), ((), ())), preferred_element_type=F32)]
    all_gather x2 -> x1, waiting for transfers between devices: 0.01 us -> 6.45 us  [body(): lax.all_gather(jnp.concatenate([out_weight, qkv_weight, filler], axis=1),...]
  transfers between devices with their start and end apart: 35 -> 32, of which waited for: 16 -> 17; matrix products, arithmetic and copies ran while one was open for 7% -> 4% of each run, Pallas kernels for 11% -> 10%
where the time goes in v3:
time: 224 us; the launch traced here: 223 us
  waiting for transfers between devices  65.1 us (29%)
  starting transfers between devices  60.8 us (27%)
  Pallas kernels  36.4 us (16%)
  local copies, waits for them, and re-layouts  24.7 us (11%)
  blocking collectives  14.8 us (7%)
  between operations  14.6 us (7%)
  matrix products  3.83 us (2%)
  other arithmetic  2.57 us (1%)
    ppermute x20, starting transfers between devices, along_x(): return lax.ppermute(array, 'seq', pairs)  32.8 us
    ppermute x6, waiting for transfers between devices, across_y(): return lax.ppermute(array, 'seq', [(i, i ^ 1) for i in range(SEQ)])  23.4 us
    ppermute x20, waiting for transfers between devices, along_x(): return lax.ppermute(array, 'seq', pairs)  22.9 us
    unnamed x57, local copies, waits for them, and re-layouts  19.3 us
    all_to_all x1, blocking collectives, chip_exchange(): lax.all_to_all(blocks, 'dp', 0, 0, axis_index_groups=groups, tiled=True)  14.8 us
    ppermute x6, starting transfers between devices, across_y(): return lax.ppermute(array, 'seq', [(i, i ^ 1) for i in range(SEQ)])  12.2 us
    all_to_all x1, waiting for transfers between devices, body(): gathered = lax.all_to_all(fold(received), 'seq', 0, 0, tiled=True)  7.94 us
    pallas_call x1, Pallas kernels, spatial_bwd(): pl.pallas_call(spatial_bwd_kernel, grid=(WIDTH // (PAIRS * LANE),), in_sp...  7.62 us
  transfers between devices with their start and end apart: 32, of which 17 were waited for; matrix products, arithmetic and copies ran while one was open for 4% of the time, Pallas kernels for 10%

profile of v3, /device:TPU:0, one launch (start us, length us, event | category | flops | bytes accessed | tf_op | source)
XLA Modules:
  0.0 222.8 jit_solution(1794986009748922318)
XLA Ops:
  12.2 2.8 %spatial_fwd.1.mixed_ref = bf16[128,1536]{1,0:T(8,128)(2,1)S(1)} custom-call(bf16[128,1536]{1,0:T(8,128)(2,1)S(1)} %bitcast.38, bf16[128,1536]{1,0:T(8,128)(2,1)S(1)} %bitcast.40, bf16[128,1536]{1,0:T(8,128)(2,1)S(1)} %bitcast.42), custom_call_target="tpu_custom_call" | custom-call | bytes 12000000 | tf_op jit(solution)/shard_map/spatial_fwd/pallas_call | solution.py:101
  15.0 2.9 %collective-permute-start.1 = (bf16[128,1536]{1,0:T(8,128)(2,1)S(1)}, bf16[128,1536]{1,0:T(8,128)(2,1)S(1)}, u32[]{:S(2)}, u32[]{:S(2)}) collective-permute-start(bf16[128,1536]{1,0:T(8,128)(2,1)S(1)} %spatial_fwd.1.mixed_ref), channel_id=1, source_target_pairs={{0,6},{1,7},{2,0},{3,1},{4,2},{5,3},{6,4},{7,5},{8,14},{9,15},{10,... | collective-permute-start | bytes 1179656 | tf_op jit(solution)/shard_map/ppermute | solution.py:485
  17.9 3.2 %collective-permute-start.4 = (bf16[128,1536]{1,0:T(8,128)(2,1)S(1)}, bf16[128,1536]{1,0:T(8,128)(2,1)S(1)}, u32[]{:S(2)}, u32[]{:S(2)}) collective-permute-start(bf16[128,1536]{1,0:T(8,128)(2,1)S(1)} %spatial_fwd.1.mixed_ref), channel_id=1, source_target_pairs={{0,1},{1,0},{2,3},{3,2},{4,5},{5,4},{6,7},{7,6},{8,9},{9,8},{10,11... | collective-permute-start | bytes 1179656 | tf_op jit(solution)/shard_map/ppermute | solution.py:489
  22.7 4.5 %all-to-all-start = ((bf16[8,128,192]{1,2,0:T(8,128)(2,1)}), bf16[8,128,192]{1,2,0:T(8,128)(2,1)S(1)}, u32[]{:S(2)}, u32[]{:S(2)}) async-start(bf16[8,128,192]{1,2,0:T(8,128)(2,1)} %copy.20), calls=%async_computation | async-start | bytes 786432 | tf_op jit(solution)/shard_map/all_to_all | solution.py:561
  27.3 3.3 %collective-permute-start.3 = (bf16[64,1536]{1,0:T(8,128)(2,1)S(1)}, bf16[64,1536]{1,0:T(8,128)(2,1)S(1)}, u32[]{:S(2)}, u32[]{:S(2)}) collective-permute-start(bf16[64,1536]{1,0:T(8,128)(2,1)S(1)} %slice.53), channel_id=1, source_target_pairs={{0,6},{1,7},{2,0},{3,1},{4,2},{5,3},{6,4},{7,5},{8,14},{9,15},{10,... | collective-permute-start | bytes 589832 | tf_op jit(solution)/shard_map/ppermute | solution.py:485
  30.7 10.7 %collective-permute-done.4 = bf16[128,1536]{1,0:T(8,128)(2,1)S(1)} collective-permute-done((bf16[128,1536]{1,0:T(8,128)(2,1)S(1)}, bf16[128,1536]{1,0:T(8,128)(2,1)S(1)}, u32[]{:S(2)}, u32[]{:S(2)}) %collective-permute-start.4) | collective-permute-done | bytes 393248 | tf_op jit(solution)/shard_map/ppermute | solution.py:489
  41.4 3.0 %collective-permute-start.6 = (bf16[128,1536]{1,0:T(8,128)(2,1)S(1)}, bf16[128,1536]{1,0:T(8,128)(2,1)S(1)}, u32[]{:S(2)}, u32[]{:S(2)}) collective-permute-start(bf16[128,1536]{1,0:T(8,128)(2,1)S(1)} %collective-permute-done.4), channel_id=1, source_target_pairs={{0,6},{1,7},{2,0},{3,1},{4,2},{5,3},{6,4},{7,5},{8,14},{9,15},{10,... | collective-permute-start | bytes 1179656 | tf_op jit(solution)/shard_map/ppermute | solution.py:485
  44.6 5.6 %collective-permute-done.6 = bf16[128,1536]{1,0:T(8,128)(2,1)S(1)} collective-permute-done((bf16[128,1536]{1,0:T(8,128)(2,1)S(1)}, bf16[128,1536]{1,0:T(8,128)(2,1)S(1)}, u32[]{:S(2)}, u32[]{:S(2)}) %collective-permute-start.6) | collective-permute-done | bytes 393248 | tf_op jit(solution)/shard_map/ppermute | solution.py:485
  50.3 3.8 %collective-permute-start.8 = (bf16[64,1536]{1,0:T(8,128)(2,1)S(1)}, bf16[64,1536]{1,0:T(8,128)(2,1)S(1)}, u32[]{:S(2)}, u32[]{:S(2)}) collective-permute-start(bf16[64,1536]{1,0:T(8,128)(2,1)S(1)} %slice.55), channel_id=1, source_target_pairs={{0,6},{1,7},{2,0},{3,1},{4,2},{5,3},{6,4},{7,5},{8,14},{9,15},{10,... | collective-permute-start | bytes 589832 | tf_op jit(solution)/shard_map/ppermute | solution.py:485
  54.3 6.8 %collective-permute-done.7 = bf16[64,1536]{1,0:T(8,128)(2,1)S(1)} collective-permute-done((bf16[64,1536]{1,0:T(8,128)(2,1)S(1)}, bf16[64,1536]{1,0:T(8,128)(2,1)S(1)}, u32[]{:S(2)}, u32[]{:S(2)}) %collective-permute-start.7) | collective-permute-done | bytes 196640 | tf_op jit(solution)/shard_map/ppermute | solution.py:485
  62.9 6.4 %all-gather.2.cloned.1.call-done.w_ref = bf16[1536,2304]{1,0:T(8,128)(2,1)} async-done(((bf16[96,2304]{1,0:T(8,128)(2,1)}), bf16[1536,2304]{1,0:T(8,128)(2,1)}) %all-gather.2.cloned.1.call-update) | async-done | bytes 7077904 | tf_op jit(solution)/shard_map/all_gather | solution.py:557
  69.4 3.0 %copy-done = bf16[1536,2304]{1,0:T(8,128)(2,1)S(1)} copy-done((bf16[1536,2304]{1,0:T(8,128)(2,1)S(1)}, bf16[1536,2304]{1,0:T(8,128)(2,1)}, u32[]{:S(2)}) %copy-start) | copy-done | bytes 7077912
  72.4 3.2 %out_norm.1 = (bf16[128,1536]{1,0:T(8,128)(2,1)}, bf16[128,1536]{1,0:T(8,128)(2,1)S(1)}) custom-call(bf16[128,1536]{1,0:T(8,128)(2,1)S(1)} %spatial_fwd.1.mixed_ref, bf16[1536,2304]{1,0:T(8,128)(2,1)S(1)} %copy-done, bf16[128,1536]{1,0:T(8,128)(2,1)S(1)} %bitcast.44, f32[1,1536]{1,0:T(1,128)S(1)} %reshape.55.gain_ref), custom_call_target="tpu_custom_call" | custom-call | bytes 12000000 | tf_op jit(solution)/shard_map/out_norm/pallas_call | solution.py:162
  75.6 3.0 %collective-permute-start.10 = (bf16[128,1536]{1,0:T(8,128)(2,1)S(1)}, bf16[128,1536]{1,0:T(8,128)(2,1)S(1)}, u32[]{:S(2)}, u32[]{:S(2)}) collective-permute-start(bf16[128,1536]{1,0:T(8,128)(2,1)S(1)} %get-tuple-element.53.refs_0_), channel_id=1, source_target_pairs={{0,6},{1,7},{2,0},{3,1},{4,2},{5,3},{6,4},{7,5},{8,14},{9,15},{10,... | collective-permute-start | bytes 1179656 | tf_op jit(solution)/shard_map/ppermute | solution.py:485
  80.7 6.6 %collective-permute-done.10.refs_2_ = bf16[128,1536]{1,0:T(8,128)(2,1)S(1)} collective-permute-done((bf16[128,1536]{1,0:T(8,128)(2,1)S(1)}, bf16[128,1536]{1,0:T(8,128)(2,1)S(1)}, u32[]{:S(2)}, u32[]{:S(2)}) %collective-permute-start.10) | collective-permute-done | bytes 393248 | tf_op jit(solution)/shard_map/ppermute | solution.py:485
  87.3 3.8 %collective-permute-start.13 = (bf16[64,1536]{1,0:T(8,128)(2,1)S(1)}, bf16[64,1536]{1,0:T(8,128)(2,1)S(1)}, u32[]{:S(2)}, u32[]{:S(2)}) collective-permute-start(bf16[64,1536]{1,0:T(8,128)(2,1)S(1)} %slice.57), channel_id=1, source_target_pairs={{0,6},{1,7},{2,0},{3,1},{4,2},{5,3},{6,4},{7,5},{8,14},{9,15},{10,... | collective-permute-start | bytes 589832 | tf_op jit(solution)/shard_map/ppermute | solution.py:485
  92.4 3.0 %copy-done.1 = bf16[1536,2304]{1,0:T(8,128)(2,1)S(1)} copy-done((bf16[1536,2304]{1,0:T(8,128)(2,1)S(1)}, bf16[1536,2304]{1,0:T(8,128)(2,1)}, u32[]{:S(2)}) %copy-start.1) | copy-done | bytes 7077912
  97.8 3.3 %collective-permute-start.15 = (bf16[128,1536]{1,0:T(8,128)(2,1)S(1)}, bf16[128,1536]{1,0:T(8,128)(2,1)S(1)}, u32[]{:S(2)}, u32[]{:S(2)}) collective-permute-start(bf16[128,1536]{1,0:T(8,128)(2,1)S(1)} %collective-permute-done.11.refs_5_), channel_id=1, source_target_pairs={{0,6},{1,7},{2,0},{3,1},{4,2},{5,3},{6,4},{7,5},{8,14},{9,15},{10,... | collective-permute-start | bytes 1179656 | tf_op jit(solution)/shard_map/ppermute | solution.py:485
  105.7 4.6 %collective-permute-done.17.refs_9_ = bf16[64,1536]{1,0:T(8,128)(2,1)S(1)} collective-permute-done((bf16[64,1536]{1,0:T(8,128)(2,1)S(1)}, bf16[64,1536]{1,0:T(8,128)(2,1)S(1)}, u32[]{:S(2)}, u32[]{:S(2)}) %collective-permute-start.17) | collective-permute-done | bytes 196640 | tf_op jit(solution)/shard_map/ppermute | solution.py:489
  113.9 5.9 %temporal.1 = (bf16[8,128,192]{2,1,0:T(8,128)(2,1)S(1)}, bf16[8,128,768]{2,1,0:T(8,128)(2,1)S(1)}) custom-call(s32[9]{0:T(128)S(1)} %stack.39.order_ref, bf16[128,768]{1,0:T(8,128)(2,1)S(1)} %convolution_convert_fusion.7.refs_0_, bf16[128,768]{1,0:T(8,128)(2,1)S(1)} %convolution_convert_fusion.6.refs_1_, ...), custom_call_target="tpu_custom_call" | custom-call | bytes 24000000 | tf_op jit(solution)/shard_map/temporal/pallas_call | solution.py:255
  119.8 2.6 %shares.2 = (bf16[128,1536]{1,0:T(8,128)(2,1)S(1)}, bf16[128,1536]{1,0:T(8,128)(2,1)}, bf16[128,1536]{1,0:T(8,128)(2,1)}, bf16[128,1536]{1,0:T(8,128)(2,1)S(1)}) custom-call(bf16[8,128,768]{2,1,0:T(8,128)(2,1)S(1)} %get-tuple-element.87.dproj_ref.refs_10_, bf16[1536,768]{1,0:T(8,128)(2,1)S(1)} %widen.1.w_ref), custom_call_target="tpu_custom_call" | custom-call | bytes 6000000 | tf_op jit(solution)/shard_map/shares/pallas_call | solution.py:285
  127.5 3.0 %collective-permute-start.18 = (bf16[128,1536]{1,0:T(8,128)(2,1)}, bf16[128,1536]{1,0:T(8,128)(2,1)}, u32[]{:S(2)}, u32[]{:S(2)}) collective-permute-start(bf16[128,1536]{1,0:T(8,128)(2,1)} %get-tuple-element.67), channel_id=1, source_target_pairs={{0,6},{1,7},{2,0},{3,1},{4,2},{5,3},{6,4},{7,5},{8,14},{9,15},{10,... | collective-permute-start | bytes 1179656 | tf_op jit(solution)/shard_map/ppermute | solution.py:485
  132.4 4.5 %qkv_product.1 = bf16[1536,576]{1,0:T(8,128)(2,1)} custom-call(bf16[128,1536]{1,0:T(8,128)(2,1)S(1)} %get-tuple-element.53.refs_0_, bf16[128,1536]{1,0:T(8,128)(2,1)S(1)} %collective-permute-done.9.refs_1_, bf16[128,1536]{1,0:T(8,128)(2,1)S(1)} %collective-permute-done.10.refs_2_, bf16[64,1536]{1,0:T(8,128)(2,1)S(1)} %collective-permute-done.12.refs_3_, ...), custom_call_target="tpu_custom_call" | custom-call | bytes 15000000 | tf_op jit(solution)/shard_map/qkv_product/pallas_call | solution.py:316
  138.2 3.2 %collective-permute-start.22 = (bf16[64,1536]{1,0:T(8,128)(2,1)S(1)}, bf16[64,1536]{1,0:T(8,128)(2,1)S(1)}, u32[]{:S(2)}, u32[]{:S(2)}) collective-permute-start(bf16[64,1536]{1,0:T(8,128)(2,1)S(1)} %get-tuple-element.94), channel_id=1, source_target_pairs={{0,6},{1,7},{2,0},{3,1},{4,2},{5,3},{6,4},{7,5},{8,14},{9,15},{10,... | collective-permute-start | bytes 589832 | tf_op jit(solution)/shard_map/ppermute | solution.py:485
  148.6 4.0 %collective-permute-done.20.sum_b = bf16[128,1536]{1,0:T(8,128)(2,1)S(1)} collective-permute-done((bf16[128,1536]{1,0:T(8,128)(2,1)S(1)}, bf16[128,1536]{1,0:T(8,128)(2,1)S(1)}, u32[]{:S(2)}, u32[]{:S(2)}) %collective-permute-start.20) | collective-permute-done | bytes 393248 | tf_op jit(solution)/shard_map/ppermute | solution.py:489
  156.9 5.6 %all-to-all-start.1 = ((bf16[8,144,448]{2,1,0:T(8,128)(2,1)}), bf16[8,144,448]{2,1,0:T(8,128)(2,1)S(1)}, u32[]{:S(2)}, u32[]{:S(2)}) async-start(bf16[8,144,448]{2,1,0:T(8,128)(2,1)} %get-tuple-element.75), calls=%async_computation.1 | async-start | bytes 2359296 | tf_op jit(solution)/shard_map/all_to_all | solution.py:582
  162.5 3.0 %copy-done.2 = bf16[1536,2304]{1,0:T(8,128)(2,1)S(1)} copy-done((bf16[1536,2304]{1,0:T(8,128)(2,1)S(1)}, bf16[1536,2304]{1,0:T(8,128)(2,1)}, u32[]{:S(2)}) %copy-start.2) | copy-done | bytes 7077912
  166.5 7.6 %spatial_bwd.1 = (bf16[128,1536]{1,0:T(8,128)(2,1)}, bf16[128,1536]{1,0:T(8,128)(2,1)}, bf16[128,1536]{1,0:T(8,128)(2,1)}) custom-call(bf16[128,1536]{1,0:T(8,128)(2,1)S(1)} %copy-done.12, bf16[1536,2304]{1,0:T(8,128)(2,1)S(1)} %copy-done.2, bf16[128,1536]{1,0:T(8,128)(2,1)S(1)} %bitcast.39, bf16[128,1536]{1,0:T(8,128)(2,1)S(1)} %bitcast.41, ...), custom_call_target="tpu_custom_call" | custom-call | bytes 27000000 | tf_op jit(solution)/shard_map/spatial_bwd/pallas_call | solution.py:128
  174.1 2.7 %all-to-all-done.1.groups_ref = bf16[8,144,448]{2,1,0:T(8,128)(2,1)S(1)} async-done(((bf16[8,144,448]{2,1,0:T(8,128)(2,1)}), bf16[8,144,448]{2,1,0:T(8,128)(2,1)S(1)}, u32[]{:S(2)}, u32[]{:S(2)}) %all-to-all-start.1) | async-done | bytes 1032224 | tf_op jit(solution)/shard_map/all_to_all | solution.py:582
  183.0 14.8 %all_to_all.20.in_ref = bf16[8,16,1536]{2,1,0:T(8,128)(2,1)S(1)} all-to-all(bf16[8,16,1536]{2,1,0:T(8,128)(2,1)S(1)} %add.102), channel_id=1, replica_groups={{0,16,32,48,64,80,96,112},{8,24,40,56,72,88,104,120},{1,17,33,49,65,81,..., dimensions={0} | all-to-all | bytes 786432 | tf_op jit(solution)/shard_map/all_to_all | solution.py:536
  198.6 5.5 %all-to-all-start.3 = ((bf16[8,16,1536]{2,1,0:T(8,128)(2,1)}), bf16[8,16,1536]{2,1,0:T(8,128)(2,1)S(1)}, u32[]{:S(2)}, u32[]{:S(2)}) async-start(bf16[8,16,1536]{2,1,0:T(8,128)(2,1)} %fold.1), calls=%async_computation.3 | async-start | bytes 786432 | tf_op jit(solution)/shard_map/all_to_all | solution.py:589
  205.6 7.9 %all-to-all-done.3.in_ref = bf16[8,16,1536]{2,1,0:T(8,128)(2,1)S(1)} async-done(((bf16[8,16,1536]{2,1,0:T(8,128)(2,1)}), bf16[8,16,1536]{2,1,0:T(8,128)(2,1)S(1)}, u32[]{:S(2)}, u32[]{:S(2)}) %all-to-all-start.3) | async-done | bytes 393248 | tf_op jit(solution)/shard_map/all_to_all | solution.py:589
  (136 shorter events, 54.2 us)
Async XLA Ops:
  7.2 62.2 %all-gather.2.cloned.1.call-start = ((), (), s32[]{:S(2)}) async-start(), calls=%async_computation.5 | async-start | bytes 7520256 | tf_op jit(solution)/shard_map/all_gather | solution.py:557
  15.0 12.3 %collective-permute-start.1 = (bf16[128,1536]{1,0:T(8,128)(2,1)S(1)}, bf16[128,1536]{1,0:T(8,128)(2,1)S(1)}, u32[]{:S(2)}, u32[]{:S(2)}) collective-permute-start(bf16[128,1536]{1,0:T(8,128)(2,1)S(1)} %spatial_fwd.1.mixed_ref), channel_id=1, source_target_pairs={{0,6},{1,7},{2,0},{3,1},{4,2},{5,3},{6,4},{7,5},{8,14},{9,15},{10,... | collective-permute-start | bytes 1179656 | tf_op jit(solution)/shard_map/ppermute | solution.py:485
  17.9 12.7 %collective-permute-start = (bf16[128,1536]{1,0:T(8,128)(2,1)S(1)}, bf16[128,1536]{1,0:T(8,128)(2,1)S(1)}, u32[]{:S(2)}, u32[]{:S(2)}) collective-permute-start(bf16[128,1536]{1,0:T(8,128)(2,1)S(1)} %spatial_fwd.1.mixed_ref), channel_id=1, source_target_pairs={{0,2},{1,3},{2,4},{3,5},{4,6},{5,7},{6,0},{7,1},{8,10},{9,11},{10,... | collective-permute-start | bytes 1179656 | tf_op jit(solution)/shard_map/ppermute | solution.py:485
  17.9 23.5 %collective-permute-start.4 = (bf16[128,1536]{1,0:T(8,128)(2,1)S(1)}, bf16[128,1536]{1,0:T(8,128)(2,1)S(1)}, u32[]{:S(2)}, u32[]{:S(2)}) collective-permute-start(bf16[128,1536]{1,0:T(8,128)(2,1)S(1)} %spatial_fwd.1.mixed_ref), channel_id=1, source_target_pairs={{0,1},{1,0},{2,3},{3,2},{4,5},{5,4},{6,7},{7,6},{8,9},{9,8},{10,11... | collective-permute-start | bytes 1179656 | tf_op jit(solution)/shard_map/ppermute | solution.py:489
  22.7 40.2 %all-to-all-start = ((bf16[8,128,192]{1,2,0:T(8,128)(2,1)}), bf16[8,128,192]{1,2,0:T(8,128)(2,1)S(1)}, u32[]{:S(2)}, u32[]{:S(2)}) async-start(bf16[8,128,192]{1,2,0:T(8,128)(2,1)} %copy.20), calls=%async_computation | async-start | bytes 786432 | tf_op jit(solution)/shard_map/all_to_all | solution.py:561
  27.2 186.4 %reduce-scatter.2.cloned.1.call-start = ((), (), s32[]{:S(2)}) async-start(), calls=%async_computation.6 | async-start | bytes 2088960 | tf_op jit(solution)/shard_map/reduce_scatter | solution.py:578
  27.3 17.2 %collective-permute-start.3 = (bf16[64,1536]{1,0:T(8,128)(2,1)S(1)}, bf16[64,1536]{1,0:T(8,128)(2,1)S(1)}, u32[]{:S(2)}, u32[]{:S(2)}) collective-permute-start(bf16[64,1536]{1,0:T(8,128)(2,1)S(1)} %slice.53), channel_id=1, source_target_pairs={{0,6},{1,7},{2,0},{3,1},{4,2},{5,3},{6,4},{7,5},{8,14},{9,15},{10,... | collective-permute-start | bytes 589832 | tf_op jit(solution)/shard_map/ppermute | solution.py:485
  30.6 13.9 %collective-permute-start.2 = (bf16[64,1536]{1,0:T(8,128)(2,1)S(1)}, bf16[64,1536]{1,0:T(8,128)(2,1)S(1)}, u32[]{:S(2)}, u32[]{:S(2)}) collective-permute-start(bf16[64,1536]{1,0:T(8,128)(2,1)S(1)} %slice.52), channel_id=1, source_target_pairs={{0,2},{1,3},{2,4},{3,5},{4,6},{5,7},{6,0},{7,1},{8,10},{9,11},{10,... | collective-permute-start | bytes 589832 | tf_op jit(solution)/shard_map/ppermute | solution.py:485
  41.4 8.8 %collective-permute-start.6 = (bf16[128,1536]{1,0:T(8,128)(2,1)S(1)}, bf16[128,1536]{1,0:T(8,128)(2,1)S(1)}, u32[]{:S(2)}, u32[]{:S(2)}) collective-permute-start(bf16[128,1536]{1,0:T(8,128)(2,1)S(1)} %collective-permute-done.4), channel_id=1, source_target_pairs={{0,6},{1,7},{2,0},{3,1},{4,2},{5,3},{6,4},{7,5},{8,14},{9,15},{10,... | collective-permute-start | bytes 1179656 | tf_op jit(solution)/shard_map/ppermute | solution.py:485
  44.5 9.7 %collective-permute-start.5 = (bf16[128,1536]{1,0:T(8,128)(2,1)S(1)}, bf16[128,1536]{1,0:T(8,128)(2,1)S(1)}, u32[]{:S(2)}, u32[]{:S(2)}) collective-permute-start(bf16[128,1536]{1,0:T(8,128)(2,1)S(1)} %collective-permute-done.4), channel_id=1, source_target_pairs={{0,2},{1,3},{2,4},{3,5},{4,6},{5,7},{6,0},{7,1},{8,10},{9,11},{10,... | collective-permute-start | bytes 1179656 | tf_op jit(solution)/shard_map/ppermute | solution.py:485
  50.3 10.8 %collective-permute-start.8 = (bf16[64,1536]{1,0:T(8,128)(2,1)S(1)}, bf16[64,1536]{1,0:T(8,128)(2,1)S(1)}, u32[]{:S(2)}, u32[]{:S(2)}) collective-permute-start(bf16[64,1536]{1,0:T(8,128)(2,1)S(1)} %slice.55), channel_id=1, source_target_pairs={{0,6},{1,7},{2,0},{3,1},{4,2},{5,3},{6,4},{7,5},{8,14},{9,15},{10,... | collective-permute-start | bytes 589832 | tf_op jit(solution)/shard_map/ppermute | solution.py:485
  54.1 6.9 %collective-permute-start.7 = (bf16[64,1536]{1,0:T(8,128)(2,1)S(1)}, bf16[64,1536]{1,0:T(8,128)(2,1)S(1)}, u32[]{:S(2)}, u32[]{:S(2)}) collective-permute-start(bf16[64,1536]{1,0:T(8,128)(2,1)S(1)} %slice.54), channel_id=1, source_target_pairs={{0,2},{1,3},{2,4},{3,5},{4,6},{5,7},{6,0},{7,1},{8,10},{9,11},{10,... | collective-permute-start | bytes 589832 | tf_op jit(solution)/shard_map/ppermute | solution.py:485
  75.6 11.7 %collective-permute-start.10 = (bf16[128,1536]{1,0:T(8,128)(2,1)S(1)}, bf16[128,1536]{1,0:T(8,128)(2,1)S(1)}, u32[]{:S(2)}, u32[]{:S(2)}) collective-permute-start(bf16[128,1536]{1,0:T(8,128)(2,1)S(1)} %get-tuple-element.53.refs_0_), channel_id=1, source_target_pairs={{0,6},{1,7},{2,0},{3,1},{4,2},{5,3},{6,4},{7,5},{8,14},{9,15},{10,... | collective-permute-start | bytes 1179656 | tf_op jit(solution)/shard_map/ppermute | solution.py:485
  78.6 12.5 %collective-permute-start.11 = (bf16[128,1536]{1,0:T(8,128)(2,1)S(1)}, bf16[128,1536]{1,0:T(8,128)(2,1)S(1)}, u32[]{:S(2)}, u32[]{:S(2)}) collective-permute-start(bf16[128,1536]{1,0:T(8,128)(2,1)S(1)} %get-tuple-element.53.refs_0_), channel_id=1, source_target_pairs={{0,1},{1,0},{2,3},{3,2},{4,5},{5,4},{6,7},{7,6},{8,9},{9,8},{10,11... | collective-permute-start | bytes 1179656 | tf_op jit(solution)/shard_map/ppermute | solution.py:489
  80.4 11.9 %collective-permute-start.9 = (bf16[128,1536]{1,0:T(8,128)(2,1)S(1)}, bf16[128,1536]{1,0:T(8,128)(2,1)S(1)}, u32[]{:S(2)}, u32[]{:S(2)}) collective-permute-start(bf16[128,1536]{1,0:T(8,128)(2,1)S(1)} %get-tuple-element.53.refs_0_), channel_id=1, source_target_pairs={{0,2},{1,3},{2,4},{3,5},{4,6},{5,7},{6,0},{7,1},{8,10},{9,11},{10,... | collective-permute-start | bytes 1179656 | tf_op jit(solution)/shard_map/ppermute | solution.py:485
  87.3 14.2 %collective-permute-start.13 = (bf16[64,1536]{1,0:T(8,128)(2,1)S(1)}, bf16[64,1536]{1,0:T(8,128)(2,1)S(1)}, u32[]{:S(2)}, u32[]{:S(2)}) collective-permute-start(bf16[64,1536]{1,0:T(8,128)(2,1)S(1)} %slice.57), channel_id=1, source_target_pairs={{0,6},{1,7},{2,0},{3,1},{4,2},{5,3},{6,4},{7,5},{8,14},{9,15},{10,... | collective-permute-start | bytes 589832 | tf_op jit(solution)/shard_map/ppermute | solution.py:485
  92.3 11.0 %collective-permute-start.12 = (bf16[64,1536]{1,0:T(8,128)(2,1)S(1)}, bf16[64,1536]{1,0:T(8,128)(2,1)S(1)}, u32[]{:S(2)}, u32[]{:S(2)}) collective-permute-start(bf16[64,1536]{1,0:T(8,128)(2,1)S(1)} %slice.56), channel_id=1, source_target_pairs={{0,2},{1,3},{2,4},{3,5},{4,6},{5,7},{6,0},{7,1},{8,10},{9,11},{10,... | collective-permute-start | bytes 589832 | tf_op jit(solution)/shard_map/ppermute | solution.py:485
  97.8 15.1 %collective-permute-start.15 = (bf16[128,1536]{1,0:T(8,128)(2,1)S(1)}, bf16[128,1536]{1,0:T(8,128)(2,1)S(1)}, u32[]{:S(2)}, u32[]{:S(2)}) collective-permute-start(bf16[128,1536]{1,0:T(8,128)(2,1)S(1)} %collective-permute-done.11.refs_5_), channel_id=1, source_target_pairs={{0,6},{1,7},{2,0},{3,1},{4,2},{5,3},{6,4},{7,5},{8,14},{9,15},{10,... | collective-permute-start | bytes 1179656 | tf_op jit(solution)/shard_map/ppermute | solution.py:485
  101.1 12.3 %collective-permute-start.14 = (bf16[128,1536]{1,0:T(8,128)(2,1)S(1)}, bf16[128,1536]{1,0:T(8,128)(2,1)S(1)}, u32[]{:S(2)}, u32[]{:S(2)}) collective-permute-start(bf16[128,1536]{1,0:T(8,128)(2,1)S(1)} %collective-permute-done.11.refs_5_), channel_id=1, source_target_pairs={{0,2},{1,3},{2,4},{3,5},{4,6},{5,7},{6,0},{7,1},{8,10},{9,11},{10,... | collective-permute-start | bytes 1179656 | tf_op jit(solution)/shard_map/ppermute | solution.py:485
  101.6 8.7 %collective-permute-start.17 = (bf16[64,1536]{1,0:T(8,128)(2,1)S(1)}, bf16[64,1536]{1,0:T(8,128)(2,1)S(1)}, u32[]{:S(2)}, u32[]{:S(2)}) collective-permute-start(bf16[64,1536]{1,0:T(8,128)(2,1)S(1)} %collective-permute-done.13.refs_4_), channel_id=1, source_target_pairs={{0,1},{1,0},{2,3},{3,2},{4,5},{5,4},{6,7},{7,6},{8,9},{9,8},{10,11... | collective-permute-start | bytes 589832 | tf_op jit(solution)/shard_map/ppermute | solution.py:489
  103.3 9.1 %collective-permute-start.16 = (bf16[64,1536]{1,0:T(8,128)(2,1)S(1)}, bf16[64,1536]{1,0:T(8,128)(2,1)S(1)}, u32[]{:S(2)}, u32[]{:S(2)}) collective-permute-start(bf16[64,1536]{1,0:T(8,128)(2,1)S(1)} %collective-permute-done.12.refs_3_), channel_id=1, source_target_pairs={{0,1},{1,0},{2,3},{3,2},{4,5},{5,4},{6,7},{7,6},{8,9},{9,8},{10,11... | collective-permute-start | bytes 589832 | tf_op jit(solution)/shard_map/ppermute | solution.py:489
  122.5 9.9 %collective-permute-start.21 = (bf16[128,1536]{1,0:T(8,128)(2,1)S(1)}, bf16[128,1536]{1,0:T(8,128)(2,1)}, u32[]{:S(2)}, u32[]{:S(2)}) collective-permute-start(bf16[128,1536]{1,0:T(8,128)(2,1)S(1)} %get-tuple-element.71), channel_id=1, source_target_pairs={{0,1},{1,0},{2,3},{3,2},{4,5},{5,4},{6,7},{7,6},{8,9},{9,8},{10,11... | collective-permute-start | bytes 1179656 | tf_op jit(solution)/shard_map/ppermute | solution.py:489
  127.5 13.9 %collective-permute-start.18 = (bf16[128,1536]{1,0:T(8,128)(2,1)}, bf16[128,1536]{1,0:T(8,128)(2,1)}, u32[]{:S(2)}, u32[]{:S(2)}) collective-permute-start(bf16[128,1536]{1,0:T(8,128)(2,1)} %get-tuple-element.67), channel_id=1, source_target_pairs={{0,6},{1,7},{2,0},{3,1},{4,2},{5,3},{6,4},{7,5},{8,14},{9,15},{10,... | collective-permute-start | bytes 1179656 | tf_op jit(solution)/shard_map/ppermute | solution.py:485
  130.5 11.0 %collective-permute-start.19 = (bf16[128,1536]{1,0:T(8,128)(2,1)}, bf16[128,1536]{1,0:T(8,128)(2,1)}, u32[]{:S(2)}, u32[]{:S(2)}) collective-permute-start(bf16[128,1536]{1,0:T(8,128)(2,1)} %get-tuple-element.68), channel_id=1, source_target_pairs={{0,2},{1,3},{2,4},{3,5},{4,6},{5,7},{6,0},{7,1},{8,10},{9,11},{10,... | collective-permute-start | bytes 1179656 | tf_op jit(solution)/shard_map/ppermute | solution.py:485
  138.1 6.9 %collective-permute-start.24 = (bf16[64,1536]{1,0:T(8,128)(2,1)S(1)}, bf16[64,1536]{1,0:T(8,128)(2,1)S(1)}, u32[]{:S(2)}, u32[]{:S(2)}) collective-permute-start(bf16[64,1536]{1,0:T(8,128)(2,1)S(1)} %get-tuple-element.93), channel_id=1, source_target_pairs={{0,2},{1,3},{2,4},{3,5},{4,6},{5,7},{6,0},{7,1},{8,10},{9,11},{10,... | collective-permute-start | bytes 589832 | tf_op jit(solution)/shard_map/ppermute | solution.py:485
  138.2 6.9 %collective-permute-start.22 = (bf16[64,1536]{1,0:T(8,128)(2,1)S(1)}, bf16[64,1536]{1,0:T(8,128)(2,1)S(1)}, u32[]{:S(2)}, u32[]{:S(2)}) collective-permute-start(bf16[64,1536]{1,0:T(8,128)(2,1)S(1)} %get-tuple-element.94), channel_id=1, source_target_pairs={{0,6},{1,7},{2,0},{3,1},{4,2},{5,3},{6,4},{7,5},{8,14},{9,15},{10,... | collective-permute-start | bytes 589832 | tf_op jit(solution)/shard_map/ppermute | solution.py:485
  142.6 10.0 %collective-permute-start.20 = (bf16[128,1536]{1,0:T(8,128)(2,1)S(1)}, bf16[128,1536]{1,0:T(8,128)(2,1)S(1)}, u32[]{:S(2)}, u32[]{:S(2)}) collective-permute-start(bf16[128,1536]{1,0:T(8,128)(2,1)S(1)} %add_add_fusion), channel_id=1, source_target_pairs={{0,1},{1,0},{2,3},{3,2},{4,5},{5,4},{6,7},{7,6},{8,9},{9,8},{10,11... | collective-permute-start | bytes 1179656 | tf_op jit(solution)/shard_map/ppermute | solution.py:489
  145.2 9.1 %collective-permute-start.25 = (bf16[128,1536]{1,0:T(8,128)(2,1)S(1)}, bf16[128,1536]{1,0:T(8,128)(2,1)S(1)}, u32[]{:S(2)}, u32[]{:S(2)}) collective-permute-start(bf16[128,1536]{1,0:T(8,128)(2,1)S(1)} %pad_maximum_fusion.1), channel_id=1, source_target_pairs={{0,2},{1,3},{2,4},{3,5},{4,6},{5,7},{6,0},{7,1},{8,10},{9,11},{10,... | collective-permute-start | bytes 1179656 | tf_op jit(solution)/shard_map/ppermute | solution.py:485
  146.5 8.1 %collective-permute-start.23 = (bf16[128,1536]{1,0:T(8,128)(2,1)S(1)}, bf16[128,1536]{1,0:T(8,128)(2,1)S(1)}, u32[]{:S(2)}, u32[]{:S(2)}) collective-permute-start(bf16[128,1536]{1,0:T(8,128)(2,1)S(1)} %pad_maximum_fusion), channel_id=1, source_target_pairs={{0,6},{1,7},{2,0},{3,1},{4,2},{5,3},{6,4},{7,5},{8,14},{9,15},{10,... | collective-permute-start | bytes 1179656 | tf_op jit(solution)/shard_map/ppermute | solution.py:485
  156.9 20.0 %all-to-all-start.1 = ((bf16[8,144,448]{2,1,0:T(8,128)(2,1)}), bf16[8,144,448]{2,1,0:T(8,128)(2,1)S(1)}, u32[]{:S(2)}, u32[]{:S(2)}) async-start(bf16[8,144,448]{2,1,0:T(8,128)(2,1)} %get-tuple-element.75), calls=%async_computation.1 | async-start | bytes 2359296 | tf_op jit(solution)/shard_map/all_to_all | solution.py:582
  181.1 1.8 collective-permute-start.26
  198.6 15.0 %all-to-all-start.3 = ((bf16[8,16,1536]{2,1,0:T(8,128)(2,1)}), bf16[8,16,1536]{2,1,0:T(8,128)(2,1)S(1)}, u32[]{:S(2)}, u32[]{:S(2)}) async-start(bf16[8,16,1536]{2,1,0:T(8,128)(2,1)} %fold.1), calls=%async_computation.3 | async-start | bytes 786432 | tf_op jit(solution)/shard_map/all_to_all | solution.py:589
  (24 other events, 201.2 us)
Sparse Core Ops, SparseCore 0:
  10.3 59.0 all-gather.1
  137.0 70.6 reduce-scatter.1

commit v4 on v3

--- a/solution.py
+++ b/solution.py
@@ -144,11 +144,27 @@
 OUT_BLOCK = 512
 
 
-def out_norm_kernel(mixed_ref, w_ref, in_ref, gain_ref, hidden_ref, normed_ref):
+PADDED = 256
+THREE = 3 * PADDED
+
+
+def widen(block, out_ref):
+    for j in range(3):
+        for h in range(3):
+            out_ref[:, j * PADDED + h * HDIM : j * PADDED + (h + 1) * HDIM] = block[
+                :, (h * 3 + j) * HDIM : (h * 3 + j + 1) * HDIM
+            ]
+        out_ref[:, j * PADDED + GROUP : (j + 1) * PADDED] = jnp.zeros(
+            (block.shape[0], PADDED - GROUP), BF
+        )
+
+
+def out_norm_kernel(mixed_ref, w_ref, in_ref, gain_ref, hidden_ref, normed_ref, wide_ref):
     step = pl.program_id(0)
-    block = in_ref[...].astype(F32) + dot_nt(mixed_ref[...], w_ref[...])
+    block = in_ref[...].astype(F32) + dot_nt(mixed_ref[...], w_ref[:, :WIDTH])
     start = pl.multiple_of(step * OUT_BLOCK, OUT_BLOCK)
     hidden_ref[:, pl.ds(start, OUT_BLOCK)] = block.astype(BF)
+    widen(w_ref[:, WIDTH:], wide_ref)
 
     @pl.when(step == pl.num_programs(0) - 1)
     def _():
@@ -157,52 +173,24 @@
         normed_ref[...] = (wide * inverse * gain_ref[...]).astype(BF)
 
 
-def out_norm(mixed, whole_out, inputs, gain):
+def out_norm(mixed, weights, inputs, gain):
     whole = pl.BlockSpec((TOK, WIDTH), lambda i: (0, 0))
     return pl.pallas_call(
         out_norm_kernel,
         grid=(WIDTH // OUT_BLOCK,),
         in_specs=[
             whole,
-            pl.BlockSpec((OUT_BLOCK, WIDTH), lambda i: (i, 0)),
+            pl.BlockSpec((OUT_BLOCK, weights.shape[1]), lambda i: (i, 0)),
             pl.BlockSpec((TOK, OUT_BLOCK), lambda i: (0, i)),
             pl.BlockSpec((1, WIDTH), lambda i: (0, 0)),
         ],
-        out_specs=[whole, whole],
-        out_shape=[jax.ShapeDtypeStruct((TOK, WIDTH), BF)] * 2,
-        compiler_params=params(),
+        out_specs=[whole, whole, pl.BlockSpec((OUT_BLOCK, THREE), lambda i: (i, 0))],
+        out_shape=[jax.ShapeDtypeStruct((TOK, WIDTH), BF)] * 2
+        + [jax.ShapeDtypeStruct((WIDTH, THREE), BF)],
+        compiler_params=params(58 * 1024 * 1024),
         name="out_norm",
-        cost_estimate=cost(4),
-    )(mixed, whole_out, inputs, gain)
-
-
-PADDED = 256
-THREE = 3 * PADDED
-
-
-def widen_kernel(w_ref, out_ref):
-    rows = w_ref.shape[0]
-    block = w_ref[...]
-    for j in range(3):
-        for h in range(3):
-            out_ref[:, j * PADDED + h * HDIM : j * PADDED + (h + 1) * HDIM] = block[
-                :, (h * 3 + j) * HDIM : (h * 3 + j + 1) * HDIM
-            ]
-        out_ref[:, j * PADDED + GROUP : (j + 1) * PADDED] = jnp.zeros((rows, PADDED - GROUP), BF)
-
-
-def widen(weights):
-    rows = 768
-    return pl.pallas_call(
-        widen_kernel,
-        grid=(WIDTH // rows,),
-        in_specs=[pl.BlockSpec((rows, THREE), lambda i: (i, WIDTH // THREE))],
-        out_specs=pl.BlockSpec((rows, THREE), lambda i: (i, 0)),
-        out_shape=jax.ShapeDtypeStruct((WIDTH, THREE), BF),
-        compiler_params=params(),
-        name="widen",
-        cost_estimate=cost(1.5),
-    )(weights)
+        cost_estimate=cost(5),
+    )(mixed, weights, inputs, gain)
 
 
 POS = 16
@@ -502,14 +490,11 @@
     )
 
 
-def gather_along_x(own):
-    behind, ahead, partner = along_x(own, 1), along_x(own, -1), across_y(own)
-    far_top, far_low = along_x(behind[:HALF], 1), along_x(ahead[HALF:], -1)
-    partner_behind, partner_ahead = along_x(partner, 1), along_x(partner, -1)
-    partner_top, partner_low = along_x(partner_behind[:HALF], 1), along_x(partner_ahead[HALF:], -1)
+def gather_by_x(own):
+    partner, behind, ahead, far = across_y(own), along_x(own, 1), along_x(own, -1), along_x(own, 2)
     return (
-        own, behind, ahead, far_top, far_low,
-        partner, partner_behind, partner_ahead, partner_top, partner_low,
+        own, behind, ahead, far,
+        partner, along_x(partner, 1), along_x(partner, -1), along_x(partner, 2),
     )
 
 
@@ -521,10 +506,8 @@
     )
 
 
-def scatter_frames(shares):
-    own, behind, ahead, far, partner, pbehind, pahead, far_share = shares
-    far = far + far_share
-    partner = partner + along_x(pbehind, -1) + along_x(pahead, 1)
+def scatter_frames(own, behind, ahead, far, partner, from_pbehind, from_pahead):
+    partner = partner + from_pbehind + from_pahead
     top, low = along_x(far[:HALF], -1), along_x(far[HALF:], 1)
     behind = jnp.concatenate([behind[:HALF] + top, behind[HALF:]], axis=0)
     ahead = jnp.concatenate([ahead[:HALF], ahead[HALF:] + low], axis=0)
@@ -553,30 +536,31 @@
         + [lax.axis_index("dp") % 2]
     ).astype(jnp.int32)
 
-    filler = jnp.zeros((out_weight.shape[0], THREE - 3 * GROUP), BF)
     weights = lax.all_gather(
-        jnp.concatenate([out_weight, qkv_weight, filler], axis=1), "dp", axis=0, tiled=True
+        jnp.concatenate([out_weight, qkv_weight], axis=1), "dp", axis=0, tiled=True
     )
     mixed = spatial_fwd(q, k, v)
     grad_heads = lax.all_to_all(
         dout.reshape(TOK, SEQ, GROUP).transpose(1, 0, 2), "seq", 0, 0, tiled=True
     )
-    mixed_parts = gather_along_x(mixed)
+    mixed_parts = gather_by_x(mixed)
     mixed_all = jnp.concatenate(mixed_parts, axis=0)
     weights, grad_heads, mixed_all = lax.optimization_barrier((weights, grad_heads, mixed_all))
-    hidden, normed = out_norm(mixed, weights, flat_in, gain)
+    hidden, normed, wide_proj = out_norm(mixed, weights, flat_in, gain)
     normed_parts = gather_frames(normed)
-    proj_weights, *first = lax.optimization_barrier((weights, *normed_parts[:3], normed_parts[5]))
-    frames = (*first[:3], *normed_parts[3:5], first[3], *normed_parts[6:])
-    wide_proj = widen(proj_weights)
-    proj = [dot_nn(f, wide_proj).astype(BF) for f in whole_frames(frames)]
+    proj = [dot_nn(f, wide_proj).astype(BF) for f in whole_frames(normed_parts)]
     heads_out, dproj = temporal(order, proj, grad_heads)
-    partner_shares = shares_of(dproj, wide_proj, 1)
-    *partner_shares, dproj = lax.optimization_barrier((*partner_shares, dproj))
-    far_share, dproj_later = lax.optimization_barrier((across_y(partner_shares[3]), dproj))
-    qkv_share = qkv_product(normed_parts, dproj_later, factor)
+    partner, pbehind, pahead, pfar = shares_of(dproj, wide_proj, 1)
+    partner, pbehind, pahead, pfar, dproj = lax.optimization_barrier(
+        (partner, pbehind, pahead, pfar, dproj)
+    )
+    qkv_share = qkv_product(normed_parts, dproj, factor)
     qkv_grad = lax.psum_scatter(qkv_share, "dp", scatter_dimension=0, tiled=True)
-    sums = scatter_frames((*shares_of(dproj, wide_proj, 0), *partner_shares[:3], far_share))
+    pfar, pbehind, pahead = lax.optimization_barrier(
+        (across_y(pfar), along_x(pbehind, -1), along_x(pahead, 1))
+    )
+    own, behind, ahead, far = shares_of(dproj, wide_proj, 0)
+    sums = scatter_frames(own, behind, ahead, far + pfar, partner, pbehind, pahead)
 
     grad_input, groups = grad_input_call(sums, hidden, resid, gain, heads_out, factor)
     groups = lax.all_to_all(groups, "seq", 0, 0, tiled=True)

time: 224 us -> 214 us (0.955)
  starting transfers between devices: 60.8 us -> 54 us
  local copies, waits for them, and re-layouts: 24.7 us -> 20.3 us
  waiting for transfers between devices: 65.1 us -> 60.7 us
  Pallas kernels: 36.4 us -> 39.1 us
    ppermute x6, waiting for transfers between devices: 23.4 us -> 6.87 us  [across_y(): return lax.ppermute(array, 'seq', [(i, i ^ 1) for i in range(SEQ)])]
    ppermute x20 -> x18, waiting for transfers between devices: 22.9 us -> 38.6 us  [along_x(): return lax.ppermute(array, 'seq', pairs)]
    unnamed x57 -> x71, local copies, waits for them, and re-layouts: 19.3 us -> 14.5 us
    ppermute x20 -> x18, starting transfers between devices: 32.8 us -> 28.4 us  [along_x(): return lax.ppermute(array, 'seq', pairs)]
    all_gather x1, waiting for transfers between devices: 6.45 us -> 2.58 us  [body(): lax.all_gather(jnp.concatenate([out_weight, qkv_weight], axis=1), 'dp', a...]
    pallas_call x1, Pallas kernels: 3.23 us -> 6.7 us  [out_norm(): pl.pallas_call(out_norm_kernel, grid=(WIDTH // OUT_BLOCK,), in_specs=[who...]
  transfers between devices with their start and end apart: 32 -> 30, of which waited for: 17 -> 18; matrix products, arithmetic and copies ran while one was open for 4% -> 7% of each run, Pallas kernels for 10% -> 10%
where the time goes in v4:
time: 214 us
  waiting for transfers between devices  60.7 us (28%)
  starting transfers between devices  54 us (25%)
  Pallas kernels  39.1 us (18%)
  local copies, waits for them, and re-layouts  20.3 us (9%)
  blocking collectives  14.7 us (7%)
  between operations  14.6 us (7%)
  matrix products  5.64 us (3%)
  other arithmetic  4.66 us (2%)
    ppermute x18, waiting for transfers between devices, along_x(): return lax.ppermute(array, 'seq', pairs)  38.6 us
    ppermute x18, starting transfers between devices, along_x(): return lax.ppermute(array, 'seq', pairs)  28.4 us
    all_to_all x1, blocking collectives, chip_exchange(): lax.all_to_all(blocks, 'dp', 0, 0, axis_index_groups=groups, tiled=True)  14.7 us
    unnamed x71, local copies, waits for them, and re-layouts  14.5 us
    ppermute x6, starting transfers between devices, across_y(): return lax.ppermute(array, 'seq', [(i, i ^ 1) for i in range(SEQ)])  12.8 us
    all_to_all x1, waiting for transfers between devices, body(): gathered = lax.all_to_all(fold(received), 'seq', 0, 0, tiled=True)  7.75 us
    pallas_call x1, Pallas kernels, spatial_bwd(): pl.pallas_call(spatial_bwd_kernel, grid=(WIDTH // (PAIRS * LANE),), in_sp...  7.64 us
    ppermute x6, waiting for transfers between devices, across_y(): return lax.ppermute(array, 'seq', [(i, i ^ 1) for i in range(SEQ)])  6.87 us
  transfers between devices with their start and end apart: 30, of which 18 were waited for; matrix products, arithmetic and copies ran while one was open for 7% of the time, Pallas kernels for 10%

profile of v4, /device:TPU:0, one launch (start us, length us, event | category | flops | bytes accessed | tf_op | source)
XLA Modules:
  0.0 213.7 jit_solution(8527344090344598798)
XLA Ops:
  12.1 2.8 %spatial_fwd.1.mixed_ref = bf16[128,1536]{1,0:T(8,128)(2,1)S(1)} custom-call(bf16[128,1536]{1,0:T(8,128)(2,1)S(1)} %bitcast.38, bf16[128,1536]{1,0:T(8,128)(2,1)S(1)} %bitcast.40, bf16[128,1536]{1,0:T(8,128)(2,1)S(1)} %bitcast.42), custom_call_target="tpu_custom_call" | custom-call | bytes 12000000 | tf_op jit(solution)/shard_map/spatial_fwd/pallas_call | solution.py:101
  14.9 3.4 %collective-permute-start.3 = (bf16[128,1536]{1,0:T(8,128)(2,1)S(1)}, bf16[128,1536]{1,0:T(8,128)(2,1)S(1)}, u32[]{:S(2)}, u32[]{:S(2)}) collective-permute-start(bf16[128,1536]{1,0:T(8,128)(2,1)S(1)} %spatial_fwd.1.mixed_ref), channel_id=1, source_target_pairs={{0,1},{1,0},{2,3},{3,2},{4,5},{5,4},{6,7},{7,6},{8,9},{9,8},{10,11... | collective-permute-start | bytes 1179656 | tf_op jit(solution)/shard_map/ppermute | solution.py:477
  24.9 3.5 %all-to-all-start = ((bf16[8,128,192]{1,2,0:T(8,128)(2,1)}), bf16[8,128,192]{1,2,0:T(8,128)(2,1)S(1)}, u32[]{:S(2)}, u32[]{:S(2)}) async-start(bf16[8,128,192]{1,2,0:T(8,128)(2,1)} %copy.20), calls=%async_computation | async-start | bytes 786432 | tf_op jit(solution)/shard_map/all_to_all | solution.py:543
  29.1 4.7 %collective-permute-done.3 = bf16[128,1536]{1,0:T(8,128)(2,1)S(1)} collective-permute-done((bf16[128,1536]{1,0:T(8,128)(2,1)S(1)}, bf16[128,1536]{1,0:T(8,128)(2,1)S(1)}, u32[]{:S(2)}, u32[]{:S(2)}) %collective-permute-start.3) | collective-permute-done | bytes 393248 | tf_op jit(solution)/shard_map/ppermute | solution.py:477
  37.0 3.2 %collective-permute-start.6 = (bf16[128,1536]{1,0:T(8,128)(2,1)S(1)}, bf16[128,1536]{1,0:T(8,128)(2,1)S(1)}, u32[]{:S(2)}, u32[]{:S(2)}) collective-permute-start(bf16[128,1536]{1,0:T(8,128)(2,1)S(1)} %collective-permute-done.3), channel_id=1, source_target_pairs={{0,4},{1,5},{2,6},{3,7},{4,0},{5,1},{6,2},{7,3},{8,12},{9,13},{10,... | collective-permute-start | bytes 1179656 | tf_op jit(solution)/shard_map/ppermute | solution.py:473
  41.1 11.0 %collective-permute-done.4 = bf16[128,1536]{1,0:T(8,128)(2,1)S(1)} collective-permute-done((bf16[128,1536]{1,0:T(8,128)(2,1)S(1)}, bf16[128,1536]{1,0:T(8,128)(2,1)S(1)}, u32[]{:S(2)}, u32[]{:S(2)}) %collective-permute-start.4) | collective-permute-done | bytes 393248 | tf_op jit(solution)/shard_map/ppermute | solution.py:473
  53.0 7.6 %collective-permute-done.6 = bf16[128,1536]{1,0:T(8,128)(2,1)S(1)} collective-permute-done((bf16[128,1536]{1,0:T(8,128)(2,1)S(1)}, bf16[128,1536]{1,0:T(8,128)(2,1)S(1)}, u32[]{:S(2)}, u32[]{:S(2)}) %collective-permute-start.6) | collective-permute-done | bytes 393248 | tf_op jit(solution)/shard_map/ppermute | solution.py:473
  62.4 2.6 %all-gather.2.cloned.1.call-done.w_ref = bf16[1536,2112]{1,0:T(8,128)(2,1)} async-done(((bf16[96,2112]{1,0:T(8,128)(2,1)}), bf16[1536,2112]{1,0:T(8,128)(2,1)}) %all-gather.2.cloned.1.call-update) | async-done | bytes 6488080 | tf_op jit(solution)/shard_map/all_gather | solution.py:539
  65.0 6.7 %out_norm.1 = (bf16[128,1536]{1,0:T(8,128)(2,1)}, bf16[128,1536]{1,0:T(8,128)(2,1)}, bf16[1536,768]{1,0:T(8,128)(2,1)}) custom-call(bf16[128,1536]{1,0:T(8,128)(2,1)} %copy-done.4, bf16[1536,2112]{1,0:T(8,128)(2,1)} %all-gather.2.cloned.1.call-done.w_ref, bf16[128,1536]{1,0:T(8,128)(2,1)} %bitcast.48, f32[1,1536]{1,0:T(1,128)} %reshape.55.gain_ref), custom_call_target="tpu_custom_call" | custom-call | bytes 15000000 | tf_op jit(solution)/shard_map/out_norm/pallas_call | solution.py:178
  71.7 2.8 %collective-permute-start.8 = (bf16[128,1536]{1,0:T(8,128)(2,1)}, bf16[128,1536]{1,0:T(8,128)(2,1)S(1)}, u32[]{:S(2)}, u32[]{:S(2)}) collective-permute-start(bf16[128,1536]{1,0:T(8,128)(2,1)} %get-tuple-element.49.refs_0_), channel_id=1, source_target_pairs={{0,6},{1,7},{2,0},{3,1},{4,2},{5,3},{6,4},{7,5},{8,14},{9,15},{10,... | collective-permute-start | bytes 1179656 | tf_op jit(solution)/shard_map/ppermute | solution.py:473
  78.4 2.3 %convolution_convert_fusion.7.refs_0_ = bf16[128,768]{1,0:T(8,128)(2,1)S(1)} fusion(bf16[128,1536]{1,0:T(8,128)(2,1)} %get-tuple-element.49.refs_0_, bf16[1536,768]{1,0:T(8,128)(2,1)} %get-tuple-element.50.w_ref), kind=kOutput, calls=%fused_computation.7 | convolution fusion | flops 302088192 | bytes 2949120 | tf_op jit(solution)/shard_map/dot_general | solution.py:44
  80.7 2.9 %collective-permute-done.8.refs_2_ = bf16[128,1536]{1,0:T(8,128)(2,1)S(1)} collective-permute-done((bf16[128,1536]{1,0:T(8,128)(2,1)}, bf16[128,1536]{1,0:T(8,128)(2,1)S(1)}, u32[]{:S(2)}, u32[]{:S(2)}) %collective-permute-start.8) | collective-permute-done | bytes 393248 | tf_op jit(solution)/shard_map/ppermute | solution.py:473
  83.6 3.7 %collective-permute-start.10 = (bf16[64,1536]{1,0:T(8,128)(2,1)S(1)}, bf16[64,1536]{1,0:T(8,128)(2,1)S(1)}, u32[]{:S(2)}, u32[]{:S(2)}) collective-permute-start(bf16[64,1536]{1,0:T(8,128)(2,1)S(1)} %slice.37), channel_id=1, source_target_pairs={{0,6},{1,7},{2,0},{3,1},{4,2},{5,3},{6,4},{7,5},{8,14},{9,15},{10,... | collective-permute-start | bytes 589832 | tf_op jit(solution)/shard_map/ppermute | solution.py:473
  88.9 3.3 %collective-permute-start.13 = (bf16[128,1536]{1,0:T(8,128)(2,1)S(1)}, bf16[128,1536]{1,0:T(8,128)(2,1)S(1)}, u32[]{:S(2)}, u32[]{:S(2)}) collective-permute-start(bf16[128,1536]{1,0:T(8,128)(2,1)S(1)} %collective-permute-done.11.refs_5_), channel_id=1, source_target_pairs={{0,6},{1,7},{2,0},{3,1},{4,2},{5,3},{6,4},{7,5},{8,14},{9,15},{10,... | collective-permute-start | bytes 1179656 | tf_op jit(solution)/shard_map/ppermute | solution.py:473
  94.0 2.3 %collective-permute-done.9.refs_3_ = bf16[64,1536]{1,0:T(8,128)(2,1)S(1)} collective-permute-done((bf16[64,1536]{1,0:T(8,128)(2,1)S(1)}, bf16[64,1536]{1,0:T(8,128)(2,1)S(1)}, u32[]{:S(2)}, u32[]{:S(2)}) %collective-permute-start.9) | collective-permute-done | bytes 196640 | tf_op jit(solution)/shard_map/ppermute | solution.py:473
  96.9 2.1 collective-permute-start.14
  98.9 4.0 %collective-permute-done.12.refs_6_ = bf16[128,1536]{1,0:T(8,128)(2,1)S(1)} collective-permute-done((bf16[128,1536]{1,0:T(8,128)(2,1)S(1)}, bf16[128,1536]{1,0:T(8,128)(2,1)S(1)}, u32[]{:S(2)}, u32[]{:S(2)}) %collective-permute-start.12) | collective-permute-done | bytes 393248 | tf_op jit(solution)/shard_map/ppermute | solution.py:473
  104.8 5.9 %temporal.1 = (bf16[8,128,192]{2,1,0:T(8,128)(2,1)S(1)}, bf16[8,128,768]{2,1,0:T(8,128)(2,1)S(1)}) custom-call(s32[9]{0:T(128)S(1)} %stack.39.order_ref, bf16[128,768]{1,0:T(8,128)(2,1)S(1)} %convolution_convert_fusion.7.refs_0_, bf16[128,768]{1,0:T(8,128)(2,1)S(1)} %convolution_convert_fusion.6.refs_1_, ...), custom_call_target="tpu_custom_call" | custom-call | bytes 24000000 | tf_op jit(solution)/shard_map/temporal/pallas_call | solution.py:243
  110.7 2.8 %shares.2 = (bf16[128,1536]{1,0:T(8,128)(2,1)S(1)}, bf16[128,1536]{1,0:T(8,128)(2,1)}, bf16[128,1536]{1,0:T(8,128)(2,1)}, bf16[128,1536]{1,0:T(8,128)(2,1)}) custom-call(bf16[8,128,768]{2,1,0:T(8,128)(2,1)S(1)} %get-tuple-element.57.dproj_ref.refs_10_, bf16[1536,768]{1,0:T(8,128)(2,1)S(1)} %copy-done), custom_call_target="tpu_custom_call" | custom-call | bytes 6000000 | tf_op jit(solution)/shard_map/shares/pallas_call | solution.py:273
  123.1 4.4 %qkv_product.1 = bf16[1536,576]{1,0:T(8,128)(2,1)} custom-call(bf16[128,1536]{1,0:T(8,128)(2,1)S(1)} %copy-done.12, bf16[128,1536]{1,0:T(8,128)(2,1)S(1)} %collective-permute-done.7.refs_1_, bf16[128,1536]{1,0:T(8,128)(2,1)S(1)} %collective-permute-done.8.refs_2_, bf16[64,1536]{1,0:T(8,128)(2,1)S(1)} %collective-permute-done.9.refs_3_, ...), custom_call_target="tpu_custom_call" | custom-call | bytes 15000000 | tf_op jit(solution)/shard_map/qkv_product/pallas_call | solution.py:304
  128.9 2.8 %collective-permute-start.20 = (bf16[64,1536]{1,0:T(8,128)(2,1)S(1)}, bf16[64,1536]{1,0:T(8,128)(2,1)S(1)}, u32[]{:S(2)}, u32[]{:S(2)}) collective-permute-start(bf16[64,1536]{1,0:T(8,128)(2,1)S(1)} %get-tuple-element.88), channel_id=1, source_target_pairs={{0,6},{1,7},{2,0},{3,1},{4,2},{5,3},{6,4},{7,5},{8,14},{9,15},{10,... | collective-permute-start | bytes 589832 | tf_op jit(solution)/shard_map/ppermute | solution.py:473
  135.0 4.0 %collective-permute-done.22 = bf16[64,1536]{1,0:T(8,128)(2,1)S(1)} collective-permute-done((bf16[64,1536]{1,0:T(8,128)(2,1)S(1)}, bf16[64,1536]{1,0:T(8,128)(2,1)S(1)}, u32[]{:S(2)}, u32[]{:S(2)}) %collective-permute-start.22) | collective-permute-done | bytes 196640 | tf_op jit(solution)/shard_map/ppermute | solution.py:473
  143.1 3.8 %collective-permute-done.21.sum_c = bf16[128,1536]{1,0:T(8,128)(2,1)S(1)} collective-permute-done((bf16[128,1536]{1,0:T(8,128)(2,1)S(1)}, bf16[128,1536]{1,0:T(8,128)(2,1)S(1)}, u32[]{:S(2)}, u32[]{:S(2)}) %collective-permute-start.21) | collective-permute-done | bytes 393248 | tf_op jit(solution)/shard_map/ppermute | solution.py:473
  148.4 2.3 %grad_input.1 = (bf16[128,1536]{1,0:T(8,128)(2,1)}, bf16[8,144,448]{2,1,0:T(8,128)(2,1)}) custom-call(bf16[128,1536]{1,0:T(8,128)(2,1)S(1)} %copy-done.19, bf16[128,1536]{1,0:T(8,128)(2,1)S(1)} %collective-permute-done.19.sum_b, bf16[128,1536]{1,0:T(8,128)(2,1)S(1)} %collective-permute-done.21.sum_c, bf16[128,1536]{1,0:T(8,128)(2,1)S(1)} %collective-permute-done.23.sum_d, ...), custom_call_target="tpu_custom_call" | custom-call | bytes 6000000 | tf_op jit(solution)/shard_map/grad_input/pallas_call | solution.py:368
  150.7 3.9 %all-to-all-start.1 = ((bf16[8,144,448]{2,1,0:T(8,128)(2,1)}), bf16[8,144,448]{2,1,0:T(8,128)(2,1)S(1)}, u32[]{:S(2)}, u32[]{:S(2)}) async-start(bf16[8,144,448]{2,1,0:T(8,128)(2,1)} %get-tuple-element.70), calls=%async_computation.1 | async-start | bytes 2359296 | tf_op jit(solution)/shard_map/all_to_all | solution.py:566
  154.6 2.9 %copy-done.1 = bf16[1536,2112]{1,0:T(8,128)(2,1)S(1)} copy-done((bf16[1536,2112]{1,0:T(8,128)(2,1)S(1)}, bf16[1536,2112]{1,0:T(8,128)(2,1)}, u32[]{:S(2)}) %copy-start.1) | copy-done | bytes 6488088
  157.5 7.6 %spatial_bwd.1 = (bf16[128,1536]{1,0:T(8,128)(2,1)}, bf16[128,1536]{1,0:T(8,128)(2,1)}, bf16[128,1536]{1,0:T(8,128)(2,1)}) custom-call(bf16[128,1536]{1,0:T(8,128)(2,1)S(1)} %copy-done.15, bf16[1536,2112]{1,0:T(8,128)(2,1)S(1)} %copy-done.1, bf16[128,1536]{1,0:T(8,128)(2,1)S(1)} %bitcast.39, bf16[128,1536]{1,0:T(8,128)(2,1)S(1)} %bitcast.41, ...), custom_call_target="tpu_custom_call" | custom-call | bytes 27000000 | tf_op jit(solution)/shard_map/spatial_bwd/pallas_call | solution.py:128
  165.2 3.1 %all-to-all-done.1.groups_ref = bf16[8,144,448]{2,1,0:T(8,128)(2,1)S(1)} async-done(((bf16[8,144,448]{2,1,0:T(8,128)(2,1)}), bf16[8,144,448]{2,1,0:T(8,128)(2,1)S(1)}, u32[]{:S(2)}, u32[]{:S(2)}) %all-to-all-start.1) | async-done | bytes 1032224 | tf_op jit(solution)/shard_map/all_to_all | solution.py:566
  170.2 2.3 %out_product.1 = (bf16[8,16,1536]{2,1,0:T(8,128)(2,1)S(1)}, bf16[8,16,1536]{2,1,0:T(8,128)(2,1)S(1)}) custom-call(s32[9]{0:T(128)S(1)} %stack.39.order_ref, bf16[8,144,448]{2,1,0:T(8,128)(2,1)S(1)} %all-to-all-done.1.groups_ref, bf16[1024,1536]{1,0:T(8,128)(2,1)S(1)} %copy-done.3), custom_call_target="tpu_custom_call" | custom-call | bytes 9000000 | tf_op jit(solution)/shard_map/out_product/pallas_call | solution.py:402
  174.4 14.7 %all_to_all.20.in_ref = bf16[8,16,1536]{2,1,0:T(8,128)(2,1)S(1)} all-to-all(bf16[8,16,1536]{2,1,0:T(8,128)(2,1)S(1)} %add.102), channel_id=1, replica_groups={{0,16,32,48,64,80,96,112},{8,24,40,56,72,88,104,120},{1,17,33,49,65,81,..., dimensions={0} | all-to-all | bytes 786432 | tf_op jit(solution)/shard_map/all_to_all | solution.py:519
  189.9 5.3 %all-to-all-start.3 = ((bf16[8,16,1536]{2,1,0:T(8,128)(2,1)}), bf16[8,16,1536]{2,1,0:T(8,128)(2,1)S(1)}, u32[]{:S(2)}, u32[]{:S(2)}) async-start(bf16[8,16,1536]{2,1,0:T(8,128)(2,1)} %fold.1), calls=%async_computation.3 | async-start | bytes 786432 | tf_op jit(solution)/shard_map/all_to_all | solution.py:573
  196.7 7.7 %all-to-all-done.3.in_ref = bf16[8,16,1536]{2,1,0:T(8,128)(2,1)S(1)} async-done(((bf16[8,16,1536]{2,1,0:T(8,128)(2,1)}), bf16[8,16,1536]{2,1,0:T(8,128)(2,1)S(1)}, u32[]{:S(2)}, u32[]{:S(2)}) %all-to-all-start.3) | async-done | bytes 393248 | tf_op jit(solution)/shard_map/all_to_all | solution.py:573
  (140 shorter events, 56.7 us)
Async XLA Ops:
  7.2 57.8 %all-gather.2.cloned.1.call-start = ((), (), s32[]{:S(2)}) async-start(), calls=%async_computation.5 | async-start | bytes 7102464 | tf_op jit(solution)/shard_map/all_gather | solution.py:539
  9.1 19.4 %copy-start.31 = (f32[1536]{0:T(1024)S(1)}, f32[1536]{0:T(1024)}, u32[]{:S(2)}) copy-start(f32[1536]{0:T(1024)} %param.14) | copy-start | bytes 18436
  14.9 25.6 %copy-start.4 = (bf16[128,1536]{1,0:T(8,128)(2,1)}, bf16[128,1536]{1,0:T(8,128)(2,1)S(1)}, u32[]{:S(2)}) copy-start(bf16[128,1536]{1,0:T(8,128)(2,1)S(1)} %spatial_fwd.1.mixed_ref) | copy-start | bytes 1179652
  14.9 18.8 %collective-permute-start.3 = (bf16[128,1536]{1,0:T(8,128)(2,1)S(1)}, bf16[128,1536]{1,0:T(8,128)(2,1)S(1)}, u32[]{:S(2)}, u32[]{:S(2)}) collective-permute-start(bf16[128,1536]{1,0:T(8,128)(2,1)S(1)} %spatial_fwd.1.mixed_ref), channel_id=1, source_target_pairs={{0,1},{1,0},{2,3},{3,2},{4,5},{5,4},{6,7},{7,6},{8,9},{9,8},{10,11... | collective-permute-start | bytes 1179656 | tf_op jit(solution)/shard_map/ppermute | solution.py:477
  18.3 18.7 %collective-permute-start = (bf16[128,1536]{1,0:T(8,128)(2,1)S(1)}, bf16[128,1536]{1,0:T(8,128)(2,1)S(1)}, u32[]{:S(2)}, u32[]{:S(2)}) collective-permute-start(bf16[128,1536]{1,0:T(8,128)(2,1)S(1)} %spatial_fwd.1.mixed_ref), channel_id=1, source_target_pairs={{0,2},{1,3},{2,4},{3,5},{4,6},{5,7},{6,0},{7,1},{8,10},{9,11},{10,... | collective-permute-start | bytes 1179656 | tf_op jit(solution)/shard_map/ppermute | solution.py:473
  19.8 20.7 %collective-permute-start.1 = (bf16[128,1536]{1,0:T(8,128)(2,1)S(1)}, bf16[128,1536]{1,0:T(8,128)(2,1)S(1)}, u32[]{:S(2)}, u32[]{:S(2)}) collective-permute-start(bf16[128,1536]{1,0:T(8,128)(2,1)S(1)} %spatial_fwd.1.mixed_ref), channel_id=1, source_target_pairs={{0,6},{1,7},{2,0},{3,1},{4,2},{5,3},{6,4},{7,5},{8,14},{9,15},{10,... | collective-permute-start | bytes 1179656 | tf_op jit(solution)/shard_map/ppermute | solution.py:473
  21.5 19.5 %collective-permute-start.2 = (bf16[128,1536]{1,0:T(8,128)(2,1)S(1)}, bf16[128,1536]{1,0:T(8,128)(2,1)S(1)}, u32[]{:S(2)}, u32[]{:S(2)}) collective-permute-start(bf16[128,1536]{1,0:T(8,128)(2,1)S(1)} %spatial_fwd.1.mixed_ref), channel_id=1, source_target_pairs={{0,4},{1,5},{2,6},{3,7},{4,0},{5,1},{6,2},{7,3},{8,12},{9,13},{10,... | collective-permute-start | bytes 1179656 | tf_op jit(solution)/shard_map/ppermute | solution.py:473
  24.9 37.5 %all-to-all-start = ((bf16[8,128,192]{1,2,0:T(8,128)(2,1)}), bf16[8,128,192]{1,2,0:T(8,128)(2,1)S(1)}, u32[]{:S(2)}, u32[]{:S(2)}) async-start(bf16[8,128,192]{1,2,0:T(8,128)(2,1)} %copy.20), calls=%async_computation | async-start | bytes 786432 | tf_op jit(solution)/shard_map/all_to_all | solution.py:543
  28.4 176.1 %reduce-scatter.2.cloned.1.call-start = ((), (), s32[]{:S(2)}) async-start(), calls=%async_computation.6 | async-start | bytes 2088960 | tf_op jit(solution)/shard_map/reduce_scatter | solution.py:558
  33.8 18.3 %collective-permute-start.4 = (bf16[128,1536]{1,0:T(8,128)(2,1)S(1)}, bf16[128,1536]{1,0:T(8,128)(2,1)S(1)}, u32[]{:S(2)}, u32[]{:S(2)}) collective-permute-start(bf16[128,1536]{1,0:T(8,128)(2,1)S(1)} %collective-permute-done.3), channel_id=1, source_target_pairs={{0,2},{1,3},{2,4},{3,5},{4,6},{5,7},{6,0},{7,1},{8,10},{9,11},{10,... | collective-permute-start | bytes 1179656 | tf_op jit(solution)/shard_map/ppermute | solution.py:473
  35.1 17.9 %collective-permute-start.5 = (bf16[128,1536]{1,0:T(8,128)(2,1)S(1)}, bf16[128,1536]{1,0:T(8,128)(2,1)S(1)}, u32[]{:S(2)}, u32[]{:S(2)}) collective-permute-start(bf16[128,1536]{1,0:T(8,128)(2,1)S(1)} %collective-permute-done.3), channel_id=1, source_target_pairs={{0,6},{1,7},{2,0},{3,1},{4,2},{5,3},{6,4},{7,5},{8,14},{9,15},{10,... | collective-permute-start | bytes 1179656 | tf_op jit(solution)/shard_map/ppermute | solution.py:473
  37.0 23.6 %collective-permute-start.6 = (bf16[128,1536]{1,0:T(8,128)(2,1)S(1)}, bf16[128,1536]{1,0:T(8,128)(2,1)S(1)}, u32[]{:S(2)}, u32[]{:S(2)}) collective-permute-start(bf16[128,1536]{1,0:T(8,128)(2,1)S(1)} %collective-permute-done.3), channel_id=1, source_target_pairs={{0,4},{1,5},{2,6},{3,7},{4,0},{5,1},{6,2},{7,3},{8,12},{9,13},{10,... | collective-permute-start | bytes 1179656 | tf_op jit(solution)/shard_map/ppermute | solution.py:473
  71.7 11.9 %collective-permute-start.8 = (bf16[128,1536]{1,0:T(8,128)(2,1)}, bf16[128,1536]{1,0:T(8,128)(2,1)S(1)}, u32[]{:S(2)}, u32[]{:S(2)}) collective-permute-start(bf16[128,1536]{1,0:T(8,128)(2,1)} %get-tuple-element.49.refs_0_), channel_id=1, source_target_pairs={{0,6},{1,7},{2,0},{3,1},{4,2},{5,3},{6,4},{7,5},{8,14},{9,15},{10,... | collective-permute-start | bytes 1179656 | tf_op jit(solution)/shard_map/ppermute | solution.py:473
  74.4 12.8 %collective-permute-start.7 = (bf16[128,1536]{1,0:T(8,128)(2,1)}, bf16[128,1536]{1,0:T(8,128)(2,1)S(1)}, u32[]{:S(2)}, u32[]{:S(2)}) collective-permute-start(bf16[128,1536]{1,0:T(8,128)(2,1)} %get-tuple-element.49.refs_0_), channel_id=1, source_target_pairs={{0,2},{1,3},{2,4},{3,5},{4,6},{5,7},{6,0},{7,1},{8,10},{9,11},{10,... | collective-permute-start | bytes 1179656 | tf_op jit(solution)/shard_map/ppermute | solution.py:473
  74.5 13.8 %collective-permute-start.11 = (bf16[128,1536]{1,0:T(8,128)(2,1)}, bf16[128,1536]{1,0:T(8,128)(2,1)S(1)}, u32[]{:S(2)}, u32[]{:S(2)}) collective-permute-start(bf16[128,1536]{1,0:T(8,128)(2,1)} %get-tuple-element.49.refs_0_), channel_id=1, source_target_pairs={{0,1},{1,0},{2,3},{3,2},{4,5},{5,4},{6,7},{7,6},{8,9},{9,8},{10,11... | collective-permute-start | bytes 1179656 | tf_op jit(solution)/shard_map/ppermute | solution.py:477
  83.6 8.6 %collective-permute-start.10 = (bf16[64,1536]{1,0:T(8,128)(2,1)S(1)}, bf16[64,1536]{1,0:T(8,128)(2,1)S(1)}, u32[]{:S(2)}, u32[]{:S(2)}) collective-permute-start(bf16[64,1536]{1,0:T(8,128)(2,1)S(1)} %slice.37), channel_id=1, source_target_pairs={{0,6},{1,7},{2,0},{3,1},{4,2},{5,3},{6,4},{7,5},{8,14},{9,15},{10,... | collective-permute-start | bytes 589832 | tf_op jit(solution)/shard_map/ppermute | solution.py:473
  87.2 9.1 %collective-permute-start.9 = (bf16[64,1536]{1,0:T(8,128)(2,1)S(1)}, bf16[64,1536]{1,0:T(8,128)(2,1)S(1)}, u32[]{:S(2)}, u32[]{:S(2)}) collective-permute-start(bf16[64,1536]{1,0:T(8,128)(2,1)S(1)} %slice.36), channel_id=1, source_target_pairs={{0,2},{1,3},{2,4},{3,5},{4,6},{5,7},{6,0},{7,1},{8,10},{9,11},{10,... | collective-permute-start | bytes 589832 | tf_op jit(solution)/shard_map/ppermute | solution.py:473
  88.3 14.6 %collective-permute-start.12 = (bf16[128,1536]{1,0:T(8,128)(2,1)S(1)}, bf16[128,1536]{1,0:T(8,128)(2,1)S(1)}, u32[]{:S(2)}, u32[]{:S(2)}) collective-permute-start(bf16[128,1536]{1,0:T(8,128)(2,1)S(1)} %collective-permute-done.11.refs_5_), channel_id=1, source_target_pairs={{0,2},{1,3},{2,4},{3,5},{4,6},{5,7},{6,0},{7,1},{8,10},{9,11},{10,... | collective-permute-start | bytes 1179656 | tf_op jit(solution)/shard_map/ppermute | solution.py:473
  88.9 14.5 %collective-permute-start.13 = (bf16[128,1536]{1,0:T(8,128)(2,1)S(1)}, bf16[128,1536]{1,0:T(8,128)(2,1)S(1)}, u32[]{:S(2)}, u32[]{:S(2)}) collective-permute-start(bf16[128,1536]{1,0:T(8,128)(2,1)S(1)} %collective-permute-done.11.refs_5_), channel_id=1, source_target_pairs={{0,6},{1,7},{2,0},{3,1},{4,2},{5,3},{6,4},{7,5},{8,14},{9,15},{10,... | collective-permute-start | bytes 1179656 | tf_op jit(solution)/shard_map/ppermute | solution.py:473
  92.2 11.7 %collective-permute-start.15 = (bf16[64,1536]{1,0:T(8,128)(2,1)S(1)}, bf16[64,1536]{1,0:T(8,128)(2,1)S(1)}, u32[]{:S(2)}, u32[]{:S(2)}) collective-permute-start(bf16[64,1536]{1,0:T(8,128)(2,1)S(1)} %collective-permute-done.10.refs_4_), channel_id=1, source_target_pairs={{0,1},{1,0},{2,3},{3,2},{4,5},{5,4},{6,7},{7,6},{8,9},{9,8},{10,11... | collective-permute-start | bytes 589832 | tf_op jit(solution)/shard_map/ppermute | solution.py:477
  96.9 7.4 %collective-permute-start.14 = (bf16[64,1536]{1,0:T(8,128)(2,1)S(1)}, bf16[64,1536]{1,0:T(8,128)(2,1)S(1)}, u32[]{:S(2)}, u32[]{:S(2)}) collective-permute-start(bf16[64,1536]{1,0:T(8,128)(2,1)S(1)} %collective-permute-done.9.refs_3_), channel_id=1, source_target_pairs={{0,1},{1,0},{2,3},{3,2},{4,5},{5,4},{6,7},{7,6},{8,9},{9,8},{10,11... | collective-permute-start | bytes 589832 | tf_op jit(solution)/shard_map/ppermute | solution.py:477
  114.2 13.3 %collective-permute-start.16 = (bf16[128,1536]{1,0:T(8,128)(2,1)}, bf16[128,1536]{1,0:T(8,128)(2,1)}, u32[]{:S(2)}, u32[]{:S(2)}) collective-permute-start(bf16[128,1536]{1,0:T(8,128)(2,1)} %get-tuple-element.60), channel_id=1, source_target_pairs={{0,1},{1,0},{2,3},{3,2},{4,5},{5,4},{6,7},{7,6},{8,9},{9,8},{10,11... | collective-permute-start | bytes 1179656 | tf_op jit(solution)/shard_map/ppermute | solution.py:477
  116.1 11.5 %collective-permute-start.17 = (bf16[128,1536]{1,0:T(8,128)(2,1)}, bf16[128,1536]{1,0:T(8,128)(2,1)}, u32[]{:S(2)}, u32[]{:S(2)}) collective-permute-start(bf16[128,1536]{1,0:T(8,128)(2,1)} %get-tuple-element.61), channel_id=1, source_target_pairs={{0,6},{1,7},{2,0},{3,1},{4,2},{5,3},{6,4},{7,5},{8,14},{9,15},{10,... | collective-permute-start | bytes 1179656 | tf_op jit(solution)/shard_map/ppermute | solution.py:473
  117.6 10.0 %collective-permute-start.18 = (bf16[128,1536]{1,0:T(8,128)(2,1)}, bf16[128,1536]{1,0:T(8,128)(2,1)}, u32[]{:S(2)}, u32[]{:S(2)}) collective-permute-start(bf16[128,1536]{1,0:T(8,128)(2,1)} %get-tuple-element.62), channel_id=1, source_target_pairs={{0,2},{1,3},{2,4},{3,5},{4,6},{5,7},{6,0},{7,1},{8,10},{9,11},{10,... | collective-permute-start | bytes 1179656 | tf_op jit(solution)/shard_map/ppermute | solution.py:473
  128.9 6.0 %collective-permute-start.20 = (bf16[64,1536]{1,0:T(8,128)(2,1)S(1)}, bf16[64,1536]{1,0:T(8,128)(2,1)S(1)}, u32[]{:S(2)}, u32[]{:S(2)}) collective-permute-start(bf16[64,1536]{1,0:T(8,128)(2,1)S(1)} %get-tuple-element.88), channel_id=1, source_target_pairs={{0,6},{1,7},{2,0},{3,1},{4,2},{5,3},{6,4},{7,5},{8,14},{9,15},{10,... | collective-permute-start | bytes 589832 | tf_op jit(solution)/shard_map/ppermute | solution.py:473
  131.7 7.3 %collective-permute-start.22 = (bf16[64,1536]{1,0:T(8,128)(2,1)S(1)}, bf16[64,1536]{1,0:T(8,128)(2,1)S(1)}, u32[]{:S(2)}, u32[]{:S(2)}) collective-permute-start(bf16[64,1536]{1,0:T(8,128)(2,1)S(1)} %get-tuple-element.87), channel_id=1, source_target_pairs={{0,2},{1,3},{2,4},{3,5},{4,6},{5,7},{6,0},{7,1},{8,10},{9,11},{10,... | collective-permute-start | bytes 589832 | tf_op jit(solution)/shard_map/ppermute | solution.py:473
  133.1 10.0 %collective-permute-start.19 = (bf16[128,1536]{1,0:T(8,128)(2,1)S(1)}, bf16[128,1536]{1,0:T(8,128)(2,1)S(1)}, u32[]{:S(2)}, u32[]{:S(2)}) collective-permute-start(bf16[128,1536]{1,0:T(8,128)(2,1)S(1)} %add_add_fusion), channel_id=1, source_target_pairs={{0,1},{1,0},{2,3},{3,2},{4,5},{5,4},{6,7},{7,6},{8,9},{9,8},{10,11... | collective-permute-start | bytes 1179656 | tf_op jit(solution)/shard_map/ppermute | solution.py:477
  139.1 7.8 %collective-permute-start.21 = (bf16[128,1536]{1,0:T(8,128)(2,1)S(1)}, bf16[128,1536]{1,0:T(8,128)(2,1)S(1)}, u32[]{:S(2)}, u32[]{:S(2)}) collective-permute-start(bf16[128,1536]{1,0:T(8,128)(2,1)S(1)} %pad_maximum_fusion.1), channel_id=1, source_target_pairs={{0,6},{1,7},{2,0},{3,1},{4,2},{5,3},{6,4},{7,5},{8,14},{9,15},{10,... | collective-permute-start | bytes 1179656 | tf_op jit(solution)/shard_map/ppermute | solution.py:473
  139.3 9.1 %collective-permute-start.23 = (bf16[128,1536]{1,0:T(8,128)(2,1)S(1)}, bf16[128,1536]{1,0:T(8,128)(2,1)S(1)}, u32[]{:S(2)}, u32[]{:S(2)}) collective-permute-start(bf16[128,1536]{1,0:T(8,128)(2,1)S(1)} %pad_maximum_fusion.2), channel_id=1, source_target_pairs={{0,2},{1,3},{2,4},{3,5},{4,6},{5,7},{6,0},{7,1},{8,10},{9,11},{10,... | collective-permute-start | bytes 1179656 | tf_op jit(solution)/shard_map/ppermute | solution.py:473
  150.7 17.6 %all-to-all-start.1 = ((bf16[8,144,448]{2,1,0:T(8,128)(2,1)}), bf16[8,144,448]{2,1,0:T(8,128)(2,1)S(1)}, u32[]{:S(2)}, u32[]{:S(2)}) async-start(bf16[8,144,448]{2,1,0:T(8,128)(2,1)} %get-tuple-element.70), calls=%async_computation.1 | async-start | bytes 2359296 | tf_op jit(solution)/shard_map/all_to_all | solution.py:566
  172.5 1.8 collective-permute-start.24
  189.9 14.5 %all-to-all-start.3 = ((bf16[8,16,1536]{2,1,0:T(8,128)(2,1)}), bf16[8,16,1536]{2,1,0:T(8,128)(2,1)S(1)}, u32[]{:S(2)}, u32[]{:S(2)}) async-start(bf16[8,16,1536]{2,1,0:T(8,128)(2,1)} %fold.1), calls=%async_computation.3 | async-start | bytes 786432 | tf_op jit(solution)/shard_map/all_to_all | solution.py:573
  (30 other events, 205.1 us)
Sparse Core Ops, SparseCore 0:
  10.3 54.6 all-gather.1
  127.7 70.8 reduce-scatter.1

commit v5 on v4

--- a/solution.py
+++ b/solution.py
@@ -21,6 +21,7 @@
 F32 = jnp.float32
 SCALE = HDIM**-0.5
 VMEM_LIMIT = 20 * 1024 * 1024
+VMEM_MOST = 58 * 1024 * 1024
 HBM_RATE = 3_000_000
 
 
@@ -104,7 +105,7 @@
         in_specs=[spec] * 3,
         out_specs=spec,
         out_shape=jax.ShapeDtypeStruct((TOK, WIDTH), BF),
-        compiler_params=params(),
+        compiler_params=params(VMEM_MOST),
         name="spatial_fwd",
         cost_estimate=cost(4),
     )(q, k, v)
@@ -187,14 +188,14 @@
         out_specs=[whole, whole, pl.BlockSpec((OUT_BLOCK, THREE), lambda i: (i, 0))],
         out_shape=[jax.ShapeDtypeStruct((TOK, WIDTH), BF)] * 2
         + [jax.ShapeDtypeStruct((WIDTH, THREE), BF)],
-        compiler_params=params(58 * 1024 * 1024),
+        compiler_params=params(VMEM_MOST),
         name="out_norm",
         cost_estimate=cost(5),
     )(mixed, weights, inputs, gain)
 
 
 POS = 16
-CHAINS = 4
+CHAINS = 8
 
 
 def temporal_block(q, keys, values, dout, valid):
@@ -377,9 +378,13 @@
     )(*sums, hidden, resid, gain, heads_out)
 
 
-def out_product_kernel(factor, order_ref, groups_ref, mixed_ref, mine_ref, other_ref):
-    left = jnp.concatenate([groups_ref[order_ref[r], :TOK] for r in range(SEQ)], axis=0)
-    product = dot_tn(left, mixed_ref[...]) * factor
+def out_product_kernel(factor, order_ref, groups_ref, mixed_ref, mine_ref, other_ref, turned):
+    @pl.when(pl.program_id(0) == 0)
+    def _():
+        for r in range(SEQ):
+            turned[:, r * TOK : (r + 1) * TOK] = groups_ref[order_ref[r], :TOK].T
+
+    product = dot_nn(turned[...], mixed_ref[...]) * factor
     extras = sum(groups_ref[r, TOK:].astype(F32) for r in range(SEQ))
     high, low = two_parts(extras[0:1] + extras[1:2])
     turn = lax.broadcasted_iota(jnp.int32, (GROUPED, GROUPED), 0) % SLOT
@@ -409,6 +414,7 @@
                 pl.BlockSpec((SEQ * TOK, cols), lambda i, o: (0, i)),
             ],
             out_specs=[spec, spec],
+            scratch_shapes=[pltpu.VMEM((GROUPED, SEQ * TOK), BF)],
         ),
         out_shape=[jax.ShapeDtypeStruct((DP // 2, SLOT, WIDTH), BF)] * 2,
         compiler_params=params(),
@@ -439,8 +445,7 @@
     )(pieces)
 
 
-def finish_kernel(in_ref, qkv_ref, out_ref, gain_ref, qkv_out_ref):
-    qkv_out_ref[...] = qkv_ref[...].astype(F32)
+def finish_kernel(in_ref, out_ref, gain_ref):
     out_ref[...] = jnp.concatenate(
         [in_ref[j].astype(F32)[:SHARE] for j in range(SEQ)], axis=0
     )
@@ -454,18 +459,17 @@
         gain_ref[pl.ds(four * rows, rows)] = back[SHARE] + back[SHARE + 1]
 
 
-def finish(gathered, qkv_rows):
+def finish(gathered):
     return pl.pallas_call(
         finish_kernel,
         out_shape=[
             jax.ShapeDtypeStruct((SEQ * SHARE, WIDTH), F32),
             jax.ShapeDtypeStruct((WIDTH,), F32),
-            jax.ShapeDtypeStruct(qkv_rows.shape, F32),
         ],
         compiler_params=params(),
         name="finish",
         cost_estimate=cost(2),
-    )(gathered, qkv_rows)
+    )(gathered)
 
 
 def along_x(array, shift):
@@ -512,6 +516,35 @@
     behind = jnp.concatenate([behind[:HALF] + top, behind[HALF:]], axis=0)
     ahead = jnp.concatenate([ahead[:HALF], ahead[HALF:] + low], axis=0)
     return own, across_y(partner), along_x(behind, -1), along_x(ahead, 1)
+
+
+def settle_kernel(in_ref, out_ref):
+    out_ref[...] = in_ref[...]
+
+
+def settle(array):
+    return pl.pallas_call(
+        settle_kernel,
+        out_shape=jax.ShapeDtypeStruct(array.shape, array.dtype),
+        compiler_params=params(),
+        name="settle",
+        cost_estimate=cost(1),
+    )(array)
+
+
+def beside_kernel(a_ref, b_ref, out_ref):
+    out_ref[:, : a_ref.shape[1]] = a_ref[...]
+    out_ref[:, a_ref.shape[1] :] = b_ref[...]
+
+
+def beside(a, b):
+    return pl.pallas_call(
+        beside_kernel,
+        out_shape=jax.ShapeDtypeStruct((a.shape[0], a.shape[1] + b.shape[1]), a.dtype),
+        compiler_params=params(VMEM_MOST),
+        name="beside",
+        cost_estimate=cost(1),
+    )(a, b)
 
 
 def chip_exchange(blocks):
@@ -537,11 +570,13 @@
     ).astype(jnp.int32)
 
     weights = lax.all_gather(
-        jnp.concatenate([out_weight, qkv_weight], axis=1), "dp", axis=0, tiled=True
+        beside(out_weight, qkv_weight), "dp", axis=0, tiled=True
     )
     mixed = spatial_fwd(q, k, v)
-    grad_heads = lax.all_to_all(
-        dout.reshape(TOK, SEQ, GROUP).transpose(1, 0, 2), "seq", 0, 0, tiled=True
+    grad_heads = settle(
+        lax.all_to_all(
+            dout.reshape(TOK, SEQ, GROUP).transpose(1, 0, 2), "seq", 0, 0, tiled=True
+        )
     )
     mixed_parts = gather_by_x(mixed)
     mixed_all = jnp.concatenate(mixed_parts, axis=0)
@@ -571,7 +606,8 @@
     received = chip_exchange(summed)
     temporal_out = groups[:, :TOK, GROUPED:].transpose(1, 0, 2).reshape(TOK, WIDTH)
     gathered = lax.all_to_all(fold(received), "seq", 0, 0, tiled=True)
-    out_grad, gain_grad, qkv_grad = finish(gathered, qkv_grad)
+    gathered, qkv_grad = lax.optimization_barrier((gathered, qkv_grad.astype(F32)))
+    out_grad, gain_grad = finish(gathered)
     return tuple(a.reshape(block_shape) for a in (hidden, temporal_out, grad_input, *grads)) + (
         qkv_grad,
         out_grad,

time: 214 us -> 213 us (level)
  waiting for transfers between devices: 60.7 us -> 45.5 us
  starting transfers between devices: 54 us -> 64.5 us
  Pallas kernels: 39.1 us -> 42.4 us
    ppermute x18, waiting for transfers between devices: 38.6 us -> 22.6 us  [along_x(): return lax.ppermute(array, 'seq', pairs)]
    all_to_all x1, waiting for transfers between devices: 0.01 us -> 7.56 us  [body(): lax.all_to_all(dout.reshape(TOK, SEQ, GROUP).transpose(1, 0, 2), 'seq', 0...]
    ppermute x6, starting transfers between devices: 12.8 us -> 17.3 us  [across_y(): return lax.ppermute(array, 'seq', [(i, i ^ 1) for i in range(SEQ)])]
    ppermute x18, starting transfers between devices: 28.4 us -> 32.7 us  [along_x(): return lax.ppermute(array, 'seq', pairs)]
    ppermute x6, waiting for transfers between devices: 6.87 us -> 2.79 us  [across_y(): return lax.ppermute(array, 'seq', [(i, i ^ 1) for i in range(SEQ)])]
    unnamed x71 -> x61, local copies, waits for them, and re-layouts: 14.5 us -> 14.1 us
  transfers between devices with their start and end apart: 30 -> 30, of which waited for: 18 -> 17; matrix products, arithmetic and copies ran while one was open for 7% -> 9% of each run, Pallas kernels for 10% -> 11%
where the time goes in v5:
time: 213 us; the launch traced here: 212 us
  starting transfers between devices  64.5 us (30%)
  waiting for transfers between devices  45.5 us (21%)
  Pallas kernels  42.4 us (20%)
  local copies, waits for them, and re-layouts  19.9 us (9%)
  blocking collectives  15 us (7%)
  between operations  14.5 us (7%)
  matrix products  5.63 us (3%)
  other arithmetic  4.3 us (2%)
    ppermute x18, starting transfers between devices, along_x(): return lax.ppermute(array, 'seq', pairs)  32.7 us
    ppermute x18, waiting for transfers between devices, along_x(): return lax.ppermute(array, 'seq', pairs)  22.6 us
    ppermute x6, starting transfers between devices, across_y(): return lax.ppermute(array, 'seq', [(i, i ^ 1) for i in range(SEQ)])  17.3 us
    all_to_all x1, blocking collectives, chip_exchange(): lax.all_to_all(blocks, 'dp', 0, 0, axis_index_groups=groups, tiled=True)  15 us
    unnamed x61, local copies, waits for them, and re-layouts  14.1 us
    pallas_call x1, Pallas kernels, spatial_bwd(): pl.pallas_call(spatial_bwd_kernel, grid=(WIDTH // (PAIRS * LANE),), in_sp...  7.64 us
    all_to_all x1, waiting for transfers between devices, body(): lax.all_to_all(dout.reshape(TOK, SEQ, GROUP).transpose(1, 0, 2), 'seq', 0...  7.56 us
    pallas_call x1, Pallas kernels, out_norm(): pl.pallas_call(out_norm_kernel, grid=(WIDTH // OUT_BLOCK,), in_specs=[who...  6.7 us
  transfers between devices with their start and end apart: 30, of which 17 were waited for; matrix products, arithmetic and copies ran while one was open for 9% of the time, Pallas kernels for 11%

profile of v5, /device:TPU:0, one launch (start us, length us, event | category | flops | bytes accessed | tf_op | source)
XLA Modules:
  0.0 211.7 jit_solution(4034571015886071921)
XLA Ops:
  9.1 4.6 %spatial_fwd.1.mixed_ref = bf16[128,1536]{1,0:T(8,128)(2,1)} custom-call(bf16[128,1536]{1,0:T(8,128)(2,1)} %bitcast.38, bf16[128,1536]{1,0:T(8,128)(2,1)} %bitcast.40, bf16[128,1536]{1,0:T(8,128)(2,1)} %bitcast.42), custom_call_target="tpu_custom_call" | custom-call | bytes 12000000 | tf_op jit(solution)/shard_map/spatial_fwd/pallas_call | solution.py:102
  13.7 3.3 %collective-permute-start.3 = (bf16[128,1536]{1,0:T(8,128)(2,1)}, bf16[128,1536]{1,0:T(8,128)(2,1)}, u32[]{:S(2)}, u32[]{:S(2)}) collective-permute-start(bf16[128,1536]{1,0:T(8,128)(2,1)} %spatial_fwd.1.mixed_ref), channel_id=1, source_target_pairs={{0,1},{1,0},{2,3},{3,2},{4,5},{5,4},{6,7},{7,6},{8,9},{9,8},{10,11... | collective-permute-start | bytes 1179656 | tf_op jit(solution)/shard_map/ppermute | solution.py:481
  20.0 4.1 %all-to-all-start = ((bf16[8,128,192]{1,2,0:T(8,128)(2,1)}), bf16[8,128,192]{1,2,0:T(8,128)(2,1)}, u32[]{:S(2)}, u32[]{:S(2)}) async-start(bf16[8,128,192]{1,2,0:T(8,128)(2,1)} %copy.20), calls=%async_computation | async-start | bytes 786432 | tf_op jit(solution)/shard_map/all_to_all | solution.py:577
  24.1 3.2 %collective-permute-start.1 = (bf16[128,1536]{1,0:T(8,128)(2,1)S(1)}, bf16[128,1536]{1,0:T(8,128)(2,1)}, u32[]{:S(2)}, u32[]{:S(2)}) collective-permute-start(bf16[128,1536]{1,0:T(8,128)(2,1)S(1)} %copy-done.24), channel_id=1, source_target_pairs={{0,6},{1,7},{2,0},{3,1},{4,2},{5,3},{6,4},{7,5},{8,14},{9,15},{10,... | collective-permute-start | bytes 1179656 | tf_op jit(solution)/shard_map/ppermute | solution.py:477
  28.8 7.6 %all-to-all-done = bf16[8,128,192]{1,2,0:T(8,128)(2,1)} async-done(((bf16[8,128,192]{1,2,0:T(8,128)(2,1)}), bf16[8,128,192]{1,2,0:T(8,128)(2,1)}, u32[]{:S(2)}, u32[]{:S(2)}) %all-to-all-start) | async-done | bytes 393248 | tf_op jit(solution)/shard_map/all_to_all | solution.py:577
  42.8 5.8 %collective-permute-start.6 = (bf16[128,1536]{1,0:T(8,128)(2,1)}, bf16[128,1536]{1,0:T(8,128)(2,1)S(1)}, u32[]{:S(2)}, u32[]{:S(2)}) collective-permute-start(bf16[128,1536]{1,0:T(8,128)(2,1)} %collective-permute-done.3), channel_id=1, source_target_pairs={{0,4},{1,5},{2,6},{3,7},{4,0},{5,1},{6,2},{7,3},{8,12},{9,13},{10,... | collective-permute-start | bytes 1179656 | tf_op jit(solution)/shard_map/ppermute | solution.py:477
  52.7 2.5 %collective-permute-done.4 = bf16[128,1536]{1,0:T(8,128)(2,1)S(1)} collective-permute-done((bf16[128,1536]{1,0:T(8,128)(2,1)}, bf16[128,1536]{1,0:T(8,128)(2,1)S(1)}, u32[]{:S(2)}, u32[]{:S(2)}) %collective-permute-start.4) | collective-permute-done | bytes 393248 | tf_op jit(solution)/shard_map/ppermute | solution.py:477
  55.2 2.1 %collective-permute-done.5 = bf16[128,1536]{1,0:T(8,128)(2,1)S(1)} collective-permute-done((bf16[128,1536]{1,0:T(8,128)(2,1)}, bf16[128,1536]{1,0:T(8,128)(2,1)S(1)}, u32[]{:S(2)}, u32[]{:S(2)}) %collective-permute-start.5) | collective-permute-done | bytes 393248 | tf_op jit(solution)/shard_map/ppermute | solution.py:477
  61.2 2.6 %all-gather.2.cloned.1.call-done.w_ref = bf16[1536,2112]{1,0:T(8,128)(2,1)} async-done(((bf16[96,2112]{1,0:T(8,128)(2,1)}), bf16[1536,2112]{1,0:T(8,128)(2,1)}) %all-gather.2.cloned.1.call-update) | async-done | bytes 6488080 | tf_op jit(solution)/shard_map/all_gather | solution.py:572
  63.8 6.7 %out_norm.1 = (bf16[128,1536]{1,0:T(8,128)(2,1)}, bf16[128,1536]{1,0:T(8,128)(2,1)}, bf16[1536,768]{1,0:T(8,128)(2,1)}) custom-call(bf16[128,1536]{1,0:T(8,128)(2,1)} %spatial_fwd.1.mixed_ref, bf16[1536,2112]{1,0:T(8,128)(2,1)} %all-gather.2.cloned.1.call-done.w_ref, bf16[128,1536]{1,0:T(8,128)(2,1)} %bitcast.48, f32[1,1536]{1,0:T(1,128)} %reshape.55.gain_ref), custom_call_target="tpu_custom_call" | custom-call | bytes 15000000 | tf_op jit(solution)/shard_map/out_norm/pallas_call | solution.py:179
  70.5 4.6 %collective-permute-start.8 = (bf16[128,1536]{1,0:T(8,128)(2,1)}, bf16[128,1536]{1,0:T(8,128)(2,1)S(1)}, u32[]{:S(2)}, u32[]{:S(2)}) collective-permute-start(bf16[128,1536]{1,0:T(8,128)(2,1)} %get-tuple-element.50.refs_0_), channel_id=1, source_target_pairs={{0,6},{1,7},{2,0},{3,1},{4,2},{5,3},{6,4},{7,5},{8,14},{9,15},{10,... | collective-permute-start | bytes 1179656 | tf_op jit(solution)/shard_map/ppermute | solution.py:477
  75.3 3.0 %collective-permute-start.11 = (bf16[128,1536]{1,0:T(8,128)(2,1)}, bf16[128,1536]{1,0:T(8,128)(2,1)S(1)}, u32[]{:S(2)}, u32[]{:S(2)}) collective-permute-start(bf16[128,1536]{1,0:T(8,128)(2,1)} %get-tuple-element.50.refs_0_), channel_id=1, source_target_pairs={{0,1},{1,0},{2,3},{3,2},{4,5},{5,4},{6,7},{7,6},{8,9},{9,8},{10,11... | collective-permute-start | bytes 1179656 | tf_op jit(solution)/shard_map/ppermute | solution.py:481
  78.2 2.3 %convolution_convert_fusion.7.refs_0_ = bf16[128,768]{1,0:T(8,128)(2,1)S(1)} fusion(bf16[128,1536]{1,0:T(8,128)(2,1)} %get-tuple-element.50.refs_0_, bf16[1536,768]{1,0:T(8,128)(2,1)} %get-tuple-element.51.w_ref), kind=kOutput, calls=%fused_computation.7 | convolution fusion | flops 302088192 | bytes 2949120 | tf_op jit(solution)/shard_map/dot_general | solution.py:45
  82.5 3.6 %collective-permute-start.10 = (bf16[64,1536]{1,0:T(8,128)(2,1)S(1)}, bf16[64,1536]{1,0:T(8,128)(2,1)S(1)}, u32[]{:S(2)}, u32[]{:S(2)}) collective-permute-start(bf16[64,1536]{1,0:T(8,128)(2,1)S(1)} %slice.37), channel_id=1, source_target_pairs={{0,6},{1,7},{2,0},{3,1},{4,2},{5,3},{6,4},{7,5},{8,14},{9,15},{10,... | collective-permute-start | bytes 589832 | tf_op jit(solution)/shard_map/ppermute | solution.py:477
  87.9 3.1 %collective-permute-start.13 = (bf16[128,1536]{1,0:T(8,128)(2,1)S(1)}, bf16[128,1536]{1,0:T(8,128)(2,1)S(1)}, u32[]{:S(2)}, u32[]{:S(2)}) collective-permute-start(bf16[128,1536]{1,0:T(8,128)(2,1)S(1)} %collective-permute-done.11.refs_5_), channel_id=1, source_target_pairs={{0,6},{1,7},{2,0},{3,1},{4,2},{5,3},{6,4},{7,5},{8,14},{9,15},{10,... | collective-permute-start | bytes 1179656 | tf_op jit(solution)/shard_map/ppermute | solution.py:477
  91.0 2.9 %collective-permute-start.15 = (bf16[64,1536]{1,0:T(8,128)(2,1)S(1)}, bf16[64,1536]{1,0:T(8,128)(2,1)S(1)}, u32[]{:S(2)}, u32[]{:S(2)}) collective-permute-start(bf16[64,1536]{1,0:T(8,128)(2,1)S(1)} %collective-permute-done.10.refs_4_), channel_id=1, source_target_pairs={{0,1},{1,0},{2,3},{3,2},{4,5},{5,4},{6,7},{7,6},{8,9},{9,8},{10,11... | collective-permute-start | bytes 589832 | tf_op jit(solution)/shard_map/ppermute | solution.py:481
  95.7 3.2 %collective-permute-start.14 = (bf16[64,1536]{1,0:T(8,128)(2,1)S(1)}, bf16[64,1536]{1,0:T(8,128)(2,1)S(1)}, u32[]{:S(2)}, u32[]{:S(2)}) collective-permute-start(bf16[64,1536]{1,0:T(8,128)(2,1)S(1)} %collective-permute-done.9.refs_3_), channel_id=1, source_target_pairs={{0,1},{1,0},{2,3},{3,2},{4,5},{5,4},{6,7},{7,6},{8,9},{9,8},{10,11... | collective-permute-start | bytes 589832 | tf_op jit(solution)/shard_map/ppermute | solution.py:481
  100.8 2.4 %collective-permute-done.14.refs_8_ = bf16[64,1536]{1,0:T(8,128)(2,1)S(1)} collective-permute-done((bf16[64,1536]{1,0:T(8,128)(2,1)S(1)}, bf16[64,1536]{1,0:T(8,128)(2,1)S(1)}, u32[]{:S(2)}, u32[]{:S(2)}) %collective-permute-start.14) | collective-permute-done | bytes 196640 | tf_op jit(solution)/shard_map/ppermute | solution.py:481
  103.6 5.5 %temporal.1 = (bf16[8,128,192]{2,1,0:T(8,128)(2,1)S(1)}, bf16[8,128,768]{2,1,0:T(8,128)(2,1)S(1)}) custom-call(s32[9]{0:T(128)S(1)} %stack.39.order_ref, bf16[128,768]{1,0:T(8,128)(2,1)S(1)} %convolution_convert_fusion.7.refs_0_, bf16[128,768]{1,0:T(8,128)(2,1)S(1)} %convolution_convert_fusion.6.refs_1_, ...), custom_call_target="tpu_custom_call" | custom-call | bytes 24000000 | tf_op jit(solution)/shard_map/temporal/pallas_call | solution.py:244
  109.1 2.8 %shares.2 = (bf16[128,1536]{1,0:T(8,128)(2,1)S(1)}, bf16[128,1536]{1,0:T(8,128)(2,1)}, bf16[128,1536]{1,0:T(8,128)(2,1)}, bf16[128,1536]{1,0:T(8,128)(2,1)}) custom-call(bf16[8,128,768]{2,1,0:T(8,128)(2,1)S(1)} %get-tuple-element.58.dproj_ref.refs_10_, bf16[1536,768]{1,0:T(8,128)(2,1)S(1)} %copy-done), custom_call_target="tpu_custom_call" | custom-call | bytes 6000000 | tf_op jit(solution)/shard_map/shares/pallas_call | solution.py:274
  111.9 3.0 %collective-permute-start.16 = (bf16[128,1536]{1,0:T(8,128)(2,1)}, bf16[128,1536]{1,0:T(8,128)(2,1)}, u32[]{:S(2)}, u32[]{:S(2)}) collective-permute-start(bf16[128,1536]{1,0:T(8,128)(2,1)} %get-tuple-element.61), channel_id=1, source_target_pairs={{0,1},{1,0},{2,3},{3,2},{4,5},{5,4},{6,7},{7,6},{8,9},{9,8},{10,11... | collective-permute-start | bytes 1179656 | tf_op jit(solution)/shard_map/ppermute | solution.py:481
  121.1 4.5 %qkv_product.1 = bf16[1536,576]{1,0:T(8,128)(2,1)} custom-call(bf16[128,1536]{1,0:T(8,128)(2,1)S(1)} %copy-done.10, bf16[128,1536]{1,0:T(8,128)(2,1)S(1)} %collective-permute-done.7.refs_1_, bf16[128,1536]{1,0:T(8,128)(2,1)S(1)} %collective-permute-done.8.refs_2_, bf16[64,1536]{1,0:T(8,128)(2,1)S(1)} %collective-permute-done.9.refs_3_, ...), custom_call_target="tpu_custom_call" | custom-call | bytes 15000000 | tf_op jit(solution)/shard_map/qkv_product/pallas_call | solution.py:305
  133.9 3.7 %collective-permute-done.22 = bf16[64,1536]{1,0:T(8,128)(2,1)S(1)} collective-permute-done((bf16[64,1536]{1,0:T(8,128)(2,1)S(1)}, bf16[64,1536]{1,0:T(8,128)(2,1)S(1)}, u32[]{:S(2)}, u32[]{:S(2)}) %collective-permute-start.22) | collective-permute-done | bytes 196640 | tf_op jit(solution)/shard_map/ppermute | solution.py:477
  140.3 5.2 %collective-permute-done.21.sum_c = bf16[128,1536]{1,0:T(8,128)(2,1)S(1)} collective-permute-done((bf16[128,1536]{1,0:T(8,128)(2,1)S(1)}, bf16[128,1536]{1,0:T(8,128)(2,1)S(1)}, u32[]{:S(2)}, u32[]{:S(2)}) %collective-permute-start.21) | collective-permute-done | bytes 393248 | tf_op jit(solution)/shard_map/ppermute | solution.py:477
  146.9 2.3 %grad_input.1 = (bf16[128,1536]{1,0:T(8,128)(2,1)}, bf16[8,144,448]{2,1,0:T(8,128)(2,1)}) custom-call(bf16[128,1536]{1,0:T(8,128)(2,1)S(1)} %get-tuple-element.59.sum_a, bf16[128,1536]{1,0:T(8,128)(2,1)S(1)} %collective-permute-done.19.sum_b, bf16[128,1536]{1,0:T(8,128)(2,1)S(1)} %collective-permute-done.21.sum_c, ...), custom_call_target="tpu_custom_call" | custom-call | bytes 6000000 | tf_op jit(solution)/shard_map/grad_input/pallas_call | solution.py:369
  149.2 4.0 %all-to-all-start.1 = ((bf16[8,144,448]{2,1,0:T(8,128)(2,1)}), bf16[8,144,448]{2,1,0:T(8,128)(2,1)S(1)}, u32[]{:S(2)}, u32[]{:S(2)}) async-start(bf16[8,144,448]{2,1,0:T(8,128)(2,1)} %get-tuple-element.71), calls=%async_computation.1 | async-start | bytes 2359296 | tf_op jit(solution)/shard_map/all_to_all | solution.py:601
  153.2 2.9 %copy-done.1 = bf16[1536,2112]{1,0:T(8,128)(2,1)S(1)} copy-done((bf16[1536,2112]{1,0:T(8,128)(2,1)S(1)}, bf16[1536,2112]{1,0:T(8,128)(2,1)}, u32[]{:S(2)}) %copy-start.1) | copy-done | bytes 6488088
  156.1 7.6 %spatial_bwd.1 = (bf16[128,1536]{1,0:T(8,128)(2,1)}, bf16[128,1536]{1,0:T(8,128)(2,1)}, bf16[128,1536]{1,0:T(8,128)(2,1)}) custom-call(bf16[128,1536]{1,0:T(8,128)(2,1)S(1)} %copy-done.13, bf16[1536,2112]{1,0:T(8,128)(2,1)S(1)} %copy-done.1, bf16[128,1536]{1,0:T(8,128)(2,1)S(1)} %bitcast.39, bf16[128,1536]{1,0:T(8,128)(2,1)S(1)} %bitcast.41, ...), custom_call_target="tpu_custom_call" | custom-call | bytes 27000000 | tf_op jit(solution)/shard_map/spatial_bwd/pallas_call | solution.py:129
  167.7 2.5 %out_product.1 = (bf16[8,16,1536]{2,1,0:T(8,128)(2,1)S(1)}, bf16[8,16,1536]{2,1,0:T(8,128)(2,1)S(1)}) custom-call(s32[9]{0:T(128)S(1)} %stack.39.order_ref, bf16[8,144,448]{2,1,0:T(8,128)(2,1)S(1)} %all-to-all-done.1.groups_ref, bf16[1024,1536]{1,0:T(8,128)(2,1)S(1)} %copy-done.3), custom_call_target="tpu_custom_call" | custom-call | bytes 9000000 | tf_op jit(solution)/shard_map/out_product/pallas_call | solution.py:407
  172.1 15.0 %all_to_all.20.in_ref = bf16[8,16,1536]{2,1,0:T(8,128)(2,1)S(1)} all-to-all(bf16[8,16,1536]{2,1,0:T(8,128)(2,1)S(1)} %add.102), channel_id=1, replica_groups={{0,16,32,48,64,80,96,112},{8,24,40,56,72,88,104,120},{1,17,33,49,65,81,..., dimensions={0} | all-to-all | bytes 786432 | tf_op jit(solution)/shard_map/all_to_all | solution.py:552
  187.9 6.4 %all-to-all-start.3 = ((bf16[8,16,1536]{2,1,0:T(8,128)(2,1)}), bf16[8,16,1536]{2,1,0:T(8,128)(2,1)S(1)}, u32[]{:S(2)}, u32[]{:S(2)}) async-start(bf16[8,16,1536]{2,1,0:T(8,128)(2,1)} %fold.1), calls=%async_computation.3 | async-start | bytes 786432 | tf_op jit(solution)/shard_map/all_to_all | solution.py:608
  197.4 6.1 %all-to-all-done.3.in_ref = bf16[8,16,1536]{2,1,0:T(8,128)(2,1)S(1)} async-done(((bf16[8,16,1536]{2,1,0:T(8,128)(2,1)}), bf16[8,16,1536]{2,1,0:T(8,128)(2,1)S(1)}, u32[]{:S(2)}, u32[]{:S(2)}) %all-to-all-start.3) | async-done | bytes 393248 | tf_op jit(solution)/shard_map/all_to_all | solution.py:608
  (132 shorter events, 58.5 us)
Async XLA Ops:
  7.2 56.6 %all-gather.2.cloned.1.call-start = ((), (), s32[]{:S(2)}) async-start(), calls=%async_computation.5 | async-start | bytes 7102464 | tf_op jit(solution)/shard_map/all_gather | solution.py:572
  9.1 19.1 %copy-start.26 = (f32[1536]{0:T(1024)S(1)}, f32[1536]{0:T(1024)}, u32[]{:S(2)}) copy-start(f32[1536]{0:T(1024)} %param.14) | copy-start | bytes 18436
  13.7 25.8 %collective-permute-start.3 = (bf16[128,1536]{1,0:T(8,128)(2,1)}, bf16[128,1536]{1,0:T(8,128)(2,1)}, u32[]{:S(2)}, u32[]{:S(2)}) collective-permute-start(bf16[128,1536]{1,0:T(8,128)(2,1)} %spatial_fwd.1.mixed_ref), channel_id=1, source_target_pairs={{0,1},{1,0},{2,3},{3,2},{4,5},{5,4},{6,7},{7,6},{8,9},{9,8},{10,11... | collective-permute-start | bytes 1179656 | tf_op jit(solution)/shard_map/ppermute | solution.py:481
  16.9 25.8 %collective-permute-start = (bf16[128,1536]{1,0:T(8,128)(2,1)}, bf16[128,1536]{1,0:T(8,128)(2,1)}, u32[]{:S(2)}, u32[]{:S(2)}) collective-permute-start(bf16[128,1536]{1,0:T(8,128)(2,1)} %spatial_fwd.1.mixed_ref), channel_id=1, source_target_pairs={{0,2},{1,3},{2,4},{3,5},{4,6},{5,7},{6,0},{7,1},{8,10},{9,11},{10,... | collective-permute-start | bytes 1179656 | tf_op jit(solution)/shard_map/ppermute | solution.py:477
  20.0 16.4 %all-to-all-start = ((bf16[8,128,192]{1,2,0:T(8,128)(2,1)}), bf16[8,128,192]{1,2,0:T(8,128)(2,1)}, u32[]{:S(2)}, u32[]{:S(2)}) async-start(bf16[8,128,192]{1,2,0:T(8,128)(2,1)} %copy.20), calls=%async_computation | async-start | bytes 786432 | tf_op jit(solution)/shard_map/all_to_all | solution.py:577
  24.1 171.7 %reduce-scatter.2.cloned.1.call-start = ((), (), s32[]{:S(2)}) async-start(), calls=%async_computation.6 | async-start | bytes 2088960 | tf_op jit(solution)/shard_map/reduce_scatter | solution.py:593
  24.1 25.5 %collective-permute-start.1 = (bf16[128,1536]{1,0:T(8,128)(2,1)S(1)}, bf16[128,1536]{1,0:T(8,128)(2,1)}, u32[]{:S(2)}, u32[]{:S(2)}) collective-permute-start(bf16[128,1536]{1,0:T(8,128)(2,1)S(1)} %copy-done.24), channel_id=1, source_target_pairs={{0,6},{1,7},{2,0},{3,1},{4,2},{5,3},{6,4},{7,5},{8,14},{9,15},{10,... | collective-permute-start | bytes 1179656 | tf_op jit(solution)/shard_map/ppermute | solution.py:477
  27.3 23.4 %collective-permute-start.2 = (bf16[128,1536]{1,0:T(8,128)(2,1)S(1)}, bf16[128,1536]{1,0:T(8,128)(2,1)}, u32[]{:S(2)}, u32[]{:S(2)}) collective-permute-start(bf16[128,1536]{1,0:T(8,128)(2,1)S(1)} %copy-done.24), channel_id=1, source_target_pairs={{0,4},{1,5},{2,6},{3,7},{4,0},{5,1},{6,2},{7,3},{8,12},{9,13},{10,... | collective-permute-start | bytes 1179656 | tf_op jit(solution)/shard_map/ppermute | solution.py:477
  39.5 15.7 %collective-permute-start.4 = (bf16[128,1536]{1,0:T(8,128)(2,1)}, bf16[128,1536]{1,0:T(8,128)(2,1)S(1)}, u32[]{:S(2)}, u32[]{:S(2)}) collective-permute-start(bf16[128,1536]{1,0:T(8,128)(2,1)} %collective-permute-done.3), channel_id=1, source_target_pairs={{0,2},{1,3},{2,4},{3,5},{4,6},{5,7},{6,0},{7,1},{8,10},{9,11},{10,... | collective-permute-start | bytes 1179656 | tf_op jit(solution)/shard_map/ppermute | solution.py:477
  40.8 16.6 %collective-permute-start.5 = (bf16[128,1536]{1,0:T(8,128)(2,1)}, bf16[128,1536]{1,0:T(8,128)(2,1)S(1)}, u32[]{:S(2)}, u32[]{:S(2)}) collective-permute-start(bf16[128,1536]{1,0:T(8,128)(2,1)} %collective-permute-done.3), channel_id=1, source_target_pairs={{0,6},{1,7},{2,0},{3,1},{4,2},{5,3},{6,4},{7,5},{8,14},{9,15},{10,... | collective-permute-start | bytes 1179656 | tf_op jit(solution)/shard_map/ppermute | solution.py:477
  42.8 16.7 %collective-permute-start.6 = (bf16[128,1536]{1,0:T(8,128)(2,1)}, bf16[128,1536]{1,0:T(8,128)(2,1)S(1)}, u32[]{:S(2)}, u32[]{:S(2)}) collective-permute-start(bf16[128,1536]{1,0:T(8,128)(2,1)} %collective-permute-done.3), channel_id=1, source_target_pairs={{0,4},{1,5},{2,6},{3,7},{4,0},{5,1},{6,2},{7,3},{8,12},{9,13},{10,... | collective-permute-start | bytes 1179656 | tf_op jit(solution)/shard_map/ppermute | solution.py:477
  70.5 11.9 %collective-permute-start.8 = (bf16[128,1536]{1,0:T(8,128)(2,1)}, bf16[128,1536]{1,0:T(8,128)(2,1)S(1)}, u32[]{:S(2)}, u32[]{:S(2)}) collective-permute-start(bf16[128,1536]{1,0:T(8,128)(2,1)} %get-tuple-element.50.refs_0_), channel_id=1, source_target_pairs={{0,6},{1,7},{2,0},{3,1},{4,2},{5,3},{6,4},{7,5},{8,14},{9,15},{10,... | collective-permute-start | bytes 1179656 | tf_op jit(solution)/shard_map/ppermute | solution.py:477
  75.2 10.9 %collective-permute-start.7 = (bf16[128,1536]{1,0:T(8,128)(2,1)}, bf16[128,1536]{1,0:T(8,128)(2,1)S(1)}, u32[]{:S(2)}, u32[]{:S(2)}) collective-permute-start(bf16[128,1536]{1,0:T(8,128)(2,1)} %get-tuple-element.50.refs_0_), channel_id=1, source_target_pairs={{0,2},{1,3},{2,4},{3,5},{4,6},{5,7},{6,0},{7,1},{8,10},{9,11},{10,... | collective-permute-start | bytes 1179656 | tf_op jit(solution)/shard_map/ppermute | solution.py:477
  75.3 11.9 %collective-permute-start.11 = (bf16[128,1536]{1,0:T(8,128)(2,1)}, bf16[128,1536]{1,0:T(8,128)(2,1)S(1)}, u32[]{:S(2)}, u32[]{:S(2)}) collective-permute-start(bf16[128,1536]{1,0:T(8,128)(2,1)} %get-tuple-element.50.refs_0_), channel_id=1, source_target_pairs={{0,1},{1,0},{2,3},{3,2},{4,5},{5,4},{6,7},{7,6},{8,9},{9,8},{10,11... | collective-permute-start | bytes 1179656 | tf_op jit(solution)/shard_map/ppermute | solution.py:481
  82.5 8.6 %collective-permute-start.10 = (bf16[64,1536]{1,0:T(8,128)(2,1)S(1)}, bf16[64,1536]{1,0:T(8,128)(2,1)S(1)}, u32[]{:S(2)}, u32[]{:S(2)}) collective-permute-start(bf16[64,1536]{1,0:T(8,128)(2,1)S(1)} %slice.37), channel_id=1, source_target_pairs={{0,6},{1,7},{2,0},{3,1},{4,2},{5,3},{6,4},{7,5},{8,14},{9,15},{10,... | collective-permute-start | bytes 589832 | tf_op jit(solution)/shard_map/ppermute | solution.py:477
  86.1 9.1 %collective-permute-start.9 = (bf16[64,1536]{1,0:T(8,128)(2,1)S(1)}, bf16[64,1536]{1,0:T(8,128)(2,1)S(1)}, u32[]{:S(2)}, u32[]{:S(2)}) collective-permute-start(bf16[64,1536]{1,0:T(8,128)(2,1)S(1)} %slice.36), channel_id=1, source_target_pairs={{0,2},{1,3},{2,4},{3,5},{4,6},{5,7},{6,0},{7,1},{8,10},{9,11},{10,... | collective-permute-start | bytes 589832 | tf_op jit(solution)/shard_map/ppermute | solution.py:477
  87.2 12.6 %collective-permute-start.12 = (bf16[128,1536]{1,0:T(8,128)(2,1)S(1)}, bf16[128,1536]{1,0:T(8,128)(2,1)S(1)}, u32[]{:S(2)}, u32[]{:S(2)}) collective-permute-start(bf16[128,1536]{1,0:T(8,128)(2,1)S(1)} %collective-permute-done.11.refs_5_), channel_id=1, source_target_pairs={{0,2},{1,3},{2,4},{3,5},{4,6},{5,7},{6,0},{7,1},{8,10},{9,11},{10,... | collective-permute-start | bytes 1179656 | tf_op jit(solution)/shard_map/ppermute | solution.py:477
  87.9 12.3 %collective-permute-start.13 = (bf16[128,1536]{1,0:T(8,128)(2,1)S(1)}, bf16[128,1536]{1,0:T(8,128)(2,1)S(1)}, u32[]{:S(2)}, u32[]{:S(2)}) collective-permute-start(bf16[128,1536]{1,0:T(8,128)(2,1)S(1)} %collective-permute-done.11.refs_5_), channel_id=1, source_target_pairs={{0,6},{1,7},{2,0},{3,1},{4,2},{5,3},{6,4},{7,5},{8,14},{9,15},{10,... | collective-permute-start | bytes 1179656 | tf_op jit(solution)/shard_map/ppermute | solution.py:477
  91.0 9.7 %collective-permute-start.15 = (bf16[64,1536]{1,0:T(8,128)(2,1)S(1)}, bf16[64,1536]{1,0:T(8,128)(2,1)S(1)}, u32[]{:S(2)}, u32[]{:S(2)}) collective-permute-start(bf16[64,1536]{1,0:T(8,128)(2,1)S(1)} %collective-permute-done.10.refs_4_), channel_id=1, source_target_pairs={{0,1},{1,0},{2,3},{3,2},{4,5},{5,4},{6,7},{7,6},{8,9},{9,8},{10,11... | collective-permute-start | bytes 589832 | tf_op jit(solution)/shard_map/ppermute | solution.py:481
  95.7 7.4 %collective-permute-start.14 = (bf16[64,1536]{1,0:T(8,128)(2,1)S(1)}, bf16[64,1536]{1,0:T(8,128)(2,1)S(1)}, u32[]{:S(2)}, u32[]{:S(2)}) collective-permute-start(bf16[64,1536]{1,0:T(8,128)(2,1)S(1)} %collective-permute-done.9.refs_3_), channel_id=1, source_target_pairs={{0,1},{1,0},{2,3},{3,2},{4,5},{5,4},{6,7},{7,6},{8,9},{9,8},{10,11... | collective-permute-start | bytes 589832 | tf_op jit(solution)/shard_map/ppermute | solution.py:481
  111.9 13.7 %collective-permute-start.16 = (bf16[128,1536]{1,0:T(8,128)(2,1)}, bf16[128,1536]{1,0:T(8,128)(2,1)}, u32[]{:S(2)}, u32[]{:S(2)}) collective-permute-start(bf16[128,1536]{1,0:T(8,128)(2,1)} %get-tuple-element.61), channel_id=1, source_target_pairs={{0,1},{1,0},{2,3},{3,2},{4,5},{5,4},{6,7},{7,6},{8,9},{9,8},{10,11... | collective-permute-start | bytes 1179656 | tf_op jit(solution)/shard_map/ppermute | solution.py:481
  114.9 10.7 %collective-permute-start.17 = (bf16[128,1536]{1,0:T(8,128)(2,1)}, bf16[128,1536]{1,0:T(8,128)(2,1)}, u32[]{:S(2)}, u32[]{:S(2)}) collective-permute-start(bf16[128,1536]{1,0:T(8,128)(2,1)} %get-tuple-element.62), channel_id=1, source_target_pairs={{0,6},{1,7},{2,0},{3,1},{4,2},{5,3},{6,4},{7,5},{8,14},{9,15},{10,... | collective-permute-start | bytes 1179656 | tf_op jit(solution)/shard_map/ppermute | solution.py:477
  115.2 10.4 %collective-permute-start.18 = (bf16[128,1536]{1,0:T(8,128)(2,1)}, bf16[128,1536]{1,0:T(8,128)(2,1)}, u32[]{:S(2)}, u32[]{:S(2)}) collective-permute-start(bf16[128,1536]{1,0:T(8,128)(2,1)} %get-tuple-element.63), channel_id=1, source_target_pairs={{0,2},{1,3},{2,4},{3,5},{4,6},{5,7},{6,0},{7,1},{8,10},{9,11},{10,... | collective-permute-start | bytes 1179656 | tf_op jit(solution)/shard_map/ppermute | solution.py:477
  126.9 7.0 %collective-permute-start.20 = (bf16[64,1536]{1,0:T(8,128)(2,1)S(1)}, bf16[64,1536]{1,0:T(8,128)(2,1)S(1)}, u32[]{:S(2)}, u32[]{:S(2)}) collective-permute-start(bf16[64,1536]{1,0:T(8,128)(2,1)S(1)} %get-tuple-element.90), channel_id=1, source_target_pairs={{0,6},{1,7},{2,0},{3,1},{4,2},{5,3},{6,4},{7,5},{8,14},{9,15},{10,... | collective-permute-start | bytes 589832 | tf_op jit(solution)/shard_map/ppermute | solution.py:477
  128.6 18.3 %copy-start.23 = (f32[1,1536]{1,0:T(1,128)S(1)}, f32[1,1536]{1,0:T(1,128)}, u32[]{:S(2)}) copy-start(f32[1,1536]{1,0:T(1,128)} %reshape.55.gain_ref) | copy-start | bytes 18436
  128.6 9.0 %collective-permute-start.22 = (bf16[64,1536]{1,0:T(8,128)(2,1)S(1)}, bf16[64,1536]{1,0:T(8,128)(2,1)S(1)}, u32[]{:S(2)}, u32[]{:S(2)}) collective-permute-start(bf16[64,1536]{1,0:T(8,128)(2,1)S(1)} %get-tuple-element.89), channel_id=1, source_target_pairs={{0,2},{1,3},{2,4},{3,5},{4,6},{5,7},{6,0},{7,1},{8,10},{9,11},{10,... | collective-permute-start | bytes 589832 | tf_op jit(solution)/shard_map/ppermute | solution.py:477
  130.3 10.0 %collective-permute-start.19 = (bf16[128,1536]{1,0:T(8,128)(2,1)S(1)}, bf16[128,1536]{1,0:T(8,128)(2,1)S(1)}, u32[]{:S(2)}, u32[]{:S(2)}) collective-permute-start(bf16[128,1536]{1,0:T(8,128)(2,1)S(1)} %add_add_fusion), channel_id=1, source_target_pairs={{0,1},{1,0},{2,3},{3,2},{4,5},{5,4},{6,7},{7,6},{8,9},{9,8},{10,11... | collective-permute-start | bytes 1179656 | tf_op jit(solution)/shard_map/ppermute | solution.py:481
  137.7 7.8 %collective-permute-start.21 = (bf16[128,1536]{1,0:T(8,128)(2,1)S(1)}, bf16[128,1536]{1,0:T(8,128)(2,1)S(1)}, u32[]{:S(2)}, u32[]{:S(2)}) collective-permute-start(bf16[128,1536]{1,0:T(8,128)(2,1)S(1)} %pad_maximum_fusion), channel_id=1, source_target_pairs={{0,6},{1,7},{2,0},{3,1},{4,2},{5,3},{6,4},{7,5},{8,14},{9,15},{10,... | collective-permute-start | bytes 1179656 | tf_op jit(solution)/shard_map/ppermute | solution.py:477
  137.8 9.1 %collective-permute-start.23 = (bf16[128,1536]{1,0:T(8,128)(2,1)S(1)}, bf16[128,1536]{1,0:T(8,128)(2,1)S(1)}, u32[]{:S(2)}, u32[]{:S(2)}) collective-permute-start(bf16[128,1536]{1,0:T(8,128)(2,1)S(1)} %pad_maximum_fusion.1), channel_id=1, source_target_pairs={{0,2},{1,3},{2,4},{3,5},{4,6},{5,7},{6,0},{7,1},{8,10},{9,11},{10,... | collective-permute-start | bytes 1179656 | tf_op jit(solution)/shard_map/ppermute | solution.py:477
  149.2 16.6 %all-to-all-start.1 = ((bf16[8,144,448]{2,1,0:T(8,128)(2,1)}), bf16[8,144,448]{2,1,0:T(8,128)(2,1)S(1)}, u32[]{:S(2)}, u32[]{:S(2)}) async-start(bf16[8,144,448]{2,1,0:T(8,128)(2,1)} %get-tuple-element.71), calls=%async_computation.1 | async-start | bytes 2359296 | tf_op jit(solution)/shard_map/all_to_all | solution.py:601
  170.2 1.8 collective-permute-start.24
  187.9 15.6 %all-to-all-start.3 = ((bf16[8,16,1536]{2,1,0:T(8,128)(2,1)}), bf16[8,16,1536]{2,1,0:T(8,128)(2,1)S(1)}, u32[]{:S(2)}, u32[]{:S(2)}) async-start(bf16[8,16,1536]{2,1,0:T(8,128)(2,1)} %fold.1), calls=%async_computation.3 | async-start | bytes 786432 | tf_op jit(solution)/shard_map/all_to_all | solution.py:608
  (25 other events, 199.7 us)
Sparse Core Ops, SparseCore 0:
  9.7 54.0 all-gather.1
  125.7 69.6 reduce-scatter.1

commit v6 on v5

--- a/solution.py
+++ b/solution.py
@@ -136,7 +136,7 @@
         + [spec] * 3,
         out_specs=[spec] * 3,
         out_shape=[jax.ShapeDtypeStruct((TOK, WIDTH), BF)] * 3,
-        compiler_params=params(),
+        compiler_params=params(VMEM_MOST),
         name="spatial_bwd",
         cost_estimate=cost(9),
     )(grad_input, whole_out, q, k, v)
@@ -319,18 +319,17 @@
 SLOT = 16
 FOUR = 4
 EXTRA = 16
-GROUPED = DP * SLOT
+GROUPED = DP * SHARE
 
 
 def mover():
-    shape = (FOUR * SHARE * SEQ, FOUR * SLOT * SEQ)
-    source = lax.broadcasted_iota(jnp.int32, shape, 0)
-    target = lax.broadcasted_iota(jnp.int32, shape, 1)
-    group = target // (FOUR * SLOT)
-    block = (target // SLOT) % FOUR
-    turn = target % SLOT
-    wanted = block * (SHARE * SEQ) + group * SHARE + turn
-    return jnp.where((source == wanted) & (turn < SHARE), 1.0, 0.0).astype(BF)
+    size = FOUR * SHARE * SEQ
+    source = lax.broadcasted_iota(jnp.int32, (size, size), 0)
+    target = lax.broadcasted_iota(jnp.int32, (size, size), 1)
+    group = target // (FOUR * SHARE)
+    block = (target // SHARE) % FOUR
+    wanted = block * (SHARE * SEQ) + group * SHARE + target % SHARE
+    return jnp.where(source == wanted, 1.0, 0.0).astype(BF)
 
 
 def two_parts(row):
@@ -356,7 +355,7 @@
     extra = jnp.where(row == 0, gain_high.astype(F32), jnp.where(row == 1, gain_low.astype(F32), 0.0))
     both = jnp.concatenate([grad, extra.astype(BF)], axis=0)
     move = mover()
-    rows, cols = FOUR * SHARE * SEQ, FOUR * SLOT
+    rows, cols = FOUR * SHARE * SEQ, FOUR * SHARE
     for four in range(DP // FOUR):
         moved = dot_nn(both[:, four * rows : (four + 1) * rows], move).astype(BF)
         for j in range(SEQ):
@@ -382,21 +381,24 @@
     @pl.when(pl.program_id(0) == 0)
     def _():
         for r in range(SEQ):
-            turned[:, r * TOK : (r + 1) * TOK] = groups_ref[order_ref[r], :TOK].T
+            turned[:, r * TOK : (r + 1) * TOK] = groups_ref[order_ref[r], :TOK, :GROUPED].T
 
     product = dot_nn(turned[...], mixed_ref[...]) * factor
-    extras = sum(groups_ref[r, TOK:].astype(F32) for r in range(SEQ))
-    high, low = two_parts(extras[0:1] + extras[1:2])
-    turn = lax.broadcasted_iota(jnp.int32, (GROUPED, GROUPED), 0) % SLOT
-    first = pl.program_id(0) == 0
-    begin = product[:, :GROUPED]
-    for place, part in ((SHARE, high), (SHARE + 1, low)):
-        begin = jnp.where((turn == place) & first, part.astype(F32), begin)
-    product = jnp.concatenate([begin, product[:, GROUPED:]], axis=1).astype(BF)
+    cols = product.shape[1]
+    extras = sum(groups_ref[r, TOK:, :GROUPED].astype(F32) for r in range(SEQ))
+    gain_parts = jnp.concatenate(
+        [part.astype(F32) for part in two_parts(extras[0:1] + extras[1:2])], axis=0
+    )
+    gain_parts = jnp.concatenate([gain_parts, jnp.zeros((2, cols - GROUPED), F32)], axis=1)
+    gain_parts = jnp.where(pl.program_id(0) == 0, gain_parts, 0.0)
+    tail = jnp.concatenate([gain_parts, jnp.zeros((SLOT - SHARE - 2, cols), F32)], axis=0)
+
+    def block(d):
+        return jnp.concatenate([product[d * SHARE : (d + 1) * SHARE], tail], axis=0).astype(BF)
+
     first_core = order_ref[SEQ] == 0
     for d in range(DP // 2):
-        even = product[2 * d * SLOT : (2 * d + 1) * SLOT]
-        odd = product[(2 * d + 1) * SLOT : (2 * d + 2) * SLOT]
+        even, odd = block(2 * d), block(2 * d + 1)
         mine_ref[d] = jnp.where(first_core, even, odd)
         other_ref[d] = jnp.where(first_core, odd, even)
 
@@ -410,7 +412,7 @@
             num_scalar_prefetch=1,
             grid=(WIDTH // cols,),
             in_specs=[
-                pl.BlockSpec((SEQ, TOK + EXTRA, GROUPED), lambda i, o: (0, 0, 0)),
+                pl.BlockSpec(groups.shape, lambda i, o: (0, 0, 0)),
                 pl.BlockSpec((SEQ * TOK, cols), lambda i, o: (0, i)),
             ],
             out_specs=[spec, spec],
@@ -450,7 +452,7 @@
         [in_ref[j].astype(F32)[:SHARE] for j in range(SEQ)], axis=0
     )
     move = mover()
-    rows, cols = FOUR * SHARE * SEQ, FOUR * SLOT
+    rows, cols = FOUR * SHARE * SEQ, FOUR * SHARE
     for four in range(DP // FOUR):
         left = jnp.concatenate(
             [in_ref[j, :, four * cols : (four + 1) * cols] for j in range(SEQ)], axis=1

time: 213 us -> 211 us (level)
  local copies, waits for them, and re-layouts: 19.9 us -> 17.3 us
    unnamed x61 -> x51, local copies, waits for them, and re-layouts: 14.1 us -> 11.3 us
  transfers between devices with their start and end apart: 30 -> 30, of which waited for: 17 -> 17; matrix products, arithmetic and copies ran while one was open for 9% -> 9% of each run, Pallas kernels for 11% -> 12%
where the time goes in v6:
time: 211 us; the launch traced here: 210 us
  starting transfers between devices  64.2 us (30%)
  waiting for transfers between devices  45.7 us (22%)
  Pallas kernels  43.5 us (21%)
  local copies, waits for them, and re-layouts  17.3 us (8%)
  blocking collectives  14.8 us (7%)
  between operations  14.5 us (7%)
  matrix products  5.63 us (3%)
  other arithmetic  4.3 us (2%)
    ppermute x18, starting transfers between devices, along_x(): return lax.ppermute(array, 'seq', pairs)  32.7 us
    ppermute x18, waiting for transfers between devices, along_x(): return lax.ppermute(array, 'seq', pairs)  22.5 us
    ppermute x6, starting transfers between devices, across_y(): return lax.ppermute(array, 'seq', [(i, i ^ 1) for i in range(SEQ)])  17.4 us
    all_to_all x1, blocking collectives, chip_exchange(): lax.all_to_all(blocks, 'dp', 0, 0, axis_index_groups=groups, tiled=True)  14.8 us
    unnamed x51, local copies, waits for them, and re-layouts  11.3 us
    pallas_call x1, Pallas kernels, spatial_bwd(): pl.pallas_call(spatial_bwd_kernel, grid=(WIDTH // (PAIRS * LANE),), in_sp...  8.8 us
    all_to_all x1, waiting for transfers between devices, body(): lax.all_to_all(dout.reshape(TOK, SEQ, GROUP).transpose(1, 0, 2), 'seq', 0...  7.54 us
    pallas_call x1, Pallas kernels, out_norm(): pl.pallas_call(out_norm_kernel, grid=(WIDTH // OUT_BLOCK,), in_specs=[who...  6.71 us
  transfers between devices with their start and end apart: 30, of which 17 were waited for; matrix products, arithmetic and copies ran while one was open for 9% of the time, Pallas kernels for 12%

profile of v6, /device:TPU:0, one launch (start us, length us, event | category | flops | bytes accessed | tf_op | source)
XLA Modules:
  0.0 209.9 jit_solution(9089596452823210688)
XLA Ops:
  9.1 4.6 %spatial_fwd.1.mixed_ref = bf16[128,1536]{1,0:T(8,128)(2,1)} custom-call(bf16[128,1536]{1,0:T(8,128)(2,1)} %bitcast.41, bf16[128,1536]{1,0:T(8,128)(2,1)} %bitcast.43, bf16[128,1536]{1,0:T(8,128)(2,1)} %bitcast.45), custom_call_target="tpu_custom_call" | custom-call | bytes 12000000 | tf_op jit(solution)/shard_map/spatial_fwd/pallas_call | solution.py:102
  13.7 3.3 %collective-permute-start.3 = (bf16[128,1536]{1,0:T(8,128)(2,1)}, bf16[128,1536]{1,0:T(8,128)(2,1)}, u32[]{:S(2)}, u32[]{:S(2)}) collective-permute-start(bf16[128,1536]{1,0:T(8,128)(2,1)} %spatial_fwd.1.mixed_ref), channel_id=1, source_target_pairs={{0,1},{1,0},{2,3},{3,2},{4,5},{5,4},{6,7},{7,6},{8,9},{9,8},{10,11... | collective-permute-start | bytes 1179656 | tf_op jit(solution)/shard_map/ppermute | solution.py:483
  20.0 4.1 %all-to-all-start = ((bf16[8,128,192]{1,2,0:T(8,128)(2,1)}), bf16[8,128,192]{1,2,0:T(8,128)(2,1)}, u32[]{:S(2)}, u32[]{:S(2)}) async-start(bf16[8,128,192]{1,2,0:T(8,128)(2,1)} %copy.20), calls=%async_computation | async-start | bytes 786432 | tf_op jit(solution)/shard_map/all_to_all | solution.py:579
  24.1 3.2 %collective-permute-start.1 = (bf16[128,1536]{1,0:T(8,128)(2,1)S(1)}, bf16[128,1536]{1,0:T(8,128)(2,1)}, u32[]{:S(2)}, u32[]{:S(2)}) collective-permute-start(bf16[128,1536]{1,0:T(8,128)(2,1)S(1)} %copy-done.19), channel_id=1, source_target_pairs={{0,6},{1,7},{2,0},{3,1},{4,2},{5,3},{6,4},{7,5},{8,14},{9,15},{10,... | collective-permute-start | bytes 1179656 | tf_op jit(solution)/shard_map/ppermute | solution.py:479
  28.8 7.5 %all-to-all-done = bf16[8,128,192]{1,2,0:T(8,128)(2,1)} async-done(((bf16[8,128,192]{1,2,0:T(8,128)(2,1)}), bf16[8,128,192]{1,2,0:T(8,128)(2,1)}, u32[]{:S(2)}, u32[]{:S(2)}) %all-to-all-start) | async-done | bytes 393248 | tf_op jit(solution)/shard_map/all_to_all | solution.py:579
  42.7 5.9 %collective-permute-start.6 = (bf16[128,1536]{1,0:T(8,128)(2,1)}, bf16[128,1536]{1,0:T(8,128)(2,1)S(1)}, u32[]{:S(2)}, u32[]{:S(2)}) collective-permute-start(bf16[128,1536]{1,0:T(8,128)(2,1)} %collective-permute-done.3), channel_id=1, source_target_pairs={{0,4},{1,5},{2,6},{3,7},{4,0},{5,1},{6,2},{7,3},{8,12},{9,13},{10,... | collective-permute-start | bytes 1179656 | tf_op jit(solution)/shard_map/ppermute | solution.py:479
  52.7 2.5 %collective-permute-done.4 = bf16[128,1536]{1,0:T(8,128)(2,1)S(1)} collective-permute-done((bf16[128,1536]{1,0:T(8,128)(2,1)}, bf16[128,1536]{1,0:T(8,128)(2,1)S(1)}, u32[]{:S(2)}, u32[]{:S(2)}) %collective-permute-start.4) | collective-permute-done | bytes 393248 | tf_op jit(solution)/shard_map/ppermute | solution.py:479
  55.2 2.1 %collective-permute-done.5 = bf16[128,1536]{1,0:T(8,128)(2,1)S(1)} collective-permute-done((bf16[128,1536]{1,0:T(8,128)(2,1)}, bf16[128,1536]{1,0:T(8,128)(2,1)S(1)}, u32[]{:S(2)}, u32[]{:S(2)}) %collective-permute-start.5) | collective-permute-done | bytes 393248 | tf_op jit(solution)/shard_map/ppermute | solution.py:479
  61.2 2.6 %all-gather.2.cloned.1.call-done.w_ref = bf16[1536,2112]{1,0:T(8,128)(2,1)} async-done(((bf16[96,2112]{1,0:T(8,128)(2,1)}), bf16[1536,2112]{1,0:T(8,128)(2,1)}) %all-gather.2.cloned.1.call-update) | async-done | bytes 6488080 | tf_op jit(solution)/shard_map/all_gather | solution.py:574
  63.8 6.7 %out_norm.1 = (bf16[128,1536]{1,0:T(8,128)(2,1)}, bf16[128,1536]{1,0:T(8,128)(2,1)}, bf16[1536,768]{1,0:T(8,128)(2,1)}) custom-call(bf16[128,1536]{1,0:T(8,128)(2,1)} %spatial_fwd.1.mixed_ref, bf16[1536,2112]{1,0:T(8,128)(2,1)} %all-gather.2.cloned.1.call-done.w_ref, bf16[128,1536]{1,0:T(8,128)(2,1)} %bitcast.48, f32[1,1536]{1,0:T(1,128)} %reshape.55.gain_ref), custom_call_target="tpu_custom_call" | custom-call | bytes 15000000 | tf_op jit(solution)/shard_map/out_norm/pallas_call | solution.py:179
  70.5 4.6 %collective-permute-start.8 = (bf16[128,1536]{1,0:T(8,128)(2,1)}, bf16[128,1536]{1,0:T(8,128)(2,1)S(1)}, u32[]{:S(2)}, u32[]{:S(2)}) collective-permute-start(bf16[128,1536]{1,0:T(8,128)(2,1)} %get-tuple-element.50.refs_0_), channel_id=1, source_target_pairs={{0,6},{1,7},{2,0},{3,1},{4,2},{5,3},{6,4},{7,5},{8,14},{9,15},{10,... | collective-permute-start | bytes 1179656 | tf_op jit(solution)/shard_map/ppermute | solution.py:479
  75.2 3.0 %collective-permute-start.11 = (bf16[128,1536]{1,0:T(8,128)(2,1)}, bf16[128,1536]{1,0:T(8,128)(2,1)S(1)}, u32[]{:S(2)}, u32[]{:S(2)}) collective-permute-start(bf16[128,1536]{1,0:T(8,128)(2,1)} %get-tuple-element.50.refs_0_), channel_id=1, source_target_pairs={{0,1},{1,0},{2,3},{3,2},{4,5},{5,4},{6,7},{7,6},{8,9},{9,8},{10,11... | collective-permute-start | bytes 1179656 | tf_op jit(solution)/shard_map/ppermute | solution.py:483
  78.2 2.3 %convolution_convert_fusion.7.refs_0_ = bf16[128,768]{1,0:T(8,128)(2,1)S(1)} fusion(bf16[128,1536]{1,0:T(8,128)(2,1)} %get-tuple-element.50.refs_0_, bf16[1536,768]{1,0:T(8,128)(2,1)} %get-tuple-element.51.w_ref), kind=kOutput, calls=%fused_computation.7 | convolution fusion | flops 302088192 | bytes 2949120 | tf_op jit(solution)/shard_map/dot_general | solution.py:45
  82.4 3.6 %collective-permute-start.10 = (bf16[64,1536]{1,0:T(8,128)(2,1)S(1)}, bf16[64,1536]{1,0:T(8,128)(2,1)S(1)}, u32[]{:S(2)}, u32[]{:S(2)}) collective-permute-start(bf16[64,1536]{1,0:T(8,128)(2,1)S(1)} %slice.37), channel_id=1, source_target_pairs={{0,6},{1,7},{2,0},{3,1},{4,2},{5,3},{6,4},{7,5},{8,14},{9,15},{10,... | collective-permute-start | bytes 589832 | tf_op jit(solution)/shard_map/ppermute | solution.py:479
  87.9 3.1 %collective-permute-start.13 = (bf16[128,1536]{1,0:T(8,128)(2,1)S(1)}, bf16[128,1536]{1,0:T(8,128)(2,1)S(1)}, u32[]{:S(2)}, u32[]{:S(2)}) collective-permute-start(bf16[128,1536]{1,0:T(8,128)(2,1)S(1)} %collective-permute-done.11.refs_5_), channel_id=1, source_target_pairs={{0,6},{1,7},{2,0},{3,1},{4,2},{5,3},{6,4},{7,5},{8,14},{9,15},{10,... | collective-permute-start | bytes 1179656 | tf_op jit(solution)/shard_map/ppermute | solution.py:479
  91.0 3.0 %collective-permute-start.15 = (bf16[64,1536]{1,0:T(8,128)(2,1)S(1)}, bf16[64,1536]{1,0:T(8,128)(2,1)S(1)}, u32[]{:S(2)}, u32[]{:S(2)}) collective-permute-start(bf16[64,1536]{1,0:T(8,128)(2,1)S(1)} %collective-permute-done.10.refs_4_), channel_id=1, source_target_pairs={{0,1},{1,0},{2,3},{3,2},{4,5},{5,4},{6,7},{7,6},{8,9},{9,8},{10,11... | collective-permute-start | bytes 589832 | tf_op jit(solution)/shard_map/ppermute | solution.py:483
  95.7 3.2 %collective-permute-start.14 = (bf16[64,1536]{1,0:T(8,128)(2,1)S(1)}, bf16[64,1536]{1,0:T(8,128)(2,1)S(1)}, u32[]{:S(2)}, u32[]{:S(2)}) collective-permute-start(bf16[64,1536]{1,0:T(8,128)(2,1)S(1)} %collective-permute-done.9.refs_3_), channel_id=1, source_target_pairs={{0,1},{1,0},{2,3},{3,2},{4,5},{5,4},{6,7},{7,6},{8,9},{9,8},{10,11... | collective-permute-start | bytes 589832 | tf_op jit(solution)/shard_map/ppermute | solution.py:483
  100.7 2.4 %collective-permute-done.14.refs_8_ = bf16[64,1536]{1,0:T(8,128)(2,1)S(1)} collective-permute-done((bf16[64,1536]{1,0:T(8,128)(2,1)S(1)}, bf16[64,1536]{1,0:T(8,128)(2,1)S(1)}, u32[]{:S(2)}, u32[]{:S(2)}) %collective-permute-start.14) | collective-permute-done | bytes 196640 | tf_op jit(solution)/shard_map/ppermute | solution.py:483
  103.6 5.5 %temporal.1 = (bf16[8,128,192]{2,1,0:T(8,128)(2,1)S(1)}, bf16[8,128,768]{2,1,0:T(8,128)(2,1)S(1)}) custom-call(s32[9]{0:T(128)S(1)} %stack.39.order_ref, bf16[128,768]{1,0:T(8,128)(2,1)S(1)} %convolution_convert_fusion.7.refs_0_, bf16[128,768]{1,0:T(8,128)(2,1)S(1)} %convolution_convert_fusion.6.refs_1_, ...), custom_call_target="tpu_custom_call" | custom-call | bytes 24000000 | tf_op jit(solution)/shard_map/temporal/pallas_call | solution.py:244
  109.1 2.8 %shares.2 = (bf16[128,1536]{1,0:T(8,128)(2,1)S(1)}, bf16[128,1536]{1,0:T(8,128)(2,1)}, bf16[128,1536]{1,0:T(8,128)(2,1)}, bf16[128,1536]{1,0:T(8,128)(2,1)}) custom-call(bf16[8,128,768]{2,1,0:T(8,128)(2,1)S(1)} %get-tuple-element.58.dproj_ref.refs_10_, bf16[1536,768]{1,0:T(8,128)(2,1)S(1)} %copy-done), custom_call_target="tpu_custom_call" | custom-call | bytes 6000000 | tf_op jit(solution)/shard_map/shares/pallas_call | solution.py:274
  111.9 3.0 %collective-permute-start.16 = (bf16[128,1536]{1,0:T(8,128)(2,1)}, bf16[128,1536]{1,0:T(8,128)(2,1)}, u32[]{:S(2)}, u32[]{:S(2)}) collective-permute-start(bf16[128,1536]{1,0:T(8,128)(2,1)} %get-tuple-element.61), channel_id=1, source_target_pairs={{0,1},{1,0},{2,3},{3,2},{4,5},{5,4},{6,7},{7,6},{8,9},{9,8},{10,11... | collective-permute-start | bytes 1179656 | tf_op jit(solution)/shard_map/ppermute | solution.py:483
  121.1 4.4 %qkv_product.1 = bf16[1536,576]{1,0:T(8,128)(2,1)} custom-call(bf16[128,1536]{1,0:T(8,128)(2,1)S(1)} %copy-done.6, bf16[128,1536]{1,0:T(8,128)(2,1)S(1)} %collective-permute-done.7.refs_1_, bf16[128,1536]{1,0:T(8,128)(2,1)S(1)} %collective-permute-done.8.refs_2_, bf16[64,1536]{1,0:T(8,128)(2,1)S(1)} %collective-permute-done.9.refs_3_, ...), custom_call_target="tpu_custom_call" | custom-call | bytes 15000000 | tf_op jit(solution)/shard_map/qkv_product/pallas_call | solution.py:305
  133.9 3.7 %collective-permute-done.22 = bf16[64,1536]{1,0:T(8,128)(2,1)S(1)} collective-permute-done((bf16[64,1536]{1,0:T(8,128)(2,1)S(1)}, bf16[64,1536]{1,0:T(8,128)(2,1)S(1)}, u32[]{:S(2)}, u32[]{:S(2)}) %collective-permute-start.22) | collective-permute-done | bytes 196640 | tf_op jit(solution)/shard_map/ppermute | solution.py:479
  140.3 5.2 %collective-permute-done.21.sum_c = bf16[128,1536]{1,0:T(8,128)(2,1)S(1)} collective-permute-done((bf16[128,1536]{1,0:T(8,128)(2,1)S(1)}, bf16[128,1536]{1,0:T(8,128)(2,1)S(1)}, u32[]{:S(2)}, u32[]{:S(2)}) %collective-permute-start.21) | collective-permute-done | bytes 393248 | tf_op jit(solution)/shard_map/ppermute | solution.py:479
  146.9 2.6 %grad_input.1 = (bf16[128,1536]{1,0:T(8,128)(2,1)}, bf16[8,144,384]{2,1,0:T(8,128)(2,1)}) custom-call(bf16[128,1536]{1,0:T(8,128)(2,1)S(1)} %get-tuple-element.59.sum_a, bf16[128,1536]{1,0:T(8,128)(2,1)S(1)} %collective-permute-done.19.sum_b, bf16[128,1536]{1,0:T(8,128)(2,1)S(1)} %collective-permute-done.21.sum_c, ...), custom_call_target="tpu_custom_call" | custom-call | bytes 6000000 | tf_op jit(solution)/shard_map/grad_input/pallas_call | solution.py:368
  149.5 3.8 %all-to-all-start.1 = ((bf16[8,144,384]{2,1,0:T(8,128)(2,1)}), bf16[8,144,384]{2,1,0:T(8,128)(2,1)S(1)}, u32[]{:S(2)}, u32[]{:S(2)}) async-start(bf16[8,144,384]{2,1,0:T(8,128)(2,1)} %get-tuple-element.71), calls=%async_computation.1 | async-start | bytes 1769472 | tf_op jit(solution)/shard_map/all_to_all | solution.py:603
  153.3 8.8 %spatial_bwd.1 = (bf16[128,1536]{1,0:T(8,128)(2,1)}, bf16[128,1536]{1,0:T(8,128)(2,1)}, bf16[128,1536]{1,0:T(8,128)(2,1)}) custom-call(bf16[128,1536]{1,0:T(8,128)(2,1)} %get-tuple-element.72.gi_ref, bf16[1536,2112]{1,0:T(8,128)(2,1)} %all-gather.2.cloned.1.call-done.w_ref, bf16[128,1536]{1,0:T(8,128)(2,1)} %bitcast.42, bf16[128,1536]{1,0:T(8,128)(2,1)} %bitcast.44, ...), custom_call_target="tpu_custom_call" | custom-call | bytes 27000000 | tf_op jit(solution)/shard_map/spatial_bwd/pallas_call | solution.py:129
  162.1 2.6 %all-to-all-done.1.groups_ref = bf16[8,144,384]{2,1,0:T(8,128)(2,1)S(1)} async-done(((bf16[8,144,384]{2,1,0:T(8,128)(2,1)}), bf16[8,144,384]{2,1,0:T(8,128)(2,1)S(1)}, u32[]{:S(2)}, u32[]{:S(2)}) %all-to-all-start.1) | async-done | bytes 884768 | tf_op jit(solution)/shard_map/all_to_all | solution.py:603
  166.7 2.3 %out_product.1 = (bf16[8,16,1536]{2,1,0:T(8,128)(2,1)S(1)}, bf16[8,16,1536]{2,1,0:T(8,128)(2,1)S(1)}) custom-call(s32[9]{0:T(128)S(1)} %stack.39.order_ref, bf16[8,144,384]{2,1,0:T(8,128)(2,1)S(1)} %all-to-all-done.1.groups_ref, bf16[1024,1536]{1,0:T(8,128)(2,1)S(1)} %copy-done.2), custom_call_target="tpu_custom_call" | custom-call | bytes 9000000 | tf_op jit(solution)/shard_map/out_product/pallas_call | solution.py:409
  170.8 14.8 %all_to_all.20.in_ref = bf16[8,16,1536]{2,1,0:T(8,128)(2,1)S(1)} all-to-all(bf16[8,16,1536]{2,1,0:T(8,128)(2,1)S(1)} %add.102), channel_id=1, replica_groups={{0,16,32,48,64,80,96,112},{8,24,40,56,72,88,104,120},{1,17,33,49,65,81,..., dimensions={0} | all-to-all | bytes 786432 | tf_op jit(solution)/shard_map/all_to_all | solution.py:554
  186.4 6.1 %all-to-all-start.3 = ((bf16[8,16,1536]{2,1,0:T(8,128)(2,1)}), bf16[8,16,1536]{2,1,0:T(8,128)(2,1)S(1)}, u32[]{:S(2)}, u32[]{:S(2)}) async-start(bf16[8,16,1536]{2,1,0:T(8,128)(2,1)} %fold.1), calls=%async_computation.3 | async-start | bytes 786432 | tf_op jit(solution)/shard_map/all_to_all | solution.py:610
  195.8 5.9 %all-to-all-done.3.in_ref = bf16[8,16,1536]{2,1,0:T(8,128)(2,1)S(1)} async-done(((bf16[8,16,1536]{2,1,0:T(8,128)(2,1)}), bf16[8,16,1536]{2,1,0:T(8,128)(2,1)S(1)}, u32[]{:S(2)}, u32[]{:S(2)}) %all-to-all-start.3) | async-done | bytes 393248 | tf_op jit(solution)/shard_map/all_to_all | solution.py:610
  (122 shorter events, 56.5 us)
Async XLA Ops:
  7.2 56.6 %all-gather.2.cloned.1.call-start = ((), (), s32[]{:S(2)}) async-start(), calls=%async_computation.5 | async-start | bytes 7102464 | tf_op jit(solution)/shard_map/all_gather | solution.py:574
  9.1 19.1 %copy-start.21 = (f32[1536]{0:T(1024)S(1)}, f32[1536]{0:T(1024)}, u32[]{:S(2)}) copy-start(f32[1536]{0:T(1024)} %param.14) | copy-start | bytes 18436
  13.7 25.8 %collective-permute-start.3 = (bf16[128,1536]{1,0:T(8,128)(2,1)}, bf16[128,1536]{1,0:T(8,128)(2,1)}, u32[]{:S(2)}, u32[]{:S(2)}) collective-permute-start(bf16[128,1536]{1,0:T(8,128)(2,1)} %spatial_fwd.1.mixed_ref), channel_id=1, source_target_pairs={{0,1},{1,0},{2,3},{3,2},{4,5},{5,4},{6,7},{7,6},{8,9},{9,8},{10,11... | collective-permute-start | bytes 1179656 | tf_op jit(solution)/shard_map/ppermute | solution.py:483
  16.9 25.8 %collective-permute-start = (bf16[128,1536]{1,0:T(8,128)(2,1)}, bf16[128,1536]{1,0:T(8,128)(2,1)}, u32[]{:S(2)}, u32[]{:S(2)}) collective-permute-start(bf16[128,1536]{1,0:T(8,128)(2,1)} %spatial_fwd.1.mixed_ref), channel_id=1, source_target_pairs={{0,2},{1,3},{2,4},{3,5},{4,6},{5,7},{6,0},{7,1},{8,10},{9,11},{10,... | collective-permute-start | bytes 1179656 | tf_op jit(solution)/shard_map/ppermute | solution.py:479
  20.0 16.3 %all-to-all-start = ((bf16[8,128,192]{1,2,0:T(8,128)(2,1)}), bf16[8,128,192]{1,2,0:T(8,128)(2,1)}, u32[]{:S(2)}, u32[]{:S(2)}) async-start(bf16[8,128,192]{1,2,0:T(8,128)(2,1)} %copy.20), calls=%async_computation | async-start | bytes 786432 | tf_op jit(solution)/shard_map/all_to_all | solution.py:579
  24.1 170.2 %reduce-scatter.2.cloned.1.call-start = ((), (), s32[]{:S(2)}) async-start(), calls=%async_computation.6 | async-start | bytes 2088960 | tf_op jit(solution)/shard_map/reduce_scatter | solution.py:595
  24.1 25.5 %collective-permute-start.1 = (bf16[128,1536]{1,0:T(8,128)(2,1)S(1)}, bf16[128,1536]{1,0:T(8,128)(2,1)}, u32[]{:S(2)}, u32[]{:S(2)}) collective-permute-start(bf16[128,1536]{1,0:T(8,128)(2,1)S(1)} %copy-done.19), channel_id=1, source_target_pairs={{0,6},{1,7},{2,0},{3,1},{4,2},{5,3},{6,4},{7,5},{8,14},{9,15},{10,... | collective-permute-start | bytes 1179656 | tf_op jit(solution)/shard_map/ppermute | solution.py:479
  27.3 23.4 %collective-permute-start.2 = (bf16[128,1536]{1,0:T(8,128)(2,1)S(1)}, bf16[128,1536]{1,0:T(8,128)(2,1)}, u32[]{:S(2)}, u32[]{:S(2)}) collective-permute-start(bf16[128,1536]{1,0:T(8,128)(2,1)S(1)} %copy-done.19), channel_id=1, source_target_pairs={{0,4},{1,5},{2,6},{3,7},{4,0},{5,1},{6,2},{7,3},{8,12},{9,13},{10,... | collective-permute-start | bytes 1179656 | tf_op jit(solution)/shard_map/ppermute | solution.py:479
  39.4 15.8 %collective-permute-start.4 = (bf16[128,1536]{1,0:T(8,128)(2,1)}, bf16[128,1536]{1,0:T(8,128)(2,1)S(1)}, u32[]{:S(2)}, u32[]{:S(2)}) collective-permute-start(bf16[128,1536]{1,0:T(8,128)(2,1)} %collective-permute-done.3), channel_id=1, source_target_pairs={{0,2},{1,3},{2,4},{3,5},{4,6},{5,7},{6,0},{7,1},{8,10},{9,11},{10,... | collective-permute-start | bytes 1179656 | tf_op jit(solution)/shard_map/ppermute | solution.py:479
  40.8 16.5 %collective-permute-start.5 = (bf16[128,1536]{1,0:T(8,128)(2,1)}, bf16[128,1536]{1,0:T(8,128)(2,1)S(1)}, u32[]{:S(2)}, u32[]{:S(2)}) collective-permute-start(bf16[128,1536]{1,0:T(8,128)(2,1)} %collective-permute-done.3), channel_id=1, source_target_pairs={{0,6},{1,7},{2,0},{3,1},{4,2},{5,3},{6,4},{7,5},{8,14},{9,15},{10,... | collective-permute-start | bytes 1179656 | tf_op jit(solution)/shard_map/ppermute | solution.py:479
  42.7 16.7 %collective-permute-start.6 = (bf16[128,1536]{1,0:T(8,128)(2,1)}, bf16[128,1536]{1,0:T(8,128)(2,1)S(1)}, u32[]{:S(2)}, u32[]{:S(2)}) collective-permute-start(bf16[128,1536]{1,0:T(8,128)(2,1)} %collective-permute-done.3), channel_id=1, source_target_pairs={{0,4},{1,5},{2,6},{3,7},{4,0},{5,1},{6,2},{7,3},{8,12},{9,13},{10,... | collective-permute-start | bytes 1179656 | tf_op jit(solution)/shard_map/ppermute | solution.py:479
  70.5 11.9 %collective-permute-start.8 = (bf16[128,1536]{1,0:T(8,128)(2,1)}, bf16[128,1536]{1,0:T(8,128)(2,1)S(1)}, u32[]{:S(2)}, u32[]{:S(2)}) collective-permute-start(bf16[128,1536]{1,0:T(8,128)(2,1)} %get-tuple-element.50.refs_0_), channel_id=1, source_target_pairs={{0,6},{1,7},{2,0},{3,1},{4,2},{5,3},{6,4},{7,5},{8,14},{9,15},{10,... | collective-permute-start | bytes 1179656 | tf_op jit(solution)/shard_map/ppermute | solution.py:479
  75.2 10.9 %collective-permute-start.7 = (bf16[128,1536]{1,0:T(8,128)(2,1)}, bf16[128,1536]{1,0:T(8,128)(2,1)S(1)}, u32[]{:S(2)}, u32[]{:S(2)}) collective-permute-start(bf16[128,1536]{1,0:T(8,128)(2,1)} %get-tuple-element.50.refs_0_), channel_id=1, source_target_pairs={{0,2},{1,3},{2,4},{3,5},{4,6},{5,7},{6,0},{7,1},{8,10},{9,11},{10,... | collective-permute-start | bytes 1179656 | tf_op jit(solution)/shard_map/ppermute | solution.py:479
  75.2 11.9 %collective-permute-start.11 = (bf16[128,1536]{1,0:T(8,128)(2,1)}, bf16[128,1536]{1,0:T(8,128)(2,1)S(1)}, u32[]{:S(2)}, u32[]{:S(2)}) collective-permute-start(bf16[128,1536]{1,0:T(8,128)(2,1)} %get-tuple-element.50.refs_0_), channel_id=1, source_target_pairs={{0,1},{1,0},{2,3},{3,2},{4,5},{5,4},{6,7},{7,6},{8,9},{9,8},{10,11... | collective-permute-start | bytes 1179656 | tf_op jit(solution)/shard_map/ppermute | solution.py:483
  82.4 8.6 %collective-permute-start.10 = (bf16[64,1536]{1,0:T(8,128)(2,1)S(1)}, bf16[64,1536]{1,0:T(8,128)(2,1)S(1)}, u32[]{:S(2)}, u32[]{:S(2)}) collective-permute-start(bf16[64,1536]{1,0:T(8,128)(2,1)S(1)} %slice.37), channel_id=1, source_target_pairs={{0,6},{1,7},{2,0},{3,1},{4,2},{5,3},{6,4},{7,5},{8,14},{9,15},{10,... | collective-permute-start | bytes 589832 | tf_op jit(solution)/shard_map/ppermute | solution.py:479
  86.1 9.1 %collective-permute-start.9 = (bf16[64,1536]{1,0:T(8,128)(2,1)S(1)}, bf16[64,1536]{1,0:T(8,128)(2,1)S(1)}, u32[]{:S(2)}, u32[]{:S(2)}) collective-permute-start(bf16[64,1536]{1,0:T(8,128)(2,1)S(1)} %slice.36), channel_id=1, source_target_pairs={{0,2},{1,3},{2,4},{3,5},{4,6},{5,7},{6,0},{7,1},{8,10},{9,11},{10,... | collective-permute-start | bytes 589832 | tf_op jit(solution)/shard_map/ppermute | solution.py:479
  87.1 12.6 %collective-permute-start.12 = (bf16[128,1536]{1,0:T(8,128)(2,1)S(1)}, bf16[128,1536]{1,0:T(8,128)(2,1)S(1)}, u32[]{:S(2)}, u32[]{:S(2)}) collective-permute-start(bf16[128,1536]{1,0:T(8,128)(2,1)S(1)} %collective-permute-done.11.refs_5_), channel_id=1, source_target_pairs={{0,2},{1,3},{2,4},{3,5},{4,6},{5,7},{6,0},{7,1},{8,10},{9,11},{10,... | collective-permute-start | bytes 1179656 | tf_op jit(solution)/shard_map/ppermute | solution.py:479
  87.9 12.3 %collective-permute-start.13 = (bf16[128,1536]{1,0:T(8,128)(2,1)S(1)}, bf16[128,1536]{1,0:T(8,128)(2,1)S(1)}, u32[]{:S(2)}, u32[]{:S(2)}) collective-permute-start(bf16[128,1536]{1,0:T(8,128)(2,1)S(1)} %collective-permute-done.11.refs_5_), channel_id=1, source_target_pairs={{0,6},{1,7},{2,0},{3,1},{4,2},{5,3},{6,4},{7,5},{8,14},{9,15},{10,... | collective-permute-start | bytes 1179656 | tf_op jit(solution)/shard_map/ppermute | solution.py:479
  91.0 9.7 %collective-permute-start.15 = (bf16[64,1536]{1,0:T(8,128)(2,1)S(1)}, bf16[64,1536]{1,0:T(8,128)(2,1)S(1)}, u32[]{:S(2)}, u32[]{:S(2)}) collective-permute-start(bf16[64,1536]{1,0:T(8,128)(2,1)S(1)} %collective-permute-done.10.refs_4_), channel_id=1, source_target_pairs={{0,1},{1,0},{2,3},{3,2},{4,5},{5,4},{6,7},{7,6},{8,9},{9,8},{10,11... | collective-permute-start | bytes 589832 | tf_op jit(solution)/shard_map/ppermute | solution.py:483
  95.7 7.4 %collective-permute-start.14 = (bf16[64,1536]{1,0:T(8,128)(2,1)S(1)}, bf16[64,1536]{1,0:T(8,128)(2,1)S(1)}, u32[]{:S(2)}, u32[]{:S(2)}) collective-permute-start(bf16[64,1536]{1,0:T(8,128)(2,1)S(1)} %collective-permute-done.9.refs_3_), channel_id=1, source_target_pairs={{0,1},{1,0},{2,3},{3,2},{4,5},{5,4},{6,7},{7,6},{8,9},{9,8},{10,11... | collective-permute-start | bytes 589832 | tf_op jit(solution)/shard_map/ppermute | solution.py:483
  111.9 13.7 %collective-permute-start.16 = (bf16[128,1536]{1,0:T(8,128)(2,1)}, bf16[128,1536]{1,0:T(8,128)(2,1)}, u32[]{:S(2)}, u32[]{:S(2)}) collective-permute-start(bf16[128,1536]{1,0:T(8,128)(2,1)} %get-tuple-element.61), channel_id=1, source_target_pairs={{0,1},{1,0},{2,3},{3,2},{4,5},{5,4},{6,7},{7,6},{8,9},{9,8},{10,11... | collective-permute-start | bytes 1179656 | tf_op jit(solution)/shard_map/ppermute | solution.py:483
  114.8 10.8 %collective-permute-start.17 = (bf16[128,1536]{1,0:T(8,128)(2,1)}, bf16[128,1536]{1,0:T(8,128)(2,1)}, u32[]{:S(2)}, u32[]{:S(2)}) collective-permute-start(bf16[128,1536]{1,0:T(8,128)(2,1)} %get-tuple-element.62), channel_id=1, source_target_pairs={{0,6},{1,7},{2,0},{3,1},{4,2},{5,3},{6,4},{7,5},{8,14},{9,15},{10,... | collective-permute-start | bytes 1179656 | tf_op jit(solution)/shard_map/ppermute | solution.py:479
  115.2 10.4 %collective-permute-start.18 = (bf16[128,1536]{1,0:T(8,128)(2,1)}, bf16[128,1536]{1,0:T(8,128)(2,1)}, u32[]{:S(2)}, u32[]{:S(2)}) collective-permute-start(bf16[128,1536]{1,0:T(8,128)(2,1)} %get-tuple-element.63), channel_id=1, source_target_pairs={{0,2},{1,3},{2,4},{3,5},{4,6},{5,7},{6,0},{7,1},{8,10},{9,11},{10,... | collective-permute-start | bytes 1179656 | tf_op jit(solution)/shard_map/ppermute | solution.py:479
  127.0 7.0 %collective-permute-start.20 = (bf16[64,1536]{1,0:T(8,128)(2,1)S(1)}, bf16[64,1536]{1,0:T(8,128)(2,1)S(1)}, u32[]{:S(2)}, u32[]{:S(2)}) collective-permute-start(bf16[64,1536]{1,0:T(8,128)(2,1)S(1)} %get-tuple-element.90), channel_id=1, source_target_pairs={{0,6},{1,7},{2,0},{3,1},{4,2},{5,3},{6,4},{7,5},{8,14},{9,15},{10,... | collective-permute-start | bytes 589832 | tf_op jit(solution)/shard_map/ppermute | solution.py:479
  128.6 18.3 %copy-start.18 = (f32[1,1536]{1,0:T(1,128)S(1)}, f32[1,1536]{1,0:T(1,128)}, u32[]{:S(2)}) copy-start(f32[1,1536]{1,0:T(1,128)} %reshape.55.gain_ref) | copy-start | bytes 18436
  128.6 9.0 %collective-permute-start.22 = (bf16[64,1536]{1,0:T(8,128)(2,1)S(1)}, bf16[64,1536]{1,0:T(8,128)(2,1)S(1)}, u32[]{:S(2)}, u32[]{:S(2)}) collective-permute-start(bf16[64,1536]{1,0:T(8,128)(2,1)S(1)} %get-tuple-element.89), channel_id=1, source_target_pairs={{0,2},{1,3},{2,4},{3,5},{4,6},{5,7},{6,0},{7,1},{8,10},{9,11},{10,... | collective-permute-start | bytes 589832 | tf_op jit(solution)/shard_map/ppermute | solution.py:479
  130.3 10.0 %collective-permute-start.19 = (bf16[128,1536]{1,0:T(8,128)(2,1)S(1)}, bf16[128,1536]{1,0:T(8,128)(2,1)S(1)}, u32[]{:S(2)}, u32[]{:S(2)}) collective-permute-start(bf16[128,1536]{1,0:T(8,128)(2,1)S(1)} %add_add_fusion), channel_id=1, source_target_pairs={{0,1},{1,0},{2,3},{3,2},{4,5},{5,4},{6,7},{7,6},{8,9},{9,8},{10,11... | collective-permute-start | bytes 1179656 | tf_op jit(solution)/shard_map/ppermute | solution.py:483
  137.7 7.8 %collective-permute-start.21 = (bf16[128,1536]{1,0:T(8,128)(2,1)S(1)}, bf16[128,1536]{1,0:T(8,128)(2,1)S(1)}, u32[]{:S(2)}, u32[]{:S(2)}) collective-permute-start(bf16[128,1536]{1,0:T(8,128)(2,1)S(1)} %pad_maximum_fusion), channel_id=1, source_target_pairs={{0,6},{1,7},{2,0},{3,1},{4,2},{5,3},{6,4},{7,5},{8,14},{9,15},{10,... | collective-permute-start | bytes 1179656 | tf_op jit(solution)/shard_map/ppermute | solution.py:479
  137.8 9.1 %collective-permute-start.23 = (bf16[128,1536]{1,0:T(8,128)(2,1)S(1)}, bf16[128,1536]{1,0:T(8,128)(2,1)S(1)}, u32[]{:S(2)}, u32[]{:S(2)}) collective-permute-start(bf16[128,1536]{1,0:T(8,128)(2,1)S(1)} %pad_maximum_fusion.1), channel_id=1, source_target_pairs={{0,2},{1,3},{2,4},{3,5},{4,6},{5,7},{6,0},{7,1},{8,10},{9,11},{10,... | collective-permute-start | bytes 1179656 | tf_op jit(solution)/shard_map/ppermute | solution.py:479
  149.5 15.3 %all-to-all-start.1 = ((bf16[8,144,384]{2,1,0:T(8,128)(2,1)}), bf16[8,144,384]{2,1,0:T(8,128)(2,1)S(1)}, u32[]{:S(2)}, u32[]{:S(2)}) async-start(bf16[8,144,384]{2,1,0:T(8,128)(2,1)} %get-tuple-element.71), calls=%async_computation.1 | async-start | bytes 1769472 | tf_op jit(solution)/shard_map/all_to_all | solution.py:603
  168.9 1.8 collective-permute-start.24
  186.4 15.3 %all-to-all-start.3 = ((bf16[8,16,1536]{2,1,0:T(8,128)(2,1)}), bf16[8,16,1536]{2,1,0:T(8,128)(2,1)S(1)}, u32[]{:S(2)}, u32[]{:S(2)}) async-start(bf16[8,16,1536]{2,1,0:T(8,128)(2,1)} %fold.1), calls=%async_computation.3 | async-start | bytes 786432 | tf_op jit(solution)/shard_map/all_to_all | solution.py:610
  (20 other events, 174.1 us)
Sparse Core Ops, SparseCore 0:
  9.7 54.0 all-gather.1
  125.7 68.4 reduce-scatter.1

commit v7 on v6

--- a/solution.py
+++ b/solution.py
@@ -286,7 +286,7 @@
     )(dproj, wide_proj)
 
 
-GRAD_ROWS = 512
+GRAD_ROWS = 384
 
 
 def qkv_grad_kernel(factor, *refs):
@@ -309,7 +309,7 @@
         + [pl.BlockSpec((SEQ, TOK, THREE), lambda i: (0, 0, 0))],
         out_specs=pl.BlockSpec((GRAD_ROWS, 3 * GROUP), lambda i: (i, 0)),
         out_shape=jax.ShapeDtypeStruct((WIDTH, 3 * GROUP), BF),
-        compiler_params=params(),
+        compiler_params=params(12 * 1024 * 1024),
         name="qkv_product",
         cost_estimate=cost(5),
     )(*frames, dproj)

time: 211 us -> 211 us (level)
  no operation moved by 1% of the time
where the time goes in v7:
time: 211 us; the launch traced here: 210 us
  starting transfers between devices  64.2 us (30%)
  waiting for transfers between devices  45.7 us (22%)
  Pallas kernels  43.9 us (21%)
  local copies, waits for them, and re-layouts  17.3 us (8%)
  blocking collectives  14.9 us (7%)
  between operations  14.5 us (7%)
  matrix products  5.63 us (3%)
  other arithmetic  4.3 us (2%)
    ppermute x18, starting transfers between devices, along_x(): return lax.ppermute(array, 'seq', pairs)  32.7 us
    ppermute x18, waiting for transfers between devices, along_x(): return lax.ppermute(array, 'seq', pairs)  22.5 us
    ppermute x6, starting transfers between devices, across_y(): return lax.ppermute(array, 'seq', [(i, i ^ 1) for i in range(SEQ)])  17.4 us
    all_to_all x1, blocking collectives, chip_exchange(): lax.all_to_all(blocks, 'dp', 0, 0, axis_index_groups=groups, tiled=True)  14.9 us
    unnamed x51, local copies, waits for them, and re-layouts  11.3 us
    pallas_call x1, Pallas kernels, spatial_bwd(): pl.pallas_call(spatial_bwd_kernel, grid=(WIDTH // (PAIRS * LANE),), in_sp...  8.81 us
    all_to_all x1, waiting for transfers between devices, body(): lax.all_to_all(dout.reshape(TOK, SEQ, GROUP).transpose(1, 0, 2), 'seq', 0...  7.54 us
    pallas_call x1, Pallas kernels, out_norm(): pl.pallas_call(out_norm_kernel, grid=(WIDTH // OUT_BLOCK,), in_specs=[who...  6.71 us
  transfers between devices with their start and end apart: 30, of which 17 were waited for; matrix products, arithmetic and copies ran while one was open for 9% of the time, Pallas kernels for 12%

profile of v7, /device:TPU:0, one launch (start us, length us, event | category | flops | bytes accessed | tf_op | source)
XLA Modules:
  0.0 210.3 jit_solution(13118352053689951723)
XLA Ops:
  9.1 4.6 %spatial_fwd.1.mixed_ref = bf16[128,1536]{1,0:T(8,128)(2,1)} custom-call(bf16[128,1536]{1,0:T(8,128)(2,1)} %bitcast.41, bf16[128,1536]{1,0:T(8,128)(2,1)} %bitcast.43, bf16[128,1536]{1,0:T(8,128)(2,1)} %bitcast.45), custom_call_target="tpu_custom_call" | custom-call | bytes 12000000 | tf_op jit(solution)/shard_map/spatial_fwd/pallas_call | solution.py:102
  13.7 3.3 %collective-permute-start.3 = (bf16[128,1536]{1,0:T(8,128)(2,1)}, bf16[128,1536]{1,0:T(8,128)(2,1)}, u32[]{:S(2)}, u32[]{:S(2)}) collective-permute-start(bf16[128,1536]{1,0:T(8,128)(2,1)} %spatial_fwd.1.mixed_ref), channel_id=1, source_target_pairs={{0,1},{1,0},{2,3},{3,2},{4,5},{5,4},{6,7},{7,6},{8,9},{9,8},{10,11... | collective-permute-start | bytes 1179656 | tf_op jit(solution)/shard_map/ppermute | solution.py:483
  20.0 4.1 %all-to-all-start = ((bf16[8,128,192]{1,2,0:T(8,128)(2,1)}), bf16[8,128,192]{1,2,0:T(8,128)(2,1)}, u32[]{:S(2)}, u32[]{:S(2)}) async-start(bf16[8,128,192]{1,2,0:T(8,128)(2,1)} %copy.20), calls=%async_computation | async-start | bytes 786432 | tf_op jit(solution)/shard_map/all_to_all | solution.py:579
  24.1 3.2 %collective-permute-start.1 = (bf16[128,1536]{1,0:T(8,128)(2,1)S(1)}, bf16[128,1536]{1,0:T(8,128)(2,1)}, u32[]{:S(2)}, u32[]{:S(2)}) collective-permute-start(bf16[128,1536]{1,0:T(8,128)(2,1)S(1)} %copy-done.19), channel_id=1, source_target_pairs={{0,6},{1,7},{2,0},{3,1},{4,2},{5,3},{6,4},{7,5},{8,14},{9,15},{10,... | collective-permute-start | bytes 1179656 | tf_op jit(solution)/shard_map/ppermute | solution.py:479
  28.8 7.5 %all-to-all-done = bf16[8,128,192]{1,2,0:T(8,128)(2,1)} async-done(((bf16[8,128,192]{1,2,0:T(8,128)(2,1)}), bf16[8,128,192]{1,2,0:T(8,128)(2,1)}, u32[]{:S(2)}, u32[]{:S(2)}) %all-to-all-start) | async-done | bytes 393248 | tf_op jit(solution)/shard_map/all_to_all | solution.py:579
  42.7 5.9 %collective-permute-start.6 = (bf16[128,1536]{1,0:T(8,128)(2,1)}, bf16[128,1536]{1,0:T(8,128)(2,1)S(1)}, u32[]{:S(2)}, u32[]{:S(2)}) collective-permute-start(bf16[128,1536]{1,0:T(8,128)(2,1)} %collective-permute-done.3), channel_id=1, source_target_pairs={{0,4},{1,5},{2,6},{3,7},{4,0},{5,1},{6,2},{7,3},{8,12},{9,13},{10,... | collective-permute-start | bytes 1179656 | tf_op jit(solution)/shard_map/ppermute | solution.py:479
  52.7 2.5 %collective-permute-done.4 = bf16[128,1536]{1,0:T(8,128)(2,1)S(1)} collective-permute-done((bf16[128,1536]{1,0:T(8,128)(2,1)}, bf16[128,1536]{1,0:T(8,128)(2,1)S(1)}, u32[]{:S(2)}, u32[]{:S(2)}) %collective-permute-start.4) | collective-permute-done | bytes 393248 | tf_op jit(solution)/shard_map/ppermute | solution.py:479
  55.2 2.1 %collective-permute-done.5 = bf16[128,1536]{1,0:T(8,128)(2,1)S(1)} collective-permute-done((bf16[128,1536]{1,0:T(8,128)(2,1)}, bf16[128,1536]{1,0:T(8,128)(2,1)S(1)}, u32[]{:S(2)}, u32[]{:S(2)}) %collective-permute-start.5) | collective-permute-done | bytes 393248 | tf_op jit(solution)/shard_map/ppermute | solution.py:479
  61.2 2.6 %all-gather.2.cloned.1.call-done.w_ref = bf16[1536,2112]{1,0:T(8,128)(2,1)} async-done(((bf16[96,2112]{1,0:T(8,128)(2,1)}), bf16[1536,2112]{1,0:T(8,128)(2,1)}) %all-gather.2.cloned.1.call-update) | async-done | bytes 6488080 | tf_op jit(solution)/shard_map/all_gather | solution.py:574
  63.8 6.7 %out_norm.1 = (bf16[128,1536]{1,0:T(8,128)(2,1)}, bf16[128,1536]{1,0:T(8,128)(2,1)}, bf16[1536,768]{1,0:T(8,128)(2,1)}) custom-call(bf16[128,1536]{1,0:T(8,128)(2,1)} %spatial_fwd.1.mixed_ref, bf16[1536,2112]{1,0:T(8,128)(2,1)} %all-gather.2.cloned.1.call-done.w_ref, bf16[128,1536]{1,0:T(8,128)(2,1)} %bitcast.48, f32[1,1536]{1,0:T(1,128)} %reshape.55.gain_ref), custom_call_target="tpu_custom_call" | custom-call | bytes 15000000 | tf_op jit(solution)/shard_map/out_norm/pallas_call | solution.py:179
  70.5 4.6 %collective-permute-start.8 = (bf16[128,1536]{1,0:T(8,128)(2,1)}, bf16[128,1536]{1,0:T(8,128)(2,1)S(1)}, u32[]{:S(2)}, u32[]{:S(2)}) collective-permute-start(bf16[128,1536]{1,0:T(8,128)(2,1)} %get-tuple-element.50.refs_0_), channel_id=1, source_target_pairs={{0,6},{1,7},{2,0},{3,1},{4,2},{5,3},{6,4},{7,5},{8,14},{9,15},{10,... | collective-permute-start | bytes 1179656 | tf_op jit(solution)/shard_map/ppermute | solution.py:479
  75.2 3.0 %collective-permute-start.11 = (bf16[128,1536]{1,0:T(8,128)(2,1)}, bf16[128,1536]{1,0:T(8,128)(2,1)S(1)}, u32[]{:S(2)}, u32[]{:S(2)}) collective-permute-start(bf16[128,1536]{1,0:T(8,128)(2,1)} %get-tuple-element.50.refs_0_), channel_id=1, source_target_pairs={{0,1},{1,0},{2,3},{3,2},{4,5},{5,4},{6,7},{7,6},{8,9},{9,8},{10,11... | collective-permute-start | bytes 1179656 | tf_op jit(solution)/shard_map/ppermute | solution.py:483
  78.2 2.3 %convolution_convert_fusion.7.refs_0_ = bf16[128,768]{1,0:T(8,128)(2,1)S(1)} fusion(bf16[128,1536]{1,0:T(8,128)(2,1)} %get-tuple-element.50.refs_0_, bf16[1536,768]{1,0:T(8,128)(2,1)} %get-tuple-element.51.w_ref), kind=kOutput, calls=%fused_computation.7 | convolution fusion | flops 302088192 | bytes 2949120 | tf_op jit(solution)/shard_map/dot_general | solution.py:45
  82.4 3.6 %collective-permute-start.10 = (bf16[64,1536]{1,0:T(8,128)(2,1)S(1)}, bf16[64,1536]{1,0:T(8,128)(2,1)S(1)}, u32[]{:S(2)}, u32[]{:S(2)}) collective-permute-start(bf16[64,1536]{1,0:T(8,128)(2,1)S(1)} %slice.37), channel_id=1, source_target_pairs={{0,6},{1,7},{2,0},{3,1},{4,2},{5,3},{6,4},{7,5},{8,14},{9,15},{10,... | collective-permute-start | bytes 589832 | tf_op jit(solution)/shard_map/ppermute | solution.py:479
  87.9 3.1 %collective-permute-start.13 = (bf16[128,1536]{1,0:T(8,128)(2,1)S(1)}, bf16[128,1536]{1,0:T(8,128)(2,1)S(1)}, u32[]{:S(2)}, u32[]{:S(2)}) collective-permute-start(bf16[128,1536]{1,0:T(8,128)(2,1)S(1)} %collective-permute-done.11.refs_5_), channel_id=1, source_target_pairs={{0,6},{1,7},{2,0},{3,1},{4,2},{5,3},{6,4},{7,5},{8,14},{9,15},{10,... | collective-permute-start | bytes 1179656 | tf_op jit(solution)/shard_map/ppermute | solution.py:479
  91.0 3.0 %collective-permute-start.15 = (bf16[64,1536]{1,0:T(8,128)(2,1)S(1)}, bf16[64,1536]{1,0:T(8,128)(2,1)S(1)}, u32[]{:S(2)}, u32[]{:S(2)}) collective-permute-start(bf16[64,1536]{1,0:T(8,128)(2,1)S(1)} %collective-permute-done.10.refs_4_), channel_id=1, source_target_pairs={{0,1},{1,0},{2,3},{3,2},{4,5},{5,4},{6,7},{7,6},{8,9},{9,8},{10,11... | collective-permute-start | bytes 589832 | tf_op jit(solution)/shard_map/ppermute | solution.py:483
  95.7 3.2 %collective-permute-start.14 = (bf16[64,1536]{1,0:T(8,128)(2,1)S(1)}, bf16[64,1536]{1,0:T(8,128)(2,1)S(1)}, u32[]{:S(2)}, u32[]{:S(2)}) collective-permute-start(bf16[64,1536]{1,0:T(8,128)(2,1)S(1)} %collective-permute-done.9.refs_3_), channel_id=1, source_target_pairs={{0,1},{1,0},{2,3},{3,2},{4,5},{5,4},{6,7},{7,6},{8,9},{9,8},{10,11... | collective-permute-start | bytes 589832 | tf_op jit(solution)/shard_map/ppermute | solution.py:483
  100.7 2.4 %collective-permute-done.14.refs_8_ = bf16[64,1536]{1,0:T(8,128)(2,1)S(1)} collective-permute-done((bf16[64,1536]{1,0:T(8,128)(2,1)S(1)}, bf16[64,1536]{1,0:T(8,128)(2,1)S(1)}, u32[]{:S(2)}, u32[]{:S(2)}) %collective-permute-start.14) | collective-permute-done | bytes 196640 | tf_op jit(solution)/shard_map/ppermute | solution.py:483
  103.6 5.5 %temporal.1 = (bf16[8,128,192]{2,1,0:T(8,128)(2,1)S(1)}, bf16[8,128,768]{2,1,0:T(8,128)(2,1)S(1)}) custom-call(s32[9]{0:T(128)S(1)} %stack.39.order_ref, bf16[128,768]{1,0:T(8,128)(2,1)S(1)} %convolution_convert_fusion.7.refs_0_, bf16[128,768]{1,0:T(8,128)(2,1)S(1)} %convolution_convert_fusion.6.refs_1_, ...), custom_call_target="tpu_custom_call" | custom-call | bytes 24000000 | tf_op jit(solution)/shard_map/temporal/pallas_call | solution.py:244
  109.1 2.8 %shares.2 = (bf16[128,1536]{1,0:T(8,128)(2,1)S(1)}, bf16[128,1536]{1,0:T(8,128)(2,1)}, bf16[128,1536]{1,0:T(8,128)(2,1)}, bf16[128,1536]{1,0:T(8,128)(2,1)}) custom-call(bf16[8,128,768]{2,1,0:T(8,128)(2,1)S(1)} %get-tuple-element.58.dproj_ref.refs_10_, bf16[1536,768]{1,0:T(8,128)(2,1)S(1)} %copy-done), custom_call_target="tpu_custom_call" | custom-call | bytes 6000000 | tf_op jit(solution)/shard_map/shares/pallas_call | solution.py:274
  111.9 3.0 %collective-permute-start.16 = (bf16[128,1536]{1,0:T(8,128)(2,1)}, bf16[128,1536]{1,0:T(8,128)(2,1)}, u32[]{:S(2)}, u32[]{:S(2)}) collective-permute-start(bf16[128,1536]{1,0:T(8,128)(2,1)} %get-tuple-element.61), channel_id=1, source_target_pairs={{0,1},{1,0},{2,3},{3,2},{4,5},{5,4},{6,7},{7,6},{8,9},{9,8},{10,11... | collective-permute-start | bytes 1179656 | tf_op jit(solution)/shard_map/ppermute | solution.py:483
  121.1 4.8 %qkv_product.1 = bf16[1536,576]{1,0:T(8,128)(2,1)} custom-call(bf16[128,1536]{1,0:T(8,128)(2,1)S(1)} %copy-done.6, bf16[128,1536]{1,0:T(8,128)(2,1)S(1)} %collective-permute-done.7.refs_1_, bf16[128,1536]{1,0:T(8,128)(2,1)S(1)} %collective-permute-done.8.refs_2_, bf16[64,1536]{1,0:T(8,128)(2,1)S(1)} %collective-permute-done.9.refs_3_, ...), custom_call_target="tpu_custom_call" | custom-call | bytes 15000000 | tf_op jit(solution)/shard_map/qkv_product/pallas_call | solution.py:305
  134.3 3.7 %collective-permute-done.22 = bf16[64,1536]{1,0:T(8,128)(2,1)S(1)} collective-permute-done((bf16[64,1536]{1,0:T(8,128)(2,1)S(1)}, bf16[64,1536]{1,0:T(8,128)(2,1)S(1)}, u32[]{:S(2)}, u32[]{:S(2)}) %collective-permute-start.22) | collective-permute-done | bytes 196640 | tf_op jit(solution)/shard_map/ppermute | solution.py:479
  140.7 5.2 %collective-permute-done.21.sum_c = bf16[128,1536]{1,0:T(8,128)(2,1)S(1)} collective-permute-done((bf16[128,1536]{1,0:T(8,128)(2,1)S(1)}, bf16[128,1536]{1,0:T(8,128)(2,1)S(1)}, u32[]{:S(2)}, u32[]{:S(2)}) %collective-permute-start.21) | collective-permute-done | bytes 393248 | tf_op jit(solution)/shard_map/ppermute | solution.py:479
  147.3 2.6 %grad_input.1 = (bf16[128,1536]{1,0:T(8,128)(2,1)}, bf16[8,144,384]{2,1,0:T(8,128)(2,1)}) custom-call(bf16[128,1536]{1,0:T(8,128)(2,1)S(1)} %get-tuple-element.59.sum_a, bf16[128,1536]{1,0:T(8,128)(2,1)S(1)} %collective-permute-done.19.sum_b, bf16[128,1536]{1,0:T(8,128)(2,1)S(1)} %collective-permute-done.21.sum_c, ...), custom_call_target="tpu_custom_call" | custom-call | bytes 6000000 | tf_op jit(solution)/shard_map/grad_input/pallas_call | solution.py:368
  149.8 3.8 %all-to-all-start.1 = ((bf16[8,144,384]{2,1,0:T(8,128)(2,1)}), bf16[8,144,384]{2,1,0:T(8,128)(2,1)S(1)}, u32[]{:S(2)}, u32[]{:S(2)}) async-start(bf16[8,144,384]{2,1,0:T(8,128)(2,1)} %get-tuple-element.71), calls=%async_computation.1 | async-start | bytes 1769472 | tf_op jit(solution)/shard_map/all_to_all | solution.py:603
  153.7 8.8 %spatial_bwd.1 = (bf16[128,1536]{1,0:T(8,128)(2,1)}, bf16[128,1536]{1,0:T(8,128)(2,1)}, bf16[128,1536]{1,0:T(8,128)(2,1)}) custom-call(bf16[128,1536]{1,0:T(8,128)(2,1)} %get-tuple-element.72.gi_ref, bf16[1536,2112]{1,0:T(8,128)(2,1)} %all-gather.2.cloned.1.call-done.w_ref, bf16[128,1536]{1,0:T(8,128)(2,1)} %bitcast.42, bf16[128,1536]{1,0:T(8,128)(2,1)} %bitcast.44, ...), custom_call_target="tpu_custom_call" | custom-call | bytes 27000000 | tf_op jit(solution)/shard_map/spatial_bwd/pallas_call | solution.py:129
  162.5 2.6 %all-to-all-done.1.groups_ref = bf16[8,144,384]{2,1,0:T(8,128)(2,1)S(1)} async-done(((bf16[8,144,384]{2,1,0:T(8,128)(2,1)}), bf16[8,144,384]{2,1,0:T(8,128)(2,1)S(1)}, u32[]{:S(2)}, u32[]{:S(2)}) %all-to-all-start.1) | async-done | bytes 884768 | tf_op jit(solution)/shard_map/all_to_all | solution.py:603
  167.0 2.3 %out_product.1 = (bf16[8,16,1536]{2,1,0:T(8,128)(2,1)S(1)}, bf16[8,16,1536]{2,1,0:T(8,128)(2,1)S(1)}) custom-call(s32[9]{0:T(128)S(1)} %stack.39.order_ref, bf16[8,144,384]{2,1,0:T(8,128)(2,1)S(1)} %all-to-all-done.1.groups_ref, bf16[1024,1536]{1,0:T(8,128)(2,1)S(1)} %copy-done.2), custom_call_target="tpu_custom_call" | custom-call | bytes 9000000 | tf_op jit(solution)/shard_map/out_product/pallas_call | solution.py:409
  171.2 14.9 %all_to_all.20.in_ref = bf16[8,16,1536]{2,1,0:T(8,128)(2,1)S(1)} all-to-all(bf16[8,16,1536]{2,1,0:T(8,128)(2,1)S(1)} %add.102), channel_id=1, replica_groups={{0,16,32,48,64,80,96,112},{8,24,40,56,72,88,104,120},{1,17,33,49,65,81,..., dimensions={0} | all-to-all | bytes 786432 | tf_op jit(solution)/shard_map/all_to_all | solution.py:554
  186.9 6.0 %all-to-all-start.3 = ((bf16[8,16,1536]{2,1,0:T(8,128)(2,1)}), bf16[8,16,1536]{2,1,0:T(8,128)(2,1)S(1)}, u32[]{:S(2)}, u32[]{:S(2)}) async-start(bf16[8,16,1536]{2,1,0:T(8,128)(2,1)} %fold.1), calls=%async_computation.3 | async-start | bytes 786432 | tf_op jit(solution)/shard_map/all_to_all | solution.py:610
  196.2 5.9 %all-to-all-done.3.in_ref = bf16[8,16,1536]{2,1,0:T(8,128)(2,1)S(1)} async-done(((bf16[8,16,1536]{2,1,0:T(8,128)(2,1)}), bf16[8,16,1536]{2,1,0:T(8,128)(2,1)S(1)}, u32[]{:S(2)}, u32[]{:S(2)}) %all-to-all-start.3) | async-done | bytes 393248 | tf_op jit(solution)/shard_map/all_to_all | solution.py:610
  (122 shorter events, 56.5 us)
Async XLA Ops:
  7.2 56.6 %all-gather.2.cloned.1.call-start = ((), (), s32[]{:S(2)}) async-start(), calls=%async_computation.5 | async-start | bytes 7102464 | tf_op jit(solution)/shard_map/all_gather | solution.py:574
  9.1 19.1 %copy-start.21 = (f32[1536]{0:T(1024)S(1)}, f32[1536]{0:T(1024)}, u32[]{:S(2)}) copy-start(f32[1536]{0:T(1024)} %param.14) | copy-start | bytes 18436
  13.7 25.8 %collective-permute-start.3 = (bf16[128,1536]{1,0:T(8,128)(2,1)}, bf16[128,1536]{1,0:T(8,128)(2,1)}, u32[]{:S(2)}, u32[]{:S(2)}) collective-permute-start(bf16[128,1536]{1,0:T(8,128)(2,1)} %spatial_fwd.1.mixed_ref), channel_id=1, source_target_pairs={{0,1},{1,0},{2,3},{3,2},{4,5},{5,4},{6,7},{7,6},{8,9},{9,8},{10,11... | collective-permute-start | bytes 1179656 | tf_op jit(solution)/shard_map/ppermute | solution.py:483
  16.9 25.8 %collective-permute-start = (bf16[128,1536]{1,0:T(8,128)(2,1)}, bf16[128,1536]{1,0:T(8,128)(2,1)}, u32[]{:S(2)}, u32[]{:S(2)}) collective-permute-start(bf16[128,1536]{1,0:T(8,128)(2,1)} %spatial_fwd.1.mixed_ref), channel_id=1, source_target_pairs={{0,2},{1,3},{2,4},{3,5},{4,6},{5,7},{6,0},{7,1},{8,10},{9,11},{10,... | collective-permute-start | bytes 1179656 | tf_op jit(solution)/shard_map/ppermute | solution.py:479
  20.0 16.3 %all-to-all-start = ((bf16[8,128,192]{1,2,0:T(8,128)(2,1)}), bf16[8,128,192]{1,2,0:T(8,128)(2,1)}, u32[]{:S(2)}, u32[]{:S(2)}) async-start(bf16[8,128,192]{1,2,0:T(8,128)(2,1)} %copy.20), calls=%async_computation | async-start | bytes 786432 | tf_op jit(solution)/shard_map/all_to_all | solution.py:579
  24.1 170.5 %reduce-scatter.2.cloned.1.call-start = ((), (), s32[]{:S(2)}) async-start(), calls=%async_computation.6 | async-start | bytes 2088960 | tf_op jit(solution)/shard_map/reduce_scatter | solution.py:595
  24.1 25.5 %collective-permute-start.1 = (bf16[128,1536]{1,0:T(8,128)(2,1)S(1)}, bf16[128,1536]{1,0:T(8,128)(2,1)}, u32[]{:S(2)}, u32[]{:S(2)}) collective-permute-start(bf16[128,1536]{1,0:T(8,128)(2,1)S(1)} %copy-done.19), channel_id=1, source_target_pairs={{0,6},{1,7},{2,0},{3,1},{4,2},{5,3},{6,4},{7,5},{8,14},{9,15},{10,... | collective-permute-start | bytes 1179656 | tf_op jit(solution)/shard_map/ppermute | solution.py:479
  27.3 23.4 %collective-permute-start.2 = (bf16[128,1536]{1,0:T(8,128)(2,1)S(1)}, bf16[128,1536]{1,0:T(8,128)(2,1)}, u32[]{:S(2)}, u32[]{:S(2)}) collective-permute-start(bf16[128,1536]{1,0:T(8,128)(2,1)S(1)} %copy-done.19), channel_id=1, source_target_pairs={{0,4},{1,5},{2,6},{3,7},{4,0},{5,1},{6,2},{7,3},{8,12},{9,13},{10,... | collective-permute-start | bytes 1179656 | tf_op jit(solution)/shard_map/ppermute | solution.py:479
  39.4 15.8 %collective-permute-start.4 = (bf16[128,1536]{1,0:T(8,128)(2,1)}, bf16[128,1536]{1,0:T(8,128)(2,1)S(1)}, u32[]{:S(2)}, u32[]{:S(2)}) collective-permute-start(bf16[128,1536]{1,0:T(8,128)(2,1)} %collective-permute-done.3), channel_id=1, source_target_pairs={{0,2},{1,3},{2,4},{3,5},{4,6},{5,7},{6,0},{7,1},{8,10},{9,11},{10,... | collective-permute-start | bytes 1179656 | tf_op jit(solution)/shard_map/ppermute | solution.py:479
  40.8 16.5 %collective-permute-start.5 = (bf16[128,1536]{1,0:T(8,128)(2,1)}, bf16[128,1536]{1,0:T(8,128)(2,1)S(1)}, u32[]{:S(2)}, u32[]{:S(2)}) collective-permute-start(bf16[128,1536]{1,0:T(8,128)(2,1)} %collective-permute-done.3), channel_id=1, source_target_pairs={{0,6},{1,7},{2,0},{3,1},{4,2},{5,3},{6,4},{7,5},{8,14},{9,15},{10,... | collective-permute-start | bytes 1179656 | tf_op jit(solution)/shard_map/ppermute | solution.py:479
  42.7 16.7 %collective-permute-start.6 = (bf16[128,1536]{1,0:T(8,128)(2,1)}, bf16[128,1536]{1,0:T(8,128)(2,1)S(1)}, u32[]{:S(2)}, u32[]{:S(2)}) collective-permute-start(bf16[128,1536]{1,0:T(8,128)(2,1)} %collective-permute-done.3), channel_id=1, source_target_pairs={{0,4},{1,5},{2,6},{3,7},{4,0},{5,1},{6,2},{7,3},{8,12},{9,13},{10,... | collective-permute-start | bytes 1179656 | tf_op jit(solution)/shard_map/ppermute | solution.py:479
  70.5 11.9 %collective-permute-start.8 = (bf16[128,1536]{1,0:T(8,128)(2,1)}, bf16[128,1536]{1,0:T(8,128)(2,1)S(1)}, u32[]{:S(2)}, u32[]{:S(2)}) collective-permute-start(bf16[128,1536]{1,0:T(8,128)(2,1)} %get-tuple-element.50.refs_0_), channel_id=1, source_target_pairs={{0,6},{1,7},{2,0},{3,1},{4,2},{5,3},{6,4},{7,5},{8,14},{9,15},{10,... | collective-permute-start | bytes 1179656 | tf_op jit(solution)/shard_map/ppermute | solution.py:479
  75.2 10.9 %collective-permute-start.7 = (bf16[128,1536]{1,0:T(8,128)(2,1)}, bf16[128,1536]{1,0:T(8,128)(2,1)S(1)}, u32[]{:S(2)}, u32[]{:S(2)}) collective-permute-start(bf16[128,1536]{1,0:T(8,128)(2,1)} %get-tuple-element.50.refs_0_), channel_id=1, source_target_pairs={{0,2},{1,3},{2,4},{3,5},{4,6},{5,7},{6,0},{7,1},{8,10},{9,11},{10,... | collective-permute-start | bytes 1179656 | tf_op jit(solution)/shard_map/ppermute | solution.py:479
  75.2 11.9 %collective-permute-start.11 = (bf16[128,1536]{1,0:T(8,128)(2,1)}, bf16[128,1536]{1,0:T(8,128)(2,1)S(1)}, u32[]{:S(2)}, u32[]{:S(2)}) collective-permute-start(bf16[128,1536]{1,0:T(8,128)(2,1)} %get-tuple-element.50.refs_0_), channel_id=1, source_target_pairs={{0,1},{1,0},{2,3},{3,2},{4,5},{5,4},{6,7},{7,6},{8,9},{9,8},{10,11... | collective-permute-start | bytes 1179656 | tf_op jit(solution)/shard_map/ppermute | solution.py:483
  82.4 8.6 %collective-permute-start.10 = (bf16[64,1536]{1,0:T(8,128)(2,1)S(1)}, bf16[64,1536]{1,0:T(8,128)(2,1)S(1)}, u32[]{:S(2)}, u32[]{:S(2)}) collective-permute-start(bf16[64,1536]{1,0:T(8,128)(2,1)S(1)} %slice.37), channel_id=1, source_target_pairs={{0,6},{1,7},{2,0},{3,1},{4,2},{5,3},{6,4},{7,5},{8,14},{9,15},{10,... | collective-permute-start | bytes 589832 | tf_op jit(solution)/shard_map/ppermute | solution.py:479
  86.1 9.1 %collective-permute-start.9 = (bf16[64,1536]{1,0:T(8,128)(2,1)S(1)}, bf16[64,1536]{1,0:T(8,128)(2,1)S(1)}, u32[]{:S(2)}, u32[]{:S(2)}) collective-permute-start(bf16[64,1536]{1,0:T(8,128)(2,1)S(1)} %slice.36), channel_id=1, source_target_pairs={{0,2},{1,3},{2,4},{3,5},{4,6},{5,7},{6,0},{7,1},{8,10},{9,11},{10,... | collective-permute-start | bytes 589832 | tf_op jit(solution)/shard_map/ppermute | solution.py:479
  87.1 12.6 %collective-permute-start.12 = (bf16[128,1536]{1,0:T(8,128)(2,1)S(1)}, bf16[128,1536]{1,0:T(8,128)(2,1)S(1)}, u32[]{:S(2)}, u32[]{:S(2)}) collective-permute-start(bf16[128,1536]{1,0:T(8,128)(2,1)S(1)} %collective-permute-done.11.refs_5_), channel_id=1, source_target_pairs={{0,2},{1,3},{2,4},{3,5},{4,6},{5,7},{6,0},{7,1},{8,10},{9,11},{10,... | collective-permute-start | bytes 1179656 | tf_op jit(solution)/shard_map/ppermute | solution.py:479
  87.9 12.3 %collective-permute-start.13 = (bf16[128,1536]{1,0:T(8,128)(2,1)S(1)}, bf16[128,1536]{1,0:T(8,128)(2,1)S(1)}, u32[]{:S(2)}, u32[]{:S(2)}) collective-permute-start(bf16[128,1536]{1,0:T(8,128)(2,1)S(1)} %collective-permute-done.11.refs_5_), channel_id=1, source_target_pairs={{0,6},{1,7},{2,0},{3,1},{4,2},{5,3},{6,4},{7,5},{8,14},{9,15},{10,... | collective-permute-start | bytes 1179656 | tf_op jit(solution)/shard_map/ppermute | solution.py:479
  91.0 9.7 %collective-permute-start.15 = (bf16[64,1536]{1,0:T(8,128)(2,1)S(1)}, bf16[64,1536]{1,0:T(8,128)(2,1)S(1)}, u32[]{:S(2)}, u32[]{:S(2)}) collective-permute-start(bf16[64,1536]{1,0:T(8,128)(2,1)S(1)} %collective-permute-done.10.refs_4_), channel_id=1, source_target_pairs={{0,1},{1,0},{2,3},{3,2},{4,5},{5,4},{6,7},{7,6},{8,9},{9,8},{10,11... | collective-permute-start | bytes 589832 | tf_op jit(solution)/shard_map/ppermute | solution.py:483
  95.7 7.4 %collective-permute-start.14 = (bf16[64,1536]{1,0:T(8,128)(2,1)S(1)}, bf16[64,1536]{1,0:T(8,128)(2,1)S(1)}, u32[]{:S(2)}, u32[]{:S(2)}) collective-permute-start(bf16[64,1536]{1,0:T(8,128)(2,1)S(1)} %collective-permute-done.9.refs_3_), channel_id=1, source_target_pairs={{0,1},{1,0},{2,3},{3,2},{4,5},{5,4},{6,7},{7,6},{8,9},{9,8},{10,11... | collective-permute-start | bytes 589832 | tf_op jit(solution)/shard_map/ppermute | solution.py:483
  111.9 14.1 %collective-permute-start.16 = (bf16[128,1536]{1,0:T(8,128)(2,1)}, bf16[128,1536]{1,0:T(8,128)(2,1)}, u32[]{:S(2)}, u32[]{:S(2)}) collective-permute-start(bf16[128,1536]{1,0:T(8,128)(2,1)} %get-tuple-element.61), channel_id=1, source_target_pairs={{0,1},{1,0},{2,3},{3,2},{4,5},{5,4},{6,7},{7,6},{8,9},{9,8},{10,11... | collective-permute-start | bytes 1179656 | tf_op jit(solution)/shard_map/ppermute | solution.py:483
  114.8 11.1 %collective-permute-start.17 = (bf16[128,1536]{1,0:T(8,128)(2,1)}, bf16[128,1536]{1,0:T(8,128)(2,1)}, u32[]{:S(2)}, u32[]{:S(2)}) collective-permute-start(bf16[128,1536]{1,0:T(8,128)(2,1)} %get-tuple-element.62), channel_id=1, source_target_pairs={{0,6},{1,7},{2,0},{3,1},{4,2},{5,3},{6,4},{7,5},{8,14},{9,15},{10,... | collective-permute-start | bytes 1179656 | tf_op jit(solution)/shard_map/ppermute | solution.py:479
  115.2 10.7 %collective-permute-start.18 = (bf16[128,1536]{1,0:T(8,128)(2,1)}, bf16[128,1536]{1,0:T(8,128)(2,1)}, u32[]{:S(2)}, u32[]{:S(2)}) collective-permute-start(bf16[128,1536]{1,0:T(8,128)(2,1)} %get-tuple-element.63), channel_id=1, source_target_pairs={{0,2},{1,3},{2,4},{3,5},{4,6},{5,7},{6,0},{7,1},{8,10},{9,11},{10,... | collective-permute-start | bytes 1179656 | tf_op jit(solution)/shard_map/ppermute | solution.py:479
  127.3 7.0 %collective-permute-start.20 = (bf16[64,1536]{1,0:T(8,128)(2,1)S(1)}, bf16[64,1536]{1,0:T(8,128)(2,1)S(1)}, u32[]{:S(2)}, u32[]{:S(2)}) collective-permute-start(bf16[64,1536]{1,0:T(8,128)(2,1)S(1)} %get-tuple-element.90), channel_id=1, source_target_pairs={{0,6},{1,7},{2,0},{3,1},{4,2},{5,3},{6,4},{7,5},{8,14},{9,15},{10,... | collective-permute-start | bytes 589832 | tf_op jit(solution)/shard_map/ppermute | solution.py:479
  129.0 18.3 %copy-start.18 = (f32[1,1536]{1,0:T(1,128)S(1)}, f32[1,1536]{1,0:T(1,128)}, u32[]{:S(2)}) copy-start(f32[1,1536]{1,0:T(1,128)} %reshape.55.gain_ref) | copy-start | bytes 18436
  129.0 9.0 %collective-permute-start.22 = (bf16[64,1536]{1,0:T(8,128)(2,1)S(1)}, bf16[64,1536]{1,0:T(8,128)(2,1)S(1)}, u32[]{:S(2)}, u32[]{:S(2)}) collective-permute-start(bf16[64,1536]{1,0:T(8,128)(2,1)S(1)} %get-tuple-element.89), channel_id=1, source_target_pairs={{0,2},{1,3},{2,4},{3,5},{4,6},{5,7},{6,0},{7,1},{8,10},{9,11},{10,... | collective-permute-start | bytes 589832 | tf_op jit(solution)/shard_map/ppermute | solution.py:479
  130.7 10.0 %collective-permute-start.19 = (bf16[128,1536]{1,0:T(8,128)(2,1)S(1)}, bf16[128,1536]{1,0:T(8,128)(2,1)S(1)}, u32[]{:S(2)}, u32[]{:S(2)}) collective-permute-start(bf16[128,1536]{1,0:T(8,128)(2,1)S(1)} %add_add_fusion), channel_id=1, source_target_pairs={{0,1},{1,0},{2,3},{3,2},{4,5},{5,4},{6,7},{7,6},{8,9},{9,8},{10,11... | collective-permute-start | bytes 1179656 | tf_op jit(solution)/shard_map/ppermute | solution.py:483
  138.1 7.8 %collective-permute-start.21 = (bf16[128,1536]{1,0:T(8,128)(2,1)S(1)}, bf16[128,1536]{1,0:T(8,128)(2,1)S(1)}, u32[]{:S(2)}, u32[]{:S(2)}) collective-permute-start(bf16[128,1536]{1,0:T(8,128)(2,1)S(1)} %pad_maximum_fusion), channel_id=1, source_target_pairs={{0,6},{1,7},{2,0},{3,1},{4,2},{5,3},{6,4},{7,5},{8,14},{9,15},{10,... | collective-permute-start | bytes 1179656 | tf_op jit(solution)/shard_map/ppermute | solution.py:479
  138.2 9.1 %collective-permute-start.23 = (bf16[128,1536]{1,0:T(8,128)(2,1)S(1)}, bf16[128,1536]{1,0:T(8,128)(2,1)S(1)}, u32[]{:S(2)}, u32[]{:S(2)}) collective-permute-start(bf16[128,1536]{1,0:T(8,128)(2,1)S(1)} %pad_maximum_fusion.1), channel_id=1, source_target_pairs={{0,2},{1,3},{2,4},{3,5},{4,6},{5,7},{6,0},{7,1},{8,10},{9,11},{10,... | collective-permute-start | bytes 1179656 | tf_op jit(solution)/shard_map/ppermute | solution.py:479
  149.8 15.3 %all-to-all-start.1 = ((bf16[8,144,384]{2,1,0:T(8,128)(2,1)}), bf16[8,144,384]{2,1,0:T(8,128)(2,1)S(1)}, u32[]{:S(2)}, u32[]{:S(2)}) async-start(bf16[8,144,384]{2,1,0:T(8,128)(2,1)} %get-tuple-element.71), calls=%async_computation.1 | async-start | bytes 1769472 | tf_op jit(solution)/shard_map/all_to_all | solution.py:603
  169.3 1.8 collective-permute-start.24
  186.9 15.2 %all-to-all-start.3 = ((bf16[8,16,1536]{2,1,0:T(8,128)(2,1)}), bf16[8,16,1536]{2,1,0:T(8,128)(2,1)S(1)}, u32[]{:S(2)}, u32[]{:S(2)}) async-start(bf16[8,16,1536]{2,1,0:T(8,128)(2,1)} %fold.1), calls=%async_computation.3 | async-start | bytes 786432 | tf_op jit(solution)/shard_map/all_to_all | solution.py:610
  (20 other events, 174.1 us)
Sparse Core Ops, SparseCore 0:
  9.7 54.0 all-gather.1
  126.1 68.4 reduce-scatter.1
